TPU v7x, 512 devices: a whole 4x8x8 slice. The times are simulated.
512 devices in a mesh: row: 32 (over x, y), col: 16 (over z, core).
Axes of the slice: x: 4, y: 8, z: 8, core: 2. Of those that a mesh axis runs over, the one named last changes fastest.
Arguments:
- cov: float32 [2, 8192, 4, 4096], P(None, 'row', None, 'col'), may hold values from 0 to 6, as said below
Outputs:
- factored: float32 [2, 8192, 4, 4096], P(None, 'row', None, 'col')
Inputs may be any that keep to these rules, and one draw needn't show every extreme that they name: cov is symmetric positive definite: s_i s_j exp(-|x_i - x_j| / ell) over site positions x in the unit square and positive site scales s, plus a nugget between 0.5 and 1.5 on the diagonal.
All inputs are finite; a program needn't handle non-finite values.
Results may differ from a plain program's by a relative error of at most 0.0003.
Values sent between devices are 32-bit elements; how exact they have to be, the bound alone decides.
No kernel may reach another device: no remote copies, remote signals or barrier semaphores. Data moves between devices by JAX's collectives and lax.ppermute only.
A program may use at most 64 MiB of HBM per device.

v0:
```python
import jax
import jax.numpy as jnp
from jax import lax
from jax.sharding import PartitionSpec as P


def spread(block, axis, source):
    block = jnp.where(lax.axis_index(axis) == source, block, jnp.zeros_like(block))
    return lax.psum(block, axis)


def on_device(cov):
    rows_dev, tile_size, cols_dev, width_last = cov.shape
    n_rows = lax.axis_size("row")
    n_cols = lax.axis_size("col")
    my_col = lax.axis_index("col")
    tile_rows = jnp.arange(rows_dev, dtype=jnp.int32) * n_rows + lax.axis_index("row")
    tile_cols = jnp.arange(cols_dev, dtype=jnp.int32) * n_cols + my_col
    identity = jnp.eye(tile_size, dtype=jnp.float32)
    highest = lax.Precision.HIGHEST
    matrix = cov
    for panel_step in range(2):
        local_diag = matrix[panel_step // n_rows, :, panel_step // n_cols, :]
        diag_tile = spread(local_diag, "row", panel_step % n_rows)
        diag_tile = jnp.where(my_col == panel_step % n_cols, diag_tile, identity)
        factor_tile = jnp.linalg.cholesky(diag_tile)
        inverse = lax.linalg.triangular_solve(factor_tile, identity, left_side=True, lower=True)
        column = matrix[:, :, panel_step // n_cols, :]
        solved = jnp.einsum("aik,jk->aij", column, inverse, precision=highest)
        solved = jnp.where((tile_rows == panel_step)[:, None, None], factor_tile[None], solved)
        solved = jnp.where((tile_rows < panel_step)[:, None, None], 0.0, solved)
        panels = spread(solved, "col", panel_step % n_cols)
        pieces = []
        for local_col in range(cols_dev):
            target = local_col * n_cols + my_col
            chosen = lax.dynamic_index_in_dim(panels, target // n_rows, 0, keepdims=False)
            pieces.append(spread(chosen, "row", target % n_rows))
        rows_used = jnp.where((tile_rows > panel_step)[:, None, None], panels, 0.0)
        cols_used = jnp.where((tile_cols > panel_step)[:, None, None], jnp.stack(pieces), 0.0)
        matrix = matrix - jnp.einsum("aik,bjk->aibj", rows_used, cols_used, precision=highest)
        block = panel_step // n_cols
        kept = jnp.where(my_col == panel_step % n_cols, panels, matrix[:, :, block, :])
        matrix = matrix.at[:, :, block, :].set(kept)
    offsets = jnp.arange(tile_size, dtype=jnp.int32)
    global_row = tile_rows[:, None, None, None] * tile_size + offsets[None, :, None, None]
    global_col = tile_cols[None, None, :, None] * tile_size + offsets[None, None, None, :]
    keep = (global_row >= 2 * tile_size) | (global_col <= global_row)
    return jnp.where(keep, matrix, 0.0)


def solution(mesh):
    placed = (P(None, "row", None, "col"),)
    return jax.shard_map(
        on_device,
        mesh=mesh,
        in_specs=placed,
        out_specs=P(None, "row", None, "col"),
        check_vma=False,
    )
```

profile of v0, /device:TPU:1, one launch (start us, length us, event | category | flops | bytes accessed | tf_op | source)
XLA Modules:
  0.0 1020.7 jit_solution(15363618330713078700)
XLA Ops:
  6.5 1.4 slice.108
  7.9 0.1 copy.32
  8.1 0.7 select_bitcast_fusion
  9.0 158.0 %all-reduce.10.cloned.1.call-done = f32[256,256]{0,1:T(8,128)} async-done(((f32[256,256]{0,1:T(8,128)}), f32[256,256]{0,1:T(8,128)}) %all-reduce.10.cloned.1.call-update) | async-done | bytes 262160 | tf_op jit(solution)/shard_map/psum | solution.py:9
  167.0 0.1 copy.3
  167.2 11.7 %cholesky.130 = f32[128,128]{1,0:T(8,128)S(1)} custom-call(f32[128,128]{1,0:T(8,128)S(1)} %cholesky.194), custom_call_target="Cholesky" | custom-call | tf_op jit(solution)/shard_map/jit(cholesky)/cholesky | solution.py:26
  179.0 9.8 custom-call.13
  188.8 0.2 constant_dynamic-update-slice_fusion.1
  189.1 0.3 convolution_subtract_fusion.5
  189.3 11.7 %cholesky.147 = f32[128,128]{1,0:T(8,128)S(1)} custom-call(f32[128,128]{1,0:T(8,128)S(1)} %convolution_subtract_fusion.5), custom_call_target="Cholesky" | custom-call | tf_op jit(solution)/shard_map/jit(cholesky)/cholesky | solution.py:26
  201.1 0.7 compare_reduce_fusion.2
  203.1 0.1 broadcast.364
  203.2 4.2 while.6
  203.4 0.6 fusion.82
  204.0 1.4 bitcast_dynamic-update-slice_fusion.5
  205.4 0.6 fusion.82
  206.0 1.4 bitcast_dynamic-update-slice_fusion.5
  207.4 19.7 %custom-call.14 = f32[2,128,128]{1,2,0:T(8,128)S(1)} custom-call(f32[2,128,128]{2,1,0:T(8,128)S(1)} %get-tuple-element.45), custom_call_target="InvertDiagBlocksLowerTriangular" | custom-call | tf_op jit(solution)/shard_map/triangular_solve/custom-call.0 | solution.py:27
  227.0 0.3 fusion.51
  227.4 0.4 convolution_subtract_fusion.3
  227.8 0.3 fusion.58
  228.1 0.1 copy.4
  228.2 1.5 fusion.4
  229.8 117.6 %all-reduce.12.cloned.1.call-done = f32[2,256,256]{1,2,0:T(8,128)} async-done(((f32[2,256,256]{1,2,0:T(8,128)}), f32[2,256,256]{1,2,0:T(8,128)}) %all-reduce.12.cloned.1.call-update) | async-done | bytes 524304 | tf_op jit(solution)/shard_map/psum | solution.py:9
  347.4 2.2 dynamic-slice_select_fusion.7
  349.7 1.8 copy.8
  351.5 156.5 %all-reduce.20.cloned.1.call-done = (f32[1,256,256]{1,2,0:T(8,128)}, f32[1,256,256]{1,2,0:T(8,128)}, f32[1,256,256]{1,2,0:T(8,128)}, f32[1,256,256]{1,2,0:T(8,128)}) async-done(((f32[1,256,256]{1,2,0:T(8,128)}, f32[1,256,256]{1,2,0:T(8,128)}, f32[1,256,256]{1,2,0:T(8,128)}, f32[1,256,256]{1,2,0:T(8,128)}), (f32[1,256,256]{1,2,0:T(8,128)}, f32[1,256,256]{1,2,0:T(8,128)}, f32[1,256,256]{1,2,0:T(8,128)}, ...) | async-done | bytes 1048592 | tf_op jit(solution)/shard_map/psum | solution.py:9
  508.0 3.9 convolution_subtract_fusion.1
  512.0 0.1 fusion.24
  512.1 0.7 fusion.33
  512.8 0.3 all-reduce.16.cloned.1.call-start
  513.1 152.4 %all-reduce.14.cloned.1.call-done = f32[256,256]{0,1:T(8,128)} async-done(((f32[256,256]{0,1:T(8,128)}), f32[256,256]{0,1:T(8,128)}) %all-reduce.14.cloned.1.call-update) | async-done | bytes 262160 | tf_op jit(solution)/shard_map/psum | solution.py:9
  665.5 1.0 fusion.47
  666.5 0.1 copy.10
  666.6 1.0 fusion.38
  667.7 11.7 %cholesky.164 = f32[128,128]{1,0:T(8,128)S(1)} custom-call(f32[128,128]{1,0:T(8,128)S(1)} %cholesky.197), custom_call_target="Cholesky" | custom-call | tf_op jit(solution)/shard_map/jit(cholesky)/cholesky | solution.py:26
  679.4 9.8 custom-call.15
  689.3 0.2 constant_dynamic-update-slice_fusion
  689.5 0.3 convolution_subtract_fusion.4
  689.7 11.7 %cholesky.181 = f32[128,128]{1,0:T(8,128)S(1)} custom-call(f32[128,128]{1,0:T(8,128)S(1)} %convolution_subtract_fusion.4), custom_call_target="Cholesky" | custom-call | tf_op jit(solution)/shard_map/jit(cholesky)/cholesky | solution.py:26
  701.5 0.6 compare_reduce_fusion.1
  702.1 0.7 compare_reduce_fusion
  704.1 0.7 fusion.40
  704.9 4.3 while.7
  705.1 0.6 fusion.83
  705.8 1.3 bitcast_dynamic-update-slice_fusion.6
  707.2 0.6 fusion.83
  707.8 1.3 bitcast_dynamic-update-slice_fusion.6
  709.2 19.7 %custom-call.16 = f32[2,128,128]{1,2,0:T(8,128)S(1)} custom-call(f32[2,128,128]{2,1,0:T(8,128)S(1)} %get-tuple-element.46), custom_call_target="InvertDiagBlocksLowerTriangular" | custom-call | tf_op jit(solution)/shard_map/triangular_solve/custom-call.0 | solution.py:27
  728.8 0.3 fusion.49
  729.2 0.4 convolution_subtract_fusion.2
  729.5 0.3 fusion.54
  729.9 1.1 copy.11
  731.0 1.5 fusion.1
  732.5 115.7 %all-reduce.16.cloned.1.call-done = f32[2,256,256]{1,2,0:T(8,128)} async-done(((f32[2,256,256]{1,2,0:T(8,128)}), f32[2,256,256]{1,2,0:T(8,128)}) %all-reduce.16.cloned.1.call-update) | async-done | bytes 524304 | tf_op jit(solution)/shard_map/psum | solution.py:9
  848.3 2.2 dynamic-slice_select_fusion.3
  850.6 0.1 broadcast_compare_fusion
  850.6 0.1 iota_add_fusion.1
  850.7 0.1 iota_add_fusion
  850.8 157.5 %all-reduce.18.cloned.1.call-done = (f32[1,256,256]{1,2,0:T(8,128)}, f32[1,256,256]{1,2,0:T(8,128)}, f32[1,256,256]{1,2,0:T(8,128)}, f32[1,256,256]{1,2,0:T(8,128)}) async-done(((f32[1,256,256]{1,2,0:T(8,128)}, f32[1,256,256]{1,2,0:T(8,128)}, f32[1,256,256]{1,2,0:T(8,128)}, f32[1,256,256]{1,2,0:T(8,128)}), (f32[1,256,256]{1,2,0:T(8,128)}, f32[1,256,256]{1,2,0:T(8,128)}, f32[1,256,256]{1,2,0:T(8,128)}, ...) | async-done | bytes 1048592 | tf_op jit(solution)/shard_map/psum | solution.py:9
  1008.3 3.2 convolution_subtract_fusion
  1011.5 0.1 fusion.23
  1011.6 0.4 or_select_fusion
  1012.1 1.8 copy.17
  (47 shorter events, 0.8 us)
Async XLA Ops:
  6.5 160.5 %all-reduce.10.cloned.1.call-start = ((), (), s32[]{:S(2)}) async-start(), calls=%async_computation | async-start | bytes 524288 | tf_op jit(solution)/shard_map/psum | solution.py:9
  8.8 338.6 %all-reduce.12.cloned.1.call-start = ((), (), s32[]{:S(2)}) async-start(), calls=%async_computation.1 | async-start | bytes 1048576 | tf_op jit(solution)/shard_map/psum | solution.py:9
  179.0 49.2 %slice-start = ((f32[2,256,4,256]{3,2,1,0:T(4,128)}), f32[2,256,1,256]{3,2,1,0:T(1,128)S(1)}, s32[]{:S(2)}) async-start(f32[2,256,4,256]{3,2,1,0:T(4,128)} %param.8), calls=%async_computation.6 | async-start | bytes 1048576 | tf_op jit(solution)/shard_map/slice | solution.py:28
  229.7 120.0 %copy-start.2 = (f32[2,256,4,256]{3,2,1,0:T(4,128)S(1)}, f32[2,256,4,256]{3,2,1,0:T(4,128)}, u32[]{:S(2)}) copy-start(f32[2,256,4,256]{3,2,1,0:T(4,128)} %param.8) | copy-start | bytes 6291460
  229.7 278.3 %all-reduce.20.cloned.1.call-start = ((), (), s32[]{:S(2)}) async-start(), calls=%async_computation.5 | async-start | bytes 2097152 | tf_op jit(solution)/shard_map/psum | solution.py:9
  349.6 158.4 %copy-start = (f32[2,256,256]{1,2,0:T(8,128)S(1)}, f32[2,256,256]{1,2,0:T(8,128)}, u32[]{:S(2)}) copy-start(f32[2,256,256]{1,2,0:T(8,128)} %all-reduce.12.cloned.1.call-done) | copy-start | bytes 1572868
  349.6 315.9 %all-reduce.14.cloned.1.call-start = ((), (), s32[]{:S(2)}) async-start(), calls=%async_computation.2 | async-start | bytes 524288 | tf_op jit(solution)/shard_map/psum | solution.py:9
  512.8 335.4 %all-reduce.16.cloned.1.call-start = ((), (), s32[]{:S(2)}) async-start(), calls=%async_computation.3 | async-start | bytes 1048576 | tf_op jit(solution)/shard_map/psum | solution.py:9
  732.4 275.8 %all-reduce.18.cloned.1.call-start = ((), (), s32[]{:S(2)}) async-start(), calls=%async_computation.4 | async-start | bytes 2097152 | tf_op jit(solution)/shard_map/psum | solution.py:9
  848.3 160.0 %copy-start.1 = (f32[2,256,256]{1,2,0:T(8,128)S(1)}, f32[2,256,256]{1,2,0:T(8,128)}, u32[]{:S(2)}) copy-start(f32[2,256,256]{1,2,0:T(8,128)} %all-reduce.16.cloned.1.call-done) | copy-start | bytes 1572868
Sparse Core Ops, SparseCore 0:
  10.8 156.1 all-reduce.9
  229.8 117.5 all-reduce.11
  351.7 156.2 all-reduce.19
  512.9 152.5 all-reduce.13
  732.6 115.6 all-reduce.15
  851.9 156.3 all-reduce.17
where the time goes:
time: 1020 us
  waiting for transfers between devices  858 us (84%)
  other arithmetic  118 us (12%)
  between operations  16.5 us (2%)
  local copies, waits for them, and re-layouts  14.7 us (1%)
  matrix products  13.1 us (1%)
    psum x6, waiting for transfers between devices, spread(): return lax.psum(block, axis)  858 us
    another operation x13, other arithmetic, on_device(): factor_tile = jnp.linalg.cholesky(diag_tile)  68.7 us
    another operation x5, other arithmetic, on_device(): lax.linalg.triangular_solve(factor_tile, identity, left_side=True, lower=...  40.1 us
  transfers between devices with their start and end apart: 6, of which 6 were waited for; matrix products, arithmetic and copies ran while one was open for 0% of the time, Pallas kernels for 0%

commit v1 on v0

v1 whole, which is shorter than its diff:
```python
import functools

import jax
import jax.numpy as jnp
from jax import lax
from jax.experimental import pallas as pl
from jax.experimental.pallas import tpu as pltpu
from jax.sharding import PartitionSpec as P

HIGHEST = lax.Precision.HIGHEST
LANE = 128
SUB = 8
X, Y, Z, CORE = 4, 8, 8, 2
N_ROW, N_COL = X * Y, Z * CORE
NB = 256
BOTH = ("row", "col")


def device(x, y, z, core):
    return (x * Y + y) * N_COL + z * CORE + core


def dot_nt(a, b):
    return lax.dot_general(a, b, (((1,), (1,)), ((), ())), precision=HIGHEST, preferred_element_type=jnp.float32)


def dot_nn(a, b):
    return lax.dot_general(a, b, (((1,), (0,)), ((), ())), precision=HIGHEST, preferred_element_type=jnp.float32)


def factor_block(rows):
    count = len(rows)
    rows = list(rows)
    sub = lax.broadcasted_iota(jnp.int32, (SUB, LANE), 0)
    lane = lax.broadcasted_iota(jnp.int32, (SUB, LANE), 1)
    aug = [jnp.where(lane == sub + SUB * g, 1.0, 0.0).astype(jnp.float32) for g in range(count)]
    for p in range(count):
        cols = [
            [jnp.broadcast_to(rows[g][:, SUB * p + k : SUB * p + k + 1], (SUB, LANE)) for g in range(p, count)]
            for k in range(SUB)
        ]
        r, e = rows[p], aug[p]
        xs, ys = [], []
        for k in range(SUB):
            scale = lax.rsqrt(jnp.broadcast_to(cols[k][0][k : k + 1, :], (SUB, LANE)))
            ck = [c * scale for c in cols[k]]
            cols[k] = ck
            x = jnp.broadcast_to(r[k : k + 1, :], (SUB, LANE)) * scale
            y = jnp.broadcast_to(e[k : k + 1, :], (SUB, LANE)) * scale
            xs.append(x)
            ys.append(y)
            if k < SUB - 1:
                below = jnp.where(sub > k, ck[0], 0.0)
                r = r - below * x
                e = e - below * y
                for m in range(k + 1, SUB):
                    s = jnp.broadcast_to(ck[0][m : m + 1, :], (SUB, LANE))
                    cols[m] = [c - d * s for c, d in zip(cols[m], ck)]
        for i, g in enumerate(range(p + 1, count)):
            a, b = rows[g], aug[g]
            for k in range(SUB):
                a = a - cols[k][i + 1] * xs[k]
                b = b - cols[k][i + 1] * ys[k]
            rows[g], aug[g] = a, b
        x, y = xs[0], ys[0]
        for k in range(1, SUB):
            x = jnp.where(sub == k, xs[k], x)
            y = jnp.where(sub == k, ys[k], y)
        rows[p] = jnp.where(lane >= sub + SUB * p, x, 0.0)
        aug[p] = y
    return rows, aug


def factor_kernel(d00_ref, d10_ref, d11_ref, l_ref, w_ref, a_ref):
    n = a_ref.shape[0]
    half = n // 2
    a_ref[:half, :half] = d00_ref[...]
    a_ref[half:, :half] = d10_ref[...]
    a_ref[:half, half:] = jnp.zeros((half, half), jnp.float32)
    a_ref[half:, half:] = d11_ref[...]
    l_ref[...] = jnp.zeros_like(l_ref)
    w_ref[...] = jnp.zeros_like(w_ref)

    def step(b, carry):
        o = pl.multiple_of(b * LANE, LANE)
        blk = pl.ds(o, LANE)
        rows = [a_ref[pl.ds(pl.multiple_of(o + SUB * g, SUB), SUB), blk] for g in range(LANE // SUB)]
        up, inv = factor_block(rows)
        up, inv = jnp.concatenate(up, 0), jnp.concatenate(inv, 0)
        below = lax.broadcasted_iota(jnp.int32, (n, LANE), 0) >= o + LANE
        panel = jnp.where(below, dot_nt(a_ref[:, blk], inv), 0.0)
        a_ref[...] = a_ref[...] - dot_nt(panel, panel)
        rest = dot_nn(l_ref[blk, :], w_ref[...])
        w_ref[blk, :] = -dot_nn(inv, rest)
        w_ref[blk, blk] = inv
        l_ref[:, blk] = panel
        l_ref[blk, blk] = up.T
        return carry

    lax.fori_loop(0, n // LANE, step, 0)


def factor(d00, d10, d11):
    n = 2 * NB
    return pl.pallas_call(
        factor_kernel,
        out_shape=[jax.ShapeDtypeStruct((n, n), jnp.float32)] * 2,
        in_specs=[pl.BlockSpec(memory_space=pltpu.VMEM)] * 3,
        out_specs=[pl.BlockSpec(memory_space=pltpu.VMEM)] * 2,
        scratch_shapes=[pltpu.VMEM((n, n), jnp.float32)],
        compiler_params=pltpu.CompilerParams(vmem_limit_bytes=32 * 2**20),
        name="factor",
    )(d00, d10, d11)


def split(x):
    hi = x.astype(jnp.bfloat16)
    return hi, (x - hi.astype(jnp.float32)).astype(jnp.bfloat16)


def dot3(a, b):
    def dot(u, v):
        return lax.dot_general(u, v, (((1,), (1,)), ((), ())), preferred_element_type=jnp.float32)

    return dot(a[0], b[0]) + (dot(a[0], b[1]) + dot(a[1], b[0]))


def solve(p0, p1, w):
    w00 = split(w[:NB, :NB])
    w10 = split(w[NB:, :NB])
    w11 = split(w[NB:, NB:])
    p0, p1 = split(p0), split(p1)
    return dot3(p0, w00), dot3(p0, w10) + dot3(p1, w11)


def update_kernel(rc_ref, cov_ref, r0_ref, r1_ref, g_ref, w_ref, l_ref, out_ref, hi_ref, lo_ref):
    step = pl.program_id(0)
    rows = cov_ref.shape[1]
    tcd = cov_ref.shape[2]

    @pl.when(step == 0)
    def _():
        w = w_ref[...]
        for b in range(tcd):
            p0 = g_ref[2 * (b % 2), :, b // 2].reshape(NB, NB)
            p1 = g_ref[2 * (b % 2) + 1, :, b // 2].reshape(NB, NB)
            for k, s in enumerate(solve(p0, p1, w)):
                hi, lo = split(s)
                hi_ref[b, :, k * NB : (k + 1) * NB] = hi
                lo_ref[b, :, k * NB : (k + 1) * NB] = lo

    s0, s1 = solve(r0_ref[0], r1_ref[0], w_ref[...])
    left = split(jnp.concatenate([s0, s1], 1))
    for b in range(tcd):
        out_ref[0, :, b, :] = cov_ref[0, :, b, :] - dot3(left, (hi_ref[b], lo_ref[b]))
    row, col = rc_ref[0], rc_ref[1]
    per_tile = NB // rows
    tile_row = row + N_ROW * (step // per_tile)

    @pl.when(jnp.logical_and(tile_row >= 2, col == 0))
    def _():
        out_ref[0, :, 0, :] = s0

    @pl.when(jnp.logical_and(tile_row >= 2, col == 1))
    def _():
        out_ref[0, :, 0, :] = s1

    @pl.when(tile_row < 2)
    def _():
        out_ref[...] = jnp.zeros_like(out_ref)

    @pl.when(jnp.logical_and(tile_row < 2, col < 2))
    def _():
        first = pl.multiple_of(tile_row * NB + lax.rem(step, per_tile) * rows, rows)
        out_ref[0, :, 0, :] = l_ref[pl.ds(first, rows), pl.ds(pl.multiple_of(col * NB, NB), NB)]


def update(cov, r0, r1, g, w, lower):
    trd, nb, tcd, _ = cov.shape
    rows = 128
    per_tile = nb // rows
    rc = jnp.stack([lax.axis_index("row"), lax.axis_index("col")]).astype(jnp.int32)
    whole = pl.BlockSpec(memory_space=pltpu.VMEM)
    block = pl.BlockSpec((1, rows, tcd, nb), lambda s: (s // per_tile, s % per_tile, 0, 0))
    piece = pl.BlockSpec((1, rows, nb), lambda s: (s // per_tile, s % per_tile, 0))
    return pl.pallas_call(
        update_kernel,
        grid=(trd * per_tile,),
        out_shape=jax.ShapeDtypeStruct(cov.shape, jnp.float32),
        in_specs=[pl.BlockSpec(memory_space=pltpu.SMEM), block, piece, piece, whole, whole, whole],
        out_specs=block,
        scratch_shapes=[pltpu.VMEM((tcd, nb, 2 * nb), jnp.bfloat16)] * 2,
        compiler_params=pltpu.CompilerParams(vmem_limit_bytes=48 * 2**20),
        name="update",
    )(rc, cov, r0, r1, g, w, lower)


def spread_diagonal(panel, x, y, z, core):
    tile = panel[0].reshape(X, NB // X, NB)
    roots = ((0, 0), (1, 0), (1, 1))
    piece = jnp.where(x == 0, tile[0], 0.0)
    for s in range(1, X):
        pairs = [(device(0, j, 0, c), device(s, j, 0, c)) for j, c in roots]
        piece = piece + lax.ppermute(tile[s], BOTH, pairs)
    first = jnp.where(y == 0, piece, 0.0)
    second = jnp.where(y == 1, piece, 0.0)
    for s in range(1, Y):
        pairs = [(device(i, j, 0, c), device(i, (j + s) % Y, 0, c)) for i in range(X) for j, c in roots]
        came = lax.ppermute(piece, BOTH, pairs)
        first = first + jnp.where(y == s, came, 0.0)
        second = second + jnp.where(y == (s + 1) % Y, came, 0.0)
    here = jnp.where(z == 0, jnp.stack([first, second]), 0.0)
    mine = here
    for s in range(1, Z):
        pairs = [(device(i, j, 0, c), device(i, j, s, c)) for i in range(X) for j in range(Y) for c in range(CORE)]
        mine = mine + lax.ppermute(here, BOTH, pairs)
    groups = [[i * Y + j for i in range(X)] for j in range(Y)]
    mine = lax.all_to_all(jnp.broadcast_to(mine[None], (X,) + mine.shape), "row", 0, 0, axis_index_groups=groups)
    mine = jnp.moveaxis(mine, 0, 1).reshape(2, NB, NB)
    other = lax.ppermute(mine, "col", [(i, i ^ 1) for i in range(N_COL)])
    d00 = jnp.where(core == 0, mine[0], other[0])
    d10 = jnp.where(core == 0, mine[1], other[1])
    d11 = jnp.where(core == 0, other[1], mine[1])
    return d00, d10, d11


def column_panels(panel, x, y):
    parts = panel.reshape(2, Y, NB // Y, NB)
    mine = None
    for s in range(Y):
        pairs = [
            (p * N_COL + k, device(2 * (p // N_COL) + k, s, (p % N_COL) // CORE, p % CORE))
            for p in range(N_ROW)
            for k in range(2)
        ]
        came = lax.ppermute(parts[:, s], BOTH, pairs)
        mine = came if mine is None else mine + came
    groups = [[i * Y + j for j in range(Y)] for i in range(X)]
    mine = lax.all_to_all(jnp.broadcast_to(mine[None], (Y,) + mine.shape), "row", 0, 0, axis_index_groups=groups)
    groups = [[i * Y + j for i in range(X)] for j in range(Y)]
    return lax.all_gather(mine, "row", axis_index_groups=groups)


def row_panels(panel, core):
    groups = [[2 * i + k for i in range(Z)] for k in range(CORE)]
    mine = lax.all_gather(panel, "col", axis_index_groups=groups)[0]
    other = lax.ppermute(mine, "col", [(i, i ^ 1) for i in range(N_COL)])
    return jnp.where(core == 0, mine, other), jnp.where(core == 0, other, mine)


def on_device(cov):
    row, col = lax.axis_index("row"), lax.axis_index("col")
    x, y, z, core = row // Y, row % Y, col // CORE, col % CORE
    panel = cov[:, :, 0, :]
    r0, r1 = row_panels(panel, core)
    g = column_panels(panel, x, y)
    d00, d10, d11 = spread_diagonal(panel, x, y, z, core)
    lower, w = factor(d00, d10, d11)
    return update(cov, r0, r1, g, w, lower)


def solution(mesh):
    placed = (P(None, "row", None, "col"),)
    return jax.shard_map(
        on_device,
        mesh=mesh,
        in_specs=placed,
        out_specs=P(None, "row", None, "col"),
        check_vma=False,
    )
```

time: 1020 us -> 177 us (0.17)
  waiting for transfers between devices: 858 us -> 10.6 us
  other arithmetic: 118 us -> 2.67 us
  starting transfers between devices: 0.43 us -> 64.5 us
  Pallas kernels: 0 us -> 36.7 us
  blocking collectives: 0 us -> 35.7 us
  matrix products: 13.1 us -> 0 us
    psum x6 -> x0, waiting for transfers between devices: 858 us -> none  [spread(): return lax.psum(block, axis)]
    another operation x18 -> x2, other arithmetic: 109 us -> 0.15 us  [the longest x1 0.08 us: update(): jnp.stack([lax.axis_index('row'), lax.axis_index('col')]).astype(jnp.int32)]
    ppermute x0 -> x27, starting transfers between devices: none -> 64.5 us  [the longest x8 30.2 us: column_panels(): came = lax.ppermute(parts[:, s], BOTH, pairs)]
    pallas_call x0 -> x2, Pallas kernels: none -> 36.7 us  [the longest x1 26.1 us: factor(): pl.pallas_call(factor_kernel, out_shape=[jax.ShapeDtypeStruct((n, n), jnp...]
    all_to_all x0 -> x2, blocking collectives: none -> 35.7 us  [the longest x1 18.2 us: column_panels(): lax.all_to_all(jnp.broadcast_to(mine[None], (Y,) + mine.shape), 'row', 0,...]
    ppermute x0 -> x27, waiting for transfers between devices: none -> 10.5 us  [the longest x7 5.77 us: spread_diagonal(): came = lax.ppermute(piece, BOTH, pairs)]
  transfers between devices with their start and end apart: 6 -> 29, of which waited for: 6 -> 5; matrix products, arithmetic and copies ran while one was open for 0% -> 4% of each run, Pallas kernels for 0% -> 15%
where the time goes in v1:
time: 177 us; the launch traced here: 176 us
  starting transfers between devices  64.5 us (36%)
  Pallas kernels  36.7 us (21%)
  blocking collectives  35.7 us (20%)
  between operations  14 us (8%)
  local copies, waits for them, and re-layouts  11.5 us (6%)
  waiting for transfers between devices  10.6 us (6%)
  other arithmetic  2.67 us (2%)
    ppermute x8, starting transfers between devices, column_panels(): came = lax.ppermute(parts[:, s], BOTH, pairs)  30.2 us
    pallas_call x1, Pallas kernels, factor(): pl.pallas_call(factor_kernel, out_shape=[jax.ShapeDtypeStruct((n, n), jnp...  26.1 us
    all_to_all x1, blocking collectives, column_panels(): lax.all_to_all(jnp.broadcast_to(mine[None], (Y,) + mine.shape), 'row', 0,...  18.2 us
    all_to_all x1, blocking collectives, spread_diagonal(): lax.all_to_all(jnp.broadcast_to(mine[None], (X,) + mine.shape), 'row', 0,...  17.5 us
    ppermute x1, starting transfers between devices, spread_diagonal(): other = lax.ppermute(mine, 'col', [(i, i ^ 1) for i in range(N_COL)])  13.9 us
    ppermute x7, starting transfers between devices, spread_diagonal(): mine = mine + lax.ppermute(here, BOTH, pairs)  11.2 us
    pallas_call x1, Pallas kernels, update(): pl.pallas_call(update_kernel, grid=(trd * per_tile,), out_shape=jax.Shape...  10.7 us
    ppermute x7, waiting for transfers between devices, spread_diagonal(): came = lax.ppermute(piece, BOTH, pairs)  5.77 us
  transfers between devices with their start and end apart: 29, of which 5 were waited for; matrix products, arithmetic and copies ran while one was open for 4% of the time, Pallas kernels for 15%

profile of v1, /device:TPU:1, one launch (start us, length us, event | category | flops | bytes accessed | tf_op | source)
XLA Modules:
  0.0 175.6 jit_solution(5164533105572091723)
XLA Ops:
  6.5 2.0 %slice.69 = f32[2,256,1,256]{3,2,1,0:T(1,128)S(1)} slice(f32[2,256,4,256]{3,2,1,0:T(4,128)} %cov_ref.1), slice={[0:2], [0:256], [0:1], [0:256]} | slice | bytes 1048576 | tf_op jit(solution)/shard_map/slice | solution.py:254
  8.5 0.8 copy.39
  9.3 0.0 all-gather.5.cloned.1.call-update
  9.3 0.0 all-gather.7.cloned.1.call-start
  9.4 1.2 slice_bitcast_fusion.9
  10.6 7.4 %collective-permute-start.8 = (f32[2,32,256]{2,1,0:T(8,128)S(1)}, f32[2,32,256]{2,1,0:T(8,128)S(1)}, u32[]{:S(2)}, u32[]{:S(2)}) collective-permute-start(f32[2,32,256]{2,1,0:T(8,128)S(1)} %get-tuple-element.28), channel_id=1, source_target_pairs={{0,112},{1,240},{16,113},{17,241},{32,114},{33,242},{48,115},{49,2... | collective-permute-start | bytes 196616 | tf_op jit(solution)/shard_map/ppermute | solution.py:236
  18.1 11.8 %collective-permute-start.7 = (f32[2,32,256]{2,1,0:T(8,128)S(1)}, f32[2,32,256]{2,1,0:T(8,128)S(1)}, u32[]{:S(2)}, u32[]{:S(2)}) collective-permute-start(f32[2,32,256]{2,1,0:T(8,128)S(1)} %get-tuple-element.29), channel_id=1, source_target_pairs={{0,96},{1,224},{16,97},{17,225},{32,98},{33,226},{48,99},{49,227},... | collective-permute-start | bytes 196616 | tf_op jit(solution)/shard_map/ppermute | solution.py:236
  29.9 1.6 collective-permute-start.6
  31.5 2.8 %collective-permute-start.5 = (f32[2,32,256]{2,1,0:T(8,128)S(1)}, f32[2,32,256]{2,1,0:T(8,128)S(1)}, u32[]{:S(2)}, u32[]{:S(2)}) collective-permute-start(f32[2,32,256]{2,1,0:T(8,128)S(1)} %get-tuple-element.24), channel_id=1, source_target_pairs={{0,64},{1,192},{16,65},{17,193},{32,66},{33,194},{48,67},{49,195},... | collective-permute-start | bytes 196616 | tf_op jit(solution)/shard_map/ppermute | solution.py:236
  34.3 1.3 collective-permute-start.4
  35.6 1.3 collective-permute-start.3
  36.9 2.8 %collective-permute-start.1 = (f32[2,32,256]{2,1,0:T(8,128)S(1)}, f32[2,32,256]{2,1,0:T(8,128)S(1)}, u32[]{:S(2)}, u32[]{:S(2)}) collective-permute-start(f32[2,32,256]{2,1,0:T(8,128)S(1)} %get-tuple-element.27), channel_id=1, source_target_pairs={{0,0},{1,128},{16,1},{17,129},{32,2},{33,130},{48,3},{49,131},{64,... | collective-permute-start | bytes 196616 | tf_op jit(solution)/shard_map/ppermute | solution.py:236
  39.7 1.3 collective-permute-start.2
  41.0 0.0 collective-permute-done.5
  41.0 0.0 collective-permute-done.3
  41.0 1.9 %collective-permute-done.1 = f32[2,32,256]{2,1,0:T(8,128)S(1)} collective-permute-done((f32[2,32,256]{2,1,0:T(8,128)S(1)}, f32[2,32,256]{2,1,0:T(8,128)S(1)}, u32[]{:S(2)}, u32[]{:S(2)}) %collective-permute-start.1) | collective-permute-done | bytes 65568 | tf_op jit(solution)/shard_map/ppermute | solution.py:236
  42.9 0.7 collective-permute-done.2
  43.7 18.2 %all_to_all.10 = f32[8,2,32,256]{3,2,1,0:T(8,128)} all-to-all(f32[8,2,32,256]{3,2,1,0:T(8,128)S(1)} %broadcast_in_dim.38), channel_id=1, replica_groups={{0,16,32,48,64,80,96,112},{128,144,160,176,192,208,224,240},{256,272,28..., dimensions={0} | all-to-all | bytes 1048576 | tf_op jit(solution)/shard_map/all_to_all | solution.py:239
  61.9 0.0 all-gather.7.cloned.1.call-update
  61.9 0.2 fusion.5
  62.1 0.7 collective-permute-start.11
  62.8 0.7 collective-permute-start.10
  63.5 0.7 collective-permute-start.9
  64.2 0.0 collective-permute-done.11
  64.2 0.0 collective-permute-done.9
  64.2 1.3 collective-permute-start.18
  65.5 0.7 collective-permute-start.17
  66.2 0.7 collective-permute-start.16
  66.9 0.7 collective-permute-start.15
  67.5 0.7 collective-permute-start.14
  68.2 5.8 %collective-permute-done.18 = f32[64,256]{1,0:T(8,128)S(1)} collective-permute-done((f32[64,256]{1,0:T(8,128)S(1)}, f32[64,256]{1,0:T(8,128)S(1)}, u32[]{:S(2)}, u32[]{:S(2)}) %collective-permute-start.18) | collective-permute-done | bytes 65568 | tf_op jit(solution)/shard_map/ppermute | solution.py:209
  74.0 0.7 collective-permute-start.13
  74.6 0.0 collective-permute-done.17
  74.6 0.7 collective-permute-start.12
  75.4 0.0 collective-permute-done.14
  75.4 0.1 add_bitcast_fusion.1
  75.5 1.3 collective-permute-start.25
  76.8 1.3 collective-permute-start.24
  78.1 3.4 %collective-permute-start.23 = (f32[2,64,256]{2,1,0:T(8,128)S(1)}, f32[2,64,256]{2,1,0:T(8,128)S(1)}, u32[]{:S(2)}, u32[]{:S(2)}) collective-permute-start(f32[2,64,256]{2,1,0:T(8,128)S(1)} %maximum_select_fusion), channel_id=1, source_target_pairs={{0,10},{1,11},{16,26},{17,27},{32,42},{33,43},{48,58},{49,59},{64,... | collective-permute-start | bytes 393224 | tf_op jit(solution)/shard_map/ppermute | solution.py:216
  81.5 1.3 collective-permute-start.22
  82.8 1.3 collective-permute-start.21
  84.1 0.0 collective-permute-done.25
  84.1 1.3 collective-permute-start.20
  85.5 1.3 collective-permute-start.19
  86.8 0.0 collective-permute-done.23
  86.8 0.7 collective-permute-done.20
  87.5 1.4 collective-permute-done.19
  88.9 0.1 add_add_fusion
  89.0 17.5 %all_to_all.11 = f32[4,2,64,256]{3,2,1,0:T(8,128)S(1)} all-to-all(f32[4,2,64,256]{3,2,1,0:T(8,128)S(1)} %broadcast_in_dim.42), channel_id=1, replica_groups={{0,128,256,384},{16,144,272,400},{32,160,288,416},{48,176,304,432},{64,..., dimensions={0} | all-to-all | bytes 1048576 | tf_op jit(solution)/shard_map/all_to_all | solution.py:218
  106.5 0.8 copy.38
  107.4 13.9 %collective-permute-start.26 = (f32[2,256,256]{2,1,0:T(8,128)}, f32[2,256,256]{2,1,0:T(8,128)}, u32[]{:S(2)}, u32[]{:S(2)}) collective-permute-start(f32[2,256,256]{2,1,0:T(8,128)} %bitcast.22), channel_id=1, source_target_pairs={{0,1},{1,0},{2,3},{3,2},{4,5},{5,4},{6,7},{7,6},{8,9},{9,8},{10,11... | collective-permute-start | bytes 1572872 | tf_op jit(solution)/shard_map/ppermute | solution.py:220
  121.3 0.0 all-gather.5.cloned.1.call-done
  121.3 1.9 %slice_bitcast_fusion = f32[2,256,256]{2,1,0:T(8,128)} fusion(f32[16,256,1,256]{3,1,0,2:T(8,128)} %bitcast.83), kind=kLoop, calls=%fused_computation | loop fusion | bytes 1048576 | tf_op jit(solution)/shard_map/squeeze | solution.py:246
  123.2 1.9 %collective-permute-start = (f32[2,256,256]{2,1,0:T(8,128)}, f32[2,256,256]{2,1,0:T(8,128)}, u32[]{:S(2)}, u32[]{:S(2)}) collective-permute-start(f32[2,256,256]{2,1,0:T(8,128)} %slice_bitcast_fusion), channel_id=1, source_target_pairs={{0,1},{1,0},{2,3},{3,2},{4,5},{5,4},{6,7},{7,6},{8,9},{9,8},{10,11... | collective-permute-start | bytes 1572872 | tf_op jit(solution)/shard_map/ppermute | solution.py:247
  125.1 0.1 pad_add_fusion.rc_ref
  125.2 1.1 bitcast_select_fusion
  126.3 26.1 %factor.1 = (f32[512,512]{1,0:T(8,128)S(1)}, f32[512,512]{1,0:T(8,128)S(1)}) custom-call(f32[256,256]{1,0:T(8,128)S(1)} %get-tuple-element.17.d00_ref, f32[256,256]{1,0:T(8,128)S(1)} %get-tuple-element.16.d10_ref, f32[256,256]{1,0:T(8,128)S(1)} %get-tuple-element.15.d11_ref), custom_call_target="tpu_custom_call" | custom-call | tf_op jit(solution)/shard_map/factor/pallas_call | solution.py:105
  152.4 1.0 copy-done.1
  153.4 1.0 copy-done.3
  154.4 1.3 broadcast_select_fusion
  155.7 0.0 all-gather.7.cloned.1.call-done
  155.7 1.2 copy-done.2
  156.9 1.2 copy-done.4
  158.1 10.7 %update.1 = f32[2,256,4,256]{3,2,1,0:T(4,128)} custom-call(s32[2]{0:T(128)S(1)} %pad_add_fusion.rc_ref, f32[2,256,4,256]{3,2,1,0:T(4,128)S(1)} %copy-done, f32[2,256,256]{2,1,0:T(8,128)S(1)} %get-tuple-element.10.r0_ref, f32[2,256,256]{2,1,0:T(8,128)S(1)} %get-tuple-element.9.r1_ref, f32[4,8,2,32,256]{4,3,2,1,0:T(8,128)} %bitcast.82, ...), custom_call_target="tpu_custom_call" | custom-call | tf_op jit(solution)/shard_map/update/pallas_call | solution.py:186
  (30 shorter events, 0.3 us)
Async XLA Ops:
  6.5 114.7 %all-gather.5.cloned.1.call-start = ((), (), s32[]{:S(2)}) async-start(), calls=%async_computation.2 | async-start | bytes 4718592 | tf_op jit(solution)/shard_map/all_gather | solution.py:246
  9.3 52.6 %copy-start = (f32[2,256,4,256]{3,2,1,0:T(4,128)S(1)}, f32[2,256,4,256]{3,2,1,0:T(4,128)}, u32[]{:S(2)}) copy-start(f32[2,256,4,256]{3,2,1,0:T(4,128)} %cov_ref.1) | copy-start | bytes 6291460
  9.3 146.3 %all-gather.7.cloned.1.call-start = ((), (), s32[]{:S(2)}) async-start(), calls=%async_computation.3 | async-start | bytes 2621440 | tf_op jit(solution)/shard_map/all_gather | solution.py:241
  10.6 24.9 %collective-permute-start.8 = (f32[2,32,256]{2,1,0:T(8,128)S(1)}, f32[2,32,256]{2,1,0:T(8,128)S(1)}, u32[]{:S(2)}, u32[]{:S(2)}) collective-permute-start(f32[2,32,256]{2,1,0:T(8,128)S(1)} %get-tuple-element.28), channel_id=1, source_target_pairs={{0,112},{1,240},{16,113},{17,241},{32,114},{33,242},{48,115},{49,2... | collective-permute-start | bytes 196616 | tf_op jit(solution)/shard_map/ppermute | solution.py:236
  18.1 18.8 %collective-permute-start.7 = (f32[2,32,256]{2,1,0:T(8,128)S(1)}, f32[2,32,256]{2,1,0:T(8,128)S(1)}, u32[]{:S(2)}, u32[]{:S(2)}) collective-permute-start(f32[2,32,256]{2,1,0:T(8,128)S(1)} %get-tuple-element.29), channel_id=1, source_target_pairs={{0,96},{1,224},{16,97},{17,225},{32,98},{33,226},{48,99},{49,227},... | collective-permute-start | bytes 196616 | tf_op jit(solution)/shard_map/ppermute | solution.py:236
  29.9 9.8 %collective-permute-start.6 = (f32[2,32,256]{2,1,0:T(8,128)S(1)}, f32[2,32,256]{2,1,0:T(8,128)S(1)}, u32[]{:S(2)}, u32[]{:S(2)}) collective-permute-start(f32[2,32,256]{2,1,0:T(8,128)S(1)} %get-tuple-element.23), channel_id=1, source_target_pairs={{0,80},{1,208},{16,81},{17,209},{32,82},{33,210},{48,83},{49,211},... | collective-permute-start | bytes 196616 | tf_op jit(solution)/shard_map/ppermute | solution.py:236
  31.5 9.5 %collective-permute-start.5 = (f32[2,32,256]{2,1,0:T(8,128)S(1)}, f32[2,32,256]{2,1,0:T(8,128)S(1)}, u32[]{:S(2)}, u32[]{:S(2)}) collective-permute-start(f32[2,32,256]{2,1,0:T(8,128)S(1)} %get-tuple-element.24), channel_id=1, source_target_pairs={{0,64},{1,192},{16,65},{17,193},{32,66},{33,194},{48,67},{49,195},... | collective-permute-start | bytes 196616 | tf_op jit(solution)/shard_map/ppermute | solution.py:236
  34.3 6.7 %collective-permute-start.4 = (f32[2,32,256]{2,1,0:T(8,128)S(1)}, f32[2,32,256]{2,1,0:T(8,128)S(1)}, u32[]{:S(2)}, u32[]{:S(2)}) collective-permute-start(f32[2,32,256]{2,1,0:T(8,128)S(1)} %get-tuple-element.25), channel_id=1, source_target_pairs={{0,48},{1,176},{16,49},{17,177},{32,50},{33,178},{48,51},{49,179},... | collective-permute-start | bytes 196616 | tf_op jit(solution)/shard_map/ppermute | solution.py:236
  35.6 5.4 %collective-permute-start.3 = (f32[2,32,256]{2,1,0:T(8,128)S(1)}, f32[2,32,256]{2,1,0:T(8,128)S(1)}, u32[]{:S(2)}, u32[]{:S(2)}) collective-permute-start(f32[2,32,256]{2,1,0:T(8,128)S(1)} %get-tuple-element.26), channel_id=1, source_target_pairs={{0,32},{1,160},{16,33},{17,161},{32,34},{33,162},{48,35},{49,163},... | collective-permute-start | bytes 196616 | tf_op jit(solution)/shard_map/ppermute | solution.py:236
  36.9 6.0 %collective-permute-start.1 = (f32[2,32,256]{2,1,0:T(8,128)S(1)}, f32[2,32,256]{2,1,0:T(8,128)S(1)}, u32[]{:S(2)}, u32[]{:S(2)}) collective-permute-start(f32[2,32,256]{2,1,0:T(8,128)S(1)} %get-tuple-element.27), channel_id=1, source_target_pairs={{0,0},{1,128},{16,1},{17,129},{32,2},{33,130},{48,3},{49,131},{64,... | collective-permute-start | bytes 196616 | tf_op jit(solution)/shard_map/ppermute | solution.py:236
  39.7 3.9 %collective-permute-start.2 = (f32[2,32,256]{2,1,0:T(8,128)S(1)}, f32[2,32,256]{2,1,0:T(8,128)S(1)}, u32[]{:S(2)}, u32[]{:S(2)}) collective-permute-start(f32[2,32,256]{2,1,0:T(8,128)S(1)} %get-tuple-element.22), channel_id=1, source_target_pairs={{0,16},{1,144},{16,17},{17,145},{32,18},{33,146},{48,19},{49,147},... | collective-permute-start | bytes 196616 | tf_op jit(solution)/shard_map/ppermute | solution.py:236
  62.1 2.1 %collective-permute-start.11 = (f32[64,256]{1,0:T(8,128)S(1)}, f32[64,256]{1,0:T(8,128)S(1)}, u32[]{:S(2)}, u32[]{:S(2)}) collective-permute-start(f32[64,256]{1,0:T(8,128)S(1)} %bitcast.85), channel_id=1, source_target_pairs={{0,384},{16,400},{17,401}} | collective-permute-start | bytes 196616 | tf_op jit(solution)/shard_map/ppermute | solution.py:204
  62.8 1.4 collective-permute-start.10
  63.5 0.7 collective-permute-start.9
  64.2 9.7 %collective-permute-start.18 = (f32[64,256]{1,0:T(8,128)S(1)}, f32[64,256]{1,0:T(8,128)S(1)}, u32[]{:S(2)}, u32[]{:S(2)}) collective-permute-start(f32[64,256]{1,0:T(8,128)S(1)} %fusion.4), channel_id=1, source_target_pairs={{0,112},{16,0},{17,1},{128,240},{144,128},{145,129},{256,368},{272... | collective-permute-start | bytes 196616 | tf_op jit(solution)/shard_map/ppermute | solution.py:209
  65.5 9.1 %collective-permute-start.17 = (f32[64,256]{1,0:T(8,128)S(1)}, f32[64,256]{1,0:T(8,128)S(1)}, u32[]{:S(2)}, u32[]{:S(2)}) collective-permute-start(f32[64,256]{1,0:T(8,128)S(1)} %fusion.4), channel_id=1, source_target_pairs={{0,96},{16,112},{17,113},{128,224},{144,240},{145,241},{256,352},{... | collective-permute-start | bytes 196616 | tf_op jit(solution)/shard_map/ppermute | solution.py:209
  66.2 9.2 %collective-permute-start.16 = (f32[64,256]{1,0:T(8,128)S(1)}, f32[64,256]{1,0:T(8,128)S(1)}, u32[]{:S(2)}, u32[]{:S(2)}) collective-permute-start(f32[64,256]{1,0:T(8,128)S(1)} %fusion.4), channel_id=1, source_target_pairs={{0,80},{16,96},{17,97},{128,208},{144,224},{145,225},{256,336},{27... | collective-permute-start | bytes 196616 | tf_op jit(solution)/shard_map/ppermute | solution.py:209
  66.9 8.5 %collective-permute-start.15 = (f32[64,256]{1,0:T(8,128)S(1)}, f32[64,256]{1,0:T(8,128)S(1)}, u32[]{:S(2)}, u32[]{:S(2)}) collective-permute-start(f32[64,256]{1,0:T(8,128)S(1)} %fusion.4), channel_id=1, source_target_pairs={{0,64},{16,80},{17,81},{128,192},{144,208},{145,209},{256,320},{27... | collective-permute-start | bytes 196616 | tf_op jit(solution)/shard_map/ppermute | solution.py:209
  67.5 7.8 %collective-permute-start.14 = (f32[64,256]{1,0:T(8,128)S(1)}, f32[64,256]{1,0:T(8,128)S(1)}, u32[]{:S(2)}, u32[]{:S(2)}) collective-permute-start(f32[64,256]{1,0:T(8,128)S(1)} %fusion.4), channel_id=1, source_target_pairs={{0,48},{16,64},{17,65},{128,176},{144,192},{145,193},{256,304},{27... | collective-permute-start | bytes 196616 | tf_op jit(solution)/shard_map/ppermute | solution.py:209
  74.0 1.4 collective-permute-start.13
  74.6 0.8 collective-permute-start.12
  75.5 8.6 %collective-permute-start.25 = (f32[2,64,256]{2,1,0:T(8,128)S(1)}, f32[2,64,256]{2,1,0:T(8,128)S(1)}, u32[]{:S(2)}, u32[]{:S(2)}) collective-permute-start(f32[2,64,256]{2,1,0:T(8,128)S(1)} %maximum_select_fusion), channel_id=1, source_target_pairs={{0,14},{1,15},{16,30},{17,31},{32,46},{33,47},{48,62},{49,63},{64,... | collective-permute-start | bytes 393224 | tf_op jit(solution)/shard_map/ppermute | solution.py:216
  76.8 8.6 %collective-permute-start.24 = (f32[2,64,256]{2,1,0:T(8,128)S(1)}, f32[2,64,256]{2,1,0:T(8,128)S(1)}, u32[]{:S(2)}, u32[]{:S(2)}) collective-permute-start(f32[2,64,256]{2,1,0:T(8,128)S(1)} %maximum_select_fusion), channel_id=1, source_target_pairs={{0,12},{1,13},{16,28},{17,29},{32,44},{33,45},{48,60},{49,61},{64,... | collective-permute-start | bytes 393224 | tf_op jit(solution)/shard_map/ppermute | solution.py:216
  78.1 8.6 %collective-permute-start.23 = (f32[2,64,256]{2,1,0:T(8,128)S(1)}, f32[2,64,256]{2,1,0:T(8,128)S(1)}, u32[]{:S(2)}, u32[]{:S(2)}) collective-permute-start(f32[2,64,256]{2,1,0:T(8,128)S(1)} %maximum_select_fusion), channel_id=1, source_target_pairs={{0,10},{1,11},{16,26},{17,27},{32,42},{33,43},{48,58},{49,59},{64,... | collective-permute-start | bytes 393224 | tf_op jit(solution)/shard_map/ppermute | solution.py:216
  81.5 5.3 %collective-permute-start.22 = (f32[2,64,256]{2,1,0:T(8,128)S(1)}, f32[2,64,256]{2,1,0:T(8,128)S(1)}, u32[]{:S(2)}, u32[]{:S(2)}) collective-permute-start(f32[2,64,256]{2,1,0:T(8,128)S(1)} %maximum_select_fusion), channel_id=1, source_target_pairs={{0,8},{1,9},{16,24},{17,25},{32,40},{33,41},{48,56},{49,57},{64,72... | collective-permute-start | bytes 393224 | tf_op jit(solution)/shard_map/ppermute | solution.py:216
  82.8 4.0 %collective-permute-start.21 = (f32[2,64,256]{2,1,0:T(8,128)S(1)}, f32[2,64,256]{2,1,0:T(8,128)S(1)}, u32[]{:S(2)}, u32[]{:S(2)}) collective-permute-start(f32[2,64,256]{2,1,0:T(8,128)S(1)} %maximum_select_fusion), channel_id=1, source_target_pairs={{0,6},{1,7},{16,22},{17,23},{32,38},{33,39},{48,54},{49,55},{64,70... | collective-permute-start | bytes 393224 | tf_op jit(solution)/shard_map/ppermute | solution.py:216
  84.1 3.4 %collective-permute-start.20 = (f32[2,64,256]{2,1,0:T(8,128)S(1)}, f32[2,64,256]{2,1,0:T(8,128)S(1)}, u32[]{:S(2)}, u32[]{:S(2)}) collective-permute-start(f32[2,64,256]{2,1,0:T(8,128)S(1)} %maximum_select_fusion), channel_id=1, source_target_pairs={{0,4},{1,5},{16,20},{17,21},{32,36},{33,37},{48,52},{49,53},{64,68... | collective-permute-start | bytes 393224 | tf_op jit(solution)/shard_map/ppermute | solution.py:216
  85.5 3.5 %collective-permute-start.19 = (f32[2,64,256]{2,1,0:T(8,128)S(1)}, f32[2,64,256]{2,1,0:T(8,128)S(1)}, u32[]{:S(2)}, u32[]{:S(2)}) collective-permute-start(f32[2,64,256]{2,1,0:T(8,128)S(1)} %maximum_select_fusion), channel_id=1, source_target_pairs={{0,2},{1,3},{16,18},{17,19},{32,34},{33,35},{48,50},{49,51},{64,66... | collective-permute-start | bytes 393224 | tf_op jit(solution)/shard_map/ppermute | solution.py:216
  107.4 17.9 %collective-permute-start.26 = (f32[2,256,256]{2,1,0:T(8,128)}, f32[2,256,256]{2,1,0:T(8,128)}, u32[]{:S(2)}, u32[]{:S(2)}) collective-permute-start(f32[2,256,256]{2,1,0:T(8,128)} %bitcast.22), channel_id=1, source_target_pairs={{0,1},{1,0},{2,3},{3,2},{4,5},{5,4},{6,7},{7,6},{8,9},{9,8},{10,11... | collective-permute-start | bytes 1572872 | tf_op jit(solution)/shard_map/ppermute | solution.py:220
  123.2 31.2 %collective-permute-start = (f32[2,256,256]{2,1,0:T(8,128)}, f32[2,256,256]{2,1,0:T(8,128)}, u32[]{:S(2)}, u32[]{:S(2)}) collective-permute-start(f32[2,256,256]{2,1,0:T(8,128)} %slice_bitcast_fusion), channel_id=1, source_target_pairs={{0,1},{1,0},{2,3},{3,2},{4,5},{5,4},{6,7},{7,6},{8,9},{9,8},{10,11... | collective-permute-start | bytes 1572872 | tf_op jit(solution)/shard_map/ppermute | solution.py:247
  152.4 1.0 copy-start.1
  153.4 1.0 copy-start.3
  155.7 1.2 copy-start.2
  156.9 1.2 copy-start.4
Sparse Core Ops, SparseCore 0:
  9.5 65.6 all-gather.4
  77.3 41.0 all-gather.6

commit v2 on v0

v2 whole, which is shorter than its diff:
```python
import jax
import jax.numpy as jnp
from jax import lax
from jax.experimental import pallas as pl
from jax.experimental.pallas import tpu as pltpu
from jax.sharding import PartitionSpec as P

LANE = 128
SUB = 8
X, Y, Z, CORE = 4, 8, 8, 2
N_ROW, N_COL = X * Y, Z * CORE
NB = 256
PART = NB // Z
BOTH = ("row", "col")
ROOTS = ((0, 0), (1, 0), (1, 1))


def device(x, y, z, core):
    return (x * Y + y) * N_COL + z * CORE + core


def dot_nt(a, b):
    return lax.dot_general(
        a, b, (((1,), (1,)), ((), ())), precision=lax.Precision.HIGHEST, preferred_element_type=jnp.float32
    )


def dot_nn(a, b):
    return lax.dot_general(
        a, b, (((1,), (0,)), ((), ())), precision=lax.Precision.HIGHEST, preferred_element_type=jnp.float32
    )


def column(rows, k):
    return jnp.broadcast_to(rows[:, k : k + 1], (SUB, LANE))


def total(terms):
    terms = list(terms)
    while len(terms) > 1:
        terms = [sum(terms[i : i + 2]) for i in range(0, len(terms), 2)]
    return terms[0]


def factor_block(rows, s_ref):
    count = len(rows)
    rows = list(rows)
    sub = lax.broadcasted_iota(jnp.int32, (SUB, LANE), 0)
    lane = lax.broadcasted_iota(jnp.int32, (SUB, LANE), 1)
    aug = [jnp.where(lane == sub + SUB * g, 1.0, 0.0).astype(jnp.float32) for g in range(count)]
    span = SUB * (SUB + 2)
    for p in range(count):
        base = (p % 2) * span
        for k in range(SUB):
            s_ref[base + SUB * k : base + SUB * (k + 1), :] = column(rows[p], SUB * p + k)
        s_ref[base + SUB * SUB : base + SUB * (SUB + 1), :] = rows[p]
        s_ref[base + SUB * (SUB + 1) : base + span, :] = aug[p]

        def spread(i, base=base):
            return jnp.broadcast_to(s_ref[base + i : base + i + 1, :], (SUB, LANE))

        a = {(m, k): spread(SUB * k + m) for k in range(SUB) for m in range(k, SUB)}
        low, scale = {}, []
        for k in range(0, SUB, 2):
            first, cross, second = a[k, k], a[k + 1, k], a[k + 1, k + 1]
            r1 = lax.rsqrt(first)
            r2 = lax.rsqrt(first * second - cross * cross) * (first * r1)
            scale += [r1, r2]
            low[k + 1, k] = cross * r1
            for m in range(k + 2, SUB):
                low[m, k] = a[m, k] * r1
                low[m, k + 1] = (a[m, k + 1] - low[m, k] * low[k + 1, k]) * r2
            for m in range(k + 2, SUB):
                for n in range(k + 2, m + 1):
                    a[m, n] = a[m, n] - (low[m, k] * low[n, k] + low[m, k + 1] * low[n, k + 1])
        xs, ys = [], []
        for k in range(SUB):
            x, y = spread(SUB * SUB + k), spread(SUB * (SUB + 1) + k)
            for j in range(k):
                x = x - low[k, j] * xs[j]
                y = y - low[k, j] * ys[j]
            xs.append(x * scale[k])
            ys.append(y * scale[k])
        for g in range(p + 1, count):
            left = []
            for k in range(SUB):
                t = column(rows[g], SUB * p + k)
                for j in range(k):
                    t = t - left[j] * low[k, j]
                left.append(t * scale[k])
            rows[g] = rows[g] - total(c * x for c, x in zip(left, xs))
            aug[g] = aug[g] - total(c * y for c, y in zip(left, ys))
        x, y = xs[0], ys[0]
        for k in range(1, SUB):
            x = jnp.where(sub == k, xs[k], x)
            y = jnp.where(sub == k, ys[k], y)
        rows[p] = jnp.where(lane >= sub + SUB * p, x, 0.0)
        aug[p] = y
    return jnp.concatenate(rows, 0), jnp.concatenate(aug, 0)


def factor_kernel(core_ref, mine_ref, other_ref, l_ref, w_ref, a_ref, s_ref):
    n = a_ref.shape[0]
    nb = n // LANE

    for core, (first, second) in enumerate(((mine_ref, other_ref), (other_ref, mine_ref))):

        @pl.when(core_ref[0] == core)
        def _():
            a_ref[:NB, :NB] = first[:, 0].reshape(NB, NB)
            a_ref[NB:, :NB] = first[:, 1].reshape(NB, NB)
            a_ref[NB:, NB:] = second[:, 1].reshape(NB, NB)

    def blk(i):
        return slice(i * LANE, (i + 1) * LANE)

    inverses = []
    for b in range(nb):
        rows = [a_ref[b * LANE + SUB * g : b * LANE + SUB * (g + 1), blk(b)] for g in range(LANE // SUB)]
        upper, inverse = factor_block(rows, s_ref)
        inverses.append(inverse)
        l_ref[blk(b), blk(b)] = upper
        for i in range(b + 1, nb):
            panel = dot_nt(a_ref[blk(i), blk(b)], inverse)
            l_ref[blk(i), blk(b)] = panel
            for j in range(b + 1, i + 1):
                a_ref[blk(i), blk(j)] = a_ref[blk(i), blk(j)] - dot_nt(panel, l_ref[blk(j), blk(b)])
        half, odd = divmod(b, 2)
        w_ref[half, blk(odd), blk(odd)] = inverse
        if odd:
            w_ref[half, blk(0), blk(1)] = jnp.zeros((LANE, LANE), jnp.float32)
            w_ref[half, blk(1), blk(0)] = -dot_nn(inverse, dot_nn(l_ref[blk(b), blk(b - 1)], inverses[b - 1]))


def factor(core, mine, other):
    n = 2 * NB
    vmem = pl.BlockSpec(memory_space=pltpu.VMEM)
    return pl.pallas_call(
        factor_kernel,
        out_shape=[jax.ShapeDtypeStruct((n, n), jnp.float32), jax.ShapeDtypeStruct((2, NB, NB), jnp.float32)],
        in_specs=[pl.BlockSpec(memory_space=pltpu.SMEM), vmem, vmem],
        out_specs=[vmem, vmem],
        scratch_shapes=[pltpu.VMEM((n, n), jnp.float32), pltpu.VMEM((2 * SUB * (SUB + 2), LANE), jnp.float32)],
        compiler_params=pltpu.CompilerParams(vmem_limit_bytes=16 * 2**20),
        name="factor",
    )(core, mine, other)


def split(x):
    hi = x.astype(jnp.bfloat16)
    rest = x - hi.astype(jnp.float32)
    mid = rest.astype(jnp.bfloat16)
    return hi, mid, (rest - mid.astype(jnp.float32)).astype(jnp.bfloat16)


def dot6(a, b):
    out = None
    for i in range(3):
        for j in range(3 - i):
            t = lax.dot_general(a[i], b[j], (((1,), (1,)), ((), ())), preferred_element_type=jnp.float32)
            out = t if out is None else out + t
    return out


def update_kernel(place_ref, cov_hbm, r_ref, g_ref, w_ref, l_ref, out_ref, cov_ref, s_ref, sem):
    trd, nb, tcd, _ = cov_ref.shape
    copy = pltpu.make_async_copy(cov_hbm, cov_ref, sem)
    copy.start()
    w0, l10, w1 = split(w_ref[0]), split(l_ref[NB:, :NB]), split(w_ref[1])

    def solve(p0, p1):
        s0 = dot6(split(p0), w0)
        a0 = split(s0)
        s1 = dot6(split(p1 - dot6(a0, l10)), w1)
        return s0, a0, s1, split(s1)

    for b in range(0, tcd, 2):
        p0, p1 = (
            jnp.concatenate([g_ref[2 * h + k, :, b // 2].reshape(NB, NB) for h in range(2)], 0) for k in range(2)
        )
        _, a0, _, a1 = solve(p0, p1)
        for j in range(3):
            for h in range(2):
                s_ref[j, b + h, :, :NB] = a0[j][h * NB : (h + 1) * NB]
                s_ref[j, b + h, :, NB:] = a1[j][h * NB : (h + 1) * NB]
    p0, p1 = (jnp.concatenate([r_ref[:, k, a].reshape(NB, NB) for a in range(trd)], 0) for k in range(2))
    s0, a0, s1, a1 = solve(p0, p1)
    left = [jnp.concatenate([u, v], 1) for u, v in zip(a0, a1)]
    copy.wait()
    for b in range(tcd):
        u = dot6(left, [s_ref[j, b] for j in range(3)])
        for a in range(trd):
            out_ref[a, :, b, :] = cov_ref[a, :, b, :] - u[a * nb : (a + 1) * nb]
    row, col = place_ref[0], place_ref[1]
    for k, s in enumerate((s0, s1)):

        @pl.when(col == k)
        def _():
            for a in range(trd):
                out_ref[a, :, 0, :] = s[a * nb : (a + 1) * nb]

    @pl.when(row < 2)
    def _():
        out_ref[0] = jnp.zeros_like(out_ref[0])

    for i in range(2):
        for j in range(i + 1):

            @pl.when(jnp.logical_and(row == i, col == j))
            def _():
                for u in range(2):
                    for v in range(2):
                        if i == j and u < v:
                            continue
                        block = l_ref[
                            i * NB + u * LANE : i * NB + (u + 1) * LANE, j * NB + v * LANE : j * NB + (v + 1) * LANE
                        ]
                        out_ref[0, u * LANE : (u + 1) * LANE, 0, v * LANE : (v + 1) * LANE] = (
                            block.T if i == j and u == v else block
                        )


def update(place, cov, r, g, w, lower):
    trd, nb, tcd, _ = cov.shape
    vmem = pl.BlockSpec(memory_space=pltpu.VMEM)
    return pl.pallas_call(
        update_kernel,
        out_shape=jax.ShapeDtypeStruct(cov.shape, jnp.float32),
        in_specs=[pl.BlockSpec(memory_space=pltpu.SMEM), pl.BlockSpec(memory_space=pl.ANY), vmem, vmem, vmem, vmem],
        out_specs=vmem,
        scratch_shapes=[
            pltpu.VMEM(cov.shape, jnp.float32),
            pltpu.VMEM((3, tcd, nb, 2 * nb), jnp.bfloat16),
            pltpu.SemaphoreType.DMA,
        ],
        compiler_params=pltpu.CompilerParams(vmem_limit_bytes=28 * 2**20),
        name="update",
    )(place, cov, r.reshape(Z, CORE, trd, PART, nb), g, w, lower)


def shared(block, groups):
    many = jnp.broadcast_to(block[None], (len(groups[0]),) + block.shape)
    return lax.all_to_all(many, "row", 0, 0, axis_index_groups=groups)


def on_device(cov):
    row, col = lax.axis_index("row"), lax.axis_index("col")
    x, z, core = row // Y, col // CORE, col % CORE
    panel = cov[:, :, 0, :].reshape(2, Z, PART, NB)

    mine = jnp.where(z == 0, panel[:, 0], 0.0)
    for s in range(1, Z):
        pairs = [(p * N_COL + k, p * N_COL + s * CORE + k) for p in range(N_ROW) for k in range(CORE)]
        mine = mine + lax.ppermute(panel[:, s], BOTH, pairs)
    r = lax.all_gather(mine, "col")

    head = jnp.where(x == 0, mine[0], 0.0)
    for s in range(1, X):
        pairs = [(device(0, y, c, k), device(s, y, c, k)) for c in range(Z) for y, k in ROOTS]
        head = head + lax.ppermute(mine[0], BOTH, pairs)

    pairs = [
        (p * N_COL + c * CORE + k, device(2 * (p // N_COL) + k, c, (p % N_COL) // CORE, p % CORE))
        for p in range(N_ROW)
        for c in range(Z)
        for k in range(CORE)
    ]
    mine = lax.ppermute(mine, BOTH, pairs)
    got = shared(jnp.concatenate([mine, head[None]]), [[i * Y + j for j in range(Y)] for i in range(X)])
    g = lax.all_gather(got[:, :2], "row", axis_index_groups=[[i * Y + j for i in range(X)] for j in range(Y)])

    many = jnp.broadcast_to(got[None, :2, 2], (Z, 2, PART, NB))
    tiles = lax.all_to_all(many, "col", 0, 0, axis_index_groups=[[c * CORE + k for c in range(Z)] for k in range(CORE)])
    other = lax.ppermute(tiles, "col", [(i, i ^ 1) for i in range(N_COL)])
    lower, w = factor(core.astype(jnp.int32).reshape(1), tiles, other)
    return update(jnp.stack([row, col]).astype(jnp.int32), cov, r, g, w, lower)


def solution(mesh):
    placed = (P(None, "row", None, "col"),)
    return jax.shard_map(
        on_device,
        mesh=mesh,
        in_specs=placed,
        out_specs=P(None, "row", None, "col"),
        check_vma=False,
    )
```

time: 1020 us -> 144 us (0.14)
  waiting for transfers between devices: 858 us -> 9.45 us
  other arithmetic: 118 us -> 1.53 us
  blocking collectives: 0 us -> 49.2 us
  starting transfers between devices: 0.43 us -> 32.8 us
  Pallas kernels: 0 us -> 26.5 us
  matrix products: 13.1 us -> 0 us
    psum x6 -> x0, waiting for transfers between devices: 858 us -> none  [spread(): return lax.psum(block, axis)]
    another operation x18 -> x1, other arithmetic: 109 us -> 0.08 us  [on_device(): return update(jnp.stack([row, col]).astype(jnp.int32), cov, r, g, w, lower)]
    all_to_all x0 -> x2, blocking collectives: none -> 49.2 us  [the longest x1 31.6 us: shared(): return lax.all_to_all(many, 'row', 0, 0, axis_index_groups=groups)]
    ppermute x0 -> x12, starting transfers between devices: none -> 32.7 us  [the longest x7 18.6 us: on_device(): mine = mine + lax.ppermute(panel[:, s], BOTH, pairs)]
    pallas_call x0 -> x2, Pallas kernels: none -> 26.5 us  [the longest x1 14.6 us: factor(): pl.pallas_call(factor_kernel, out_shape=[jax.ShapeDtypeStruct((n, n), jnp...]
  transfers between devices with their start and end apart: 6 -> 14, of which waited for: 6 -> 3; matrix products, arithmetic and copies ran while one was open for 0% -> 2% of each run, Pallas kernels for 0% -> 10%
where the time goes in v2:
time: 144 us
  blocking collectives  49.2 us (34%)
  starting transfers between devices  32.8 us (23%)
  Pallas kernels  26.5 us (18%)
  between operations  13.7 us (10%)
  local copies, waits for them, and re-layouts  10.6 us (7%)
  waiting for transfers between devices  9.45 us (7%)
  other arithmetic  1.53 us (1%)
    all_to_all x1, blocking collectives, shared(): return lax.all_to_all(many, 'row', 0, 0, axis_index_groups=groups)  31.6 us
    ppermute x7, starting transfers between devices, on_device(): mine = mine + lax.ppermute(panel[:, s], BOTH, pairs)  18.6 us
    all_to_all x1, blocking collectives, on_device(): lax.all_to_all(many, 'col', 0, 0, axis_index_groups=[[c * CORE + k for c...  17.6 us
    pallas_call x1, Pallas kernels, factor(): pl.pallas_call(factor_kernel, out_shape=[jax.ShapeDtypeStruct((n, n), jnp...  14.6 us
    pallas_call x1, Pallas kernels, update(): pl.pallas_call(update_kernel, out_shape=jax.ShapeDtypeStruct(cov.shape, j...  11.9 us
    ppermute x1, starting transfers between devices, on_device(): other = lax.ppermute(tiles, 'col', [(i, i ^ 1) for i in range(N_COL)])  7.37 us
    unnamed x15, local copies, waits for them, and re-layouts  6.88 us
    ppermute x1, waiting for transfers between devices, on_device(): mine = lax.ppermute(mine, BOTH, pairs)  6.3 us
  transfers between devices with their start and end apart: 14, of which 3 were waited for; matrix products, arithmetic and copies ran while one was open for 2% of the time, Pallas kernels for 10%

profile of v2, /device:TPU:1, one launch (start us, length us, event | category | flops | bytes accessed | tf_op | source)
XLA Modules:
  0.0 143.7 jit_solution(5901444426407765872)
XLA Ops:
  6.5 0.0 all-gather.5.cloned.1.call-start
  6.5 2.0 %slice.39 = f32[2,256,1,256]{3,2,1,0:T(1,128)S(1)} slice(f32[2,256,4,256]{3,2,1,0:T(4,128)} %cov_hbm.1), slice={[0:2], [0:256], [0:1], [0:256]} | slice | bytes 1048576 | tf_op jit(solution)/shard_map/slice | solution.py:249
  8.6 4.8 %collective-permute-start = (f32[2,32,256]{2,1,0:T(8,128)S(1)}, f32[2,32,256]{2,1,0:T(8,128)S(1)}, u32[]{:S(2)}, u32[]{:S(2)}) collective-permute-start(f32[2,32,256]{2,1,0:T(8,128)S(1)} %get-tuple-element.9), channel_id=1, source_target_pairs={{0,2},{1,3},{16,18},{17,19},{32,34},{33,35},{48,50},{49,51},{64,66... | collective-permute-start | bytes 196616 | tf_op jit(solution)/shard_map/ppermute | solution.py:254
  13.4 7.3 %collective-permute-start.4 = (f32[2,32,256]{2,1,0:T(8,128)S(1)}, f32[2,32,256]{2,1,0:T(8,128)S(1)}, u32[]{:S(2)}, u32[]{:S(2)}) collective-permute-start(f32[2,32,256]{2,1,0:T(8,128)S(1)} %get-tuple-element.10), channel_id=1, source_target_pairs={{0,10},{1,11},{16,26},{17,27},{32,42},{33,43},{48,58},{49,59},{64,... | collective-permute-start | bytes 196616 | tf_op jit(solution)/shard_map/ppermute | solution.py:254
  20.7 1.3 collective-permute-start.3
  22.0 1.3 collective-permute-start.2
  23.3 1.3 collective-permute-start.1
  24.6 0.0 collective-permute-done
  24.6 1.3 collective-permute-start.6
  25.9 0.0 collective-permute-done.4
  26.0 1.3 collective-permute-start.5
  27.3 0.0 collective-permute-done.3
  27.3 0.0 collective-permute-done.2
  27.3 0.0 collective-permute-done.1
  27.3 0.0 collective-permute-done.6
  27.3 1.7 %collective-permute-done.5 = f32[2,32,256]{2,1,0:T(8,128)S(1)} collective-permute-done((f32[2,32,256]{2,1,0:T(8,128)S(1)}, f32[2,32,256]{2,1,0:T(8,128)S(1)}, u32[]{:S(2)}, u32[]{:S(2)}) %collective-permute-start.5) | collective-permute-done | bytes 65568 | tf_op jit(solution)/shard_map/ppermute | solution.py:254
  29.0 0.7 fusion.8
  29.6 0.0 all-gather.5.cloned.1.call-update
  29.7 0.0 all-gather.7.cloned.1.call-start
  29.7 0.8 slice_bitcast_fusion.9
  30.5 0.7 collective-permute-start.9
  31.1 0.7 collective-permute-start.8
  31.8 0.7 collective-permute-start.10
  32.5 4.8 %collective-permute-start.7 = (f32[2,32,256]{2,1,0:T(8,128)}, f32[2,32,256]{2,1,0:T(8,128)S(1)}, u32[]{:S(2)}, u32[]{:S(2)}) collective-permute-start(f32[2,32,256]{2,1,0:T(8,128)} %fusion.8), channel_id=1, source_target_pairs={{0,0},{1,128},{2,16},{3,144},{4,32},{5,160},{6,48},{7,176},{8,64},... | collective-permute-start | bytes 196616 | tf_op jit(solution)/shard_map/ppermute | solution.py:268
  37.3 0.0 collective-permute-done.9
  37.3 0.0 collective-permute-done.8
  37.3 0.0 collective-permute-done.10
  37.3 0.8 add_bitcast_fusion
  38.1 6.3 %collective-permute-done.7 = f32[2,32,256]{2,1,0:T(8,128)S(1)} collective-permute-done((f32[2,32,256]{2,1,0:T(8,128)}, f32[2,32,256]{2,1,0:T(8,128)S(1)}, u32[]{:S(2)}, u32[]{:S(2)}) %collective-permute-start.7) | collective-permute-done | bytes 65568 | tf_op jit(solution)/shard_map/ppermute | solution.py:268
  44.4 0.1 broadcast_in_dim.27
  44.5 31.6 %all_to_all.10 = f32[8,3,32,256]{3,2,1,0:T(8,128)S(1)} all-to-all(f32[8,3,32,256]{3,2,1,0:T(8,128)S(1)} %broadcast_in_dim.27), channel_id=1, replica_groups={{0,16,32,48,64,80,96,112},{128,144,160,176,192,208,224,240},{256,272,28..., dimensions={0} | all-to-all | bytes 1572864 | tf_op jit(solution)/shard_map/all_to_all | solution.py:243
  76.1 0.0 copy-start
  76.1 0.8 slice.60
  76.9 0.0 all-gather.7.cloned.1.call-update
  77.0 17.6 %all_to_all.11.mine_ref = f32[8,2,32,256]{3,2,1,0:T(8,128)S(1)} all-to-all(f32[8,2,32,256]{3,2,1,0:T(8,128)S(1)} %broadcast_in_dim.29), channel_id=1, replica_groups={{0,2,4,6,8,10,12,14},{1,3,5,7,9,11,13,15},{16,18,20,22,24,26,28,30},{17..., dimensions={0} | all-to-all | bytes 1048576 | tf_op jit(solution)/shard_map/all_to_all | solution.py:273
  94.6 7.4 %collective-permute-start.11 = (f32[8,2,32,256]{3,2,1,0:T(8,128)S(1)}, f32[8,2,32,256]{3,2,1,0:T(8,128)S(1)}, u32[]{:S(2)}, u32[]{:S(2)}) collective-permute-start(f32[8,2,32,256]{3,2,1,0:T(8,128)S(1)} %all_to_all.11.mine_ref), channel_id=1, source_target_pairs={{0,1},{1,0},{2,3},{3,2},{4,5},{5,4},{6,7},{7,6},{8,9},{9,8},{10,11... | collective-permute-start | bytes 1572872 | tf_op jit(solution)/shard_map/ppermute | solution.py:274
  102.0 0.1 pad_add_fusion.place_ref
  102.1 1.4 collective-permute-done.11.other_ref
  103.5 0.0 copy-start.5
  103.5 0.8 copy-done.5
  104.3 0.0 copy-start.6
  104.3 1.0 copy-done.6
  105.4 14.6 %factor.1 = (f32[512,512]{1,0:T(8,128)S(1)}, f32[2,256,256]{2,1,0:T(8,128)S(1)}) custom-call(s32[1]{0:T(128)} %bitcast.15.core_ref, f32[8,2,32,256]{3,2,1,0:T(8,128)S(1)} %all_to_all.11.mine_ref, f32[8,2,32,256]{3,2,1,0:T(8,128)S(1)} %copy-done.6), custom_call_target="tpu_custom_call" | custom-call | tf_op jit(solution)/shard_map/factor/pallas_call | solution.py:138
  120.0 0.0 copy-start.3
  120.0 1.0 copy-done.3
  121.0 0.0 all-gather.5.cloned.1.call-done
  121.0 0.0 all-gather.7.cloned.1.call-done
  121.0 0.0 copy-done
  121.0 0.0 copy-start.1
  121.0 1.6 %copy-done.1 = f32[32,2,32,256]{3,2,1,0:T(8,128)S(1)} copy-done((f32[32,2,32,256]{3,2,1,0:T(8,128)S(1)}, f32[32,2,32,256]{3,2,1,0:T(8,128)}, u32[]{:S(2)}) %copy-start.1) | copy-done | bytes 2097176
  122.6 0.0 copy-start.2
  122.6 1.2 copy-done.2
  123.8 0.0 copy-start.4
  123.8 1.2 copy-done.4
  125.0 11.9 %update.1 = f32[2,256,4,256]{3,2,1,0:T(4,128)} custom-call(s32[2]{0:T(128)S(1)} %pad_add_fusion.place_ref, f32[2,256,4,256]{3,2,1,0:T(4,128)S(1)} %copy-done, f32[8,2,2,32,256]{4,3,2,1,0:T(8,128)S(1)} %bitcast.77, f32[4,8,2,32,256]{4,3,2,1,0:T(8,128)S(1)} %bitcast.76, f32[2,256,256]{2,1,0:T(8,128)S(1)} %get-tuple-element.7.w_ref, f32[512,512]{1,0:T(8,128)S(1)} %copy-done.4), custom_call_target="tpu_custom_call" | custom-call | tf_op jit(solution)/shard_map/update/pallas_call | solution.py:226
  (5 shorter events, 0.1 us)
Async XLA Ops:
  6.5 114.4 %all-gather.5.cloned.1.call-start = ((), (), s32[]{:S(2)}) async-start(), calls=%async_computation.2 | async-start | bytes 1114112 | tf_op jit(solution)/shard_map/all_gather | solution.py:255
  8.6 16.1 %collective-permute-start = (f32[2,32,256]{2,1,0:T(8,128)S(1)}, f32[2,32,256]{2,1,0:T(8,128)S(1)}, u32[]{:S(2)}, u32[]{:S(2)}) collective-permute-start(f32[2,32,256]{2,1,0:T(8,128)S(1)} %get-tuple-element.9), channel_id=1, source_target_pairs={{0,2},{1,3},{16,18},{17,19},{32,34},{33,35},{48,50},{49,51},{64,66... | collective-permute-start | bytes 196616 | tf_op jit(solution)/shard_map/ppermute | solution.py:254
  13.4 12.5 %collective-permute-start.4 = (f32[2,32,256]{2,1,0:T(8,128)S(1)}, f32[2,32,256]{2,1,0:T(8,128)S(1)}, u32[]{:S(2)}, u32[]{:S(2)}) collective-permute-start(f32[2,32,256]{2,1,0:T(8,128)S(1)} %get-tuple-element.10), channel_id=1, source_target_pairs={{0,10},{1,11},{16,26},{17,27},{32,42},{33,43},{48,58},{49,59},{64,... | collective-permute-start | bytes 196616 | tf_op jit(solution)/shard_map/ppermute | solution.py:254
  20.7 6.5 %collective-permute-start.3 = (f32[2,32,256]{2,1,0:T(8,128)S(1)}, f32[2,32,256]{2,1,0:T(8,128)S(1)}, u32[]{:S(2)}, u32[]{:S(2)}) collective-permute-start(f32[2,32,256]{2,1,0:T(8,128)S(1)} %get-tuple-element.11), channel_id=1, source_target_pairs={{0,8},{1,9},{16,24},{17,25},{32,40},{33,41},{48,56},{49,57},{64,72... | collective-permute-start | bytes 196616 | tf_op jit(solution)/shard_map/ppermute | solution.py:254
  22.0 5.3 %collective-permute-start.2 = (f32[2,32,256]{2,1,0:T(8,128)S(1)}, f32[2,32,256]{2,1,0:T(8,128)S(1)}, u32[]{:S(2)}, u32[]{:S(2)}) collective-permute-start(f32[2,32,256]{2,1,0:T(8,128)S(1)} %get-tuple-element.12), channel_id=1, source_target_pairs={{0,6},{1,7},{16,22},{17,23},{32,38},{33,39},{48,54},{49,55},{64,70... | collective-permute-start | bytes 196616 | tf_op jit(solution)/shard_map/ppermute | solution.py:254
  23.3 4.0 %collective-permute-start.1 = (f32[2,32,256]{2,1,0:T(8,128)S(1)}, f32[2,32,256]{2,1,0:T(8,128)S(1)}, u32[]{:S(2)}, u32[]{:S(2)}) collective-permute-start(f32[2,32,256]{2,1,0:T(8,128)S(1)} %get-tuple-element.13), channel_id=1, source_target_pairs={{0,4},{1,5},{16,20},{17,21},{32,36},{33,37},{48,52},{49,53},{64,68... | collective-permute-start | bytes 196616 | tf_op jit(solution)/shard_map/ppermute | solution.py:254
  24.6 2.7 %collective-permute-start.6 = (f32[2,32,256]{2,1,0:T(8,128)S(1)}, f32[2,32,256]{2,1,0:T(8,128)S(1)}, u32[]{:S(2)}, u32[]{:S(2)}) collective-permute-start(f32[2,32,256]{2,1,0:T(8,128)S(1)} %get-tuple-element.14), channel_id=1, source_target_pairs={{0,14},{1,15},{16,30},{17,31},{32,46},{33,47},{48,62},{49,63},{64,... | collective-permute-start | bytes 196616 | tf_op jit(solution)/shard_map/ppermute | solution.py:254
  26.0 3.0 %collective-permute-start.5 = (f32[2,32,256]{2,1,0:T(8,128)S(1)}, f32[2,32,256]{2,1,0:T(8,128)S(1)}, u32[]{:S(2)}, u32[]{:S(2)}) collective-permute-start(f32[2,32,256]{2,1,0:T(8,128)S(1)} %get-tuple-element.15), channel_id=1, source_target_pairs={{0,12},{1,13},{16,28},{17,29},{32,44},{33,45},{48,60},{49,61},{64,... | collective-permute-start | bytes 196616 | tf_op jit(solution)/shard_map/ppermute | solution.py:254
  29.7 91.3 %all-gather.7.cloned.1.call-start = ((), (), s32[]{:S(2)}) async-start(), calls=%async_computation.3 | async-start | bytes 2621440 | tf_op jit(solution)/shard_map/all_gather | solution.py:270
  30.5 6.8 %collective-permute-start.9 = (f32[32,256]{1,0:T(8,128)S(1)}, f32[32,256]{1,0:T(8,128)S(1)}, u32[]{:S(2)}, u32[]{:S(2)}) collective-permute-start(f32[32,256]{1,0:T(8,128)S(1)} %slice_bitcast_fusion.9), channel_id=1, source_target_pairs={{0,256},{16,272},{17,273},{2,258},{18,274},{19,275},{4,260},{20,27... | collective-permute-start | bytes 98312 | tf_op jit(solution)/shard_map/ppermute | solution.py:260
  31.1 6.1 %collective-permute-start.8 = (f32[32,256]{1,0:T(8,128)S(1)}, f32[32,256]{1,0:T(8,128)S(1)}, u32[]{:S(2)}, u32[]{:S(2)}) collective-permute-start(f32[32,256]{1,0:T(8,128)S(1)} %slice_bitcast_fusion.9), channel_id=1, source_target_pairs={{0,128},{16,144},{17,145},{2,130},{18,146},{19,147},{4,132},{20,14... | collective-permute-start | bytes 98312 | tf_op jit(solution)/shard_map/ppermute | solution.py:260
  31.8 5.5 %collective-permute-start.10 = (f32[32,256]{1,0:T(8,128)S(1)}, f32[32,256]{1,0:T(8,128)S(1)}, u32[]{:S(2)}, u32[]{:S(2)}) collective-permute-start(f32[32,256]{1,0:T(8,128)S(1)} %slice_bitcast_fusion.9), channel_id=1, source_target_pairs={{0,384},{16,400},{17,401},{2,386},{18,402},{19,403},{4,388},{20,40... | collective-permute-start | bytes 98312 | tf_op jit(solution)/shard_map/ppermute | solution.py:260
  32.5 11.9 %collective-permute-start.7 = (f32[2,32,256]{2,1,0:T(8,128)}, f32[2,32,256]{2,1,0:T(8,128)S(1)}, u32[]{:S(2)}, u32[]{:S(2)}) collective-permute-start(f32[2,32,256]{2,1,0:T(8,128)} %fusion.8), channel_id=1, source_target_pairs={{0,0},{1,128},{2,16},{3,144},{4,32},{5,160},{6,48},{7,176},{8,64},... | collective-permute-start | bytes 196616 | tf_op jit(solution)/shard_map/ppermute | solution.py:268
  76.1 44.9 %copy-start = (f32[2,256,4,256]{3,2,1,0:T(4,128)S(1)}, f32[2,256,4,256]{3,2,1,0:T(4,128)}, u32[]{:S(2)}) copy-start(f32[2,256,4,256]{3,2,1,0:T(4,128)} %cov_hbm.1) | copy-start | bytes 6291460
  94.6 8.9 %collective-permute-start.11 = (f32[8,2,32,256]{3,2,1,0:T(8,128)S(1)}, f32[8,2,32,256]{3,2,1,0:T(8,128)S(1)}, u32[]{:S(2)}, u32[]{:S(2)}) collective-permute-start(f32[8,2,32,256]{3,2,1,0:T(8,128)S(1)} %all_to_all.11.mine_ref), channel_id=1, source_target_pairs={{0,1},{1,0},{2,3},{3,2},{4,5},{5,4},{6,7},{7,6},{8,9},{9,8},{10,11... | collective-permute-start | bytes 1572872 | tf_op jit(solution)/shard_map/ppermute | solution.py:274
  103.5 0.8 copy-start.5
  104.3 1.0 copy-start.6
  120.0 1.0 copy-start.3
  121.0 1.6 %copy-start.1 = (f32[32,2,32,256]{3,2,1,0:T(8,128)S(1)}, f32[32,2,32,256]{3,2,1,0:T(8,128)}, u32[]{:S(2)}) copy-start(f32[32,2,32,256]{3,2,1,0:T(8,128)} %all-gather.7.cloned.1.call-done) | copy-start | bytes 6291460
  122.6 1.2 copy-start.2
  123.8 1.2 copy-start.4
Sparse Core Ops, SparseCore 0:
  29.8 43.0 all-gather.4
  77.1 31.6 all-gather.6

commit v3 on v2

--- a/solution.py
+++ b/solution.py
@@ -99,17 +99,33 @@
     return jnp.concatenate(rows, 0), jnp.concatenate(aug, 0)
 
 
-def factor_kernel(core_ref, mine_ref, other_ref, l_ref, w_ref, a_ref, s_ref):
+def split(x):
+    hi = x.astype(jnp.bfloat16)
+    rest = x - hi.astype(jnp.float32)
+    mid = rest.astype(jnp.bfloat16)
+    return hi, mid, (rest - mid.astype(jnp.float32)).astype(jnp.bfloat16)
+
+
+def dot6(a, b):
+    out = None
+    for i in range(3):
+        for j in range(3 - i):
+            t = lax.dot_general(a[i], b[j], (((1,), (1,)), ((), ())), preferred_element_type=jnp.float32)
+            out = t if out is None else out + t
+    return out
+
+
+def solve(p0, p1, w0, l10, w1):
+    a0 = split(dot6(split(p0), w0))
+    return a0, split(dot6(split(p1 - dot6(a0, l10)), w1))
+
+
+def factor_kernel(tiles_ref, r_ref, l_ref, w_ref, s_ref, a_ref, v_ref, spread_ref):
     n = a_ref.shape[0]
     nb = n // LANE
-
-    for core, (first, second) in enumerate(((mine_ref, other_ref), (other_ref, mine_ref))):
-
-        @pl.when(core_ref[0] == core)
-        def _():
-            a_ref[:NB, :NB] = first[:, 0].reshape(NB, NB)
-            a_ref[NB:, :NB] = first[:, 1].reshape(NB, NB)
-            a_ref[NB:, NB:] = second[:, 1].reshape(NB, NB)
+    a_ref[:NB, :NB] = tiles_ref[:, 0].reshape(NB, NB)
+    a_ref[NB:, :NB] = tiles_ref[:, 1].reshape(NB, NB)
+    a_ref[NB:, NB:] = tiles_ref[:, 2].reshape(NB, NB)
 
     def blk(i):
         return slice(i * LANE, (i + 1) * LANE)
@@ -117,7 +133,7 @@
     inverses = []
     for b in range(nb):
         rows = [a_ref[b * LANE + SUB * g : b * LANE + SUB * (g + 1), blk(b)] for g in range(LANE // SUB)]
-        upper, inverse = factor_block(rows, s_ref)
+        upper, inverse = factor_block(rows, spread_ref)
         inverses.append(inverse)
         l_ref[blk(b), blk(b)] = upper
         for i in range(b + 1, nb):
@@ -126,76 +142,72 @@
             for j in range(b + 1, i + 1):
                 a_ref[blk(i), blk(j)] = a_ref[blk(i), blk(j)] - dot_nt(panel, l_ref[blk(j), blk(b)])
         half, odd = divmod(b, 2)
-        w_ref[half, blk(odd), blk(odd)] = inverse
+        v_ref[half, blk(odd), blk(odd)] = inverse
         if odd:
-            w_ref[half, blk(0), blk(1)] = jnp.zeros((LANE, LANE), jnp.float32)
-            w_ref[half, blk(1), blk(0)] = -dot_nn(inverse, dot_nn(l_ref[blk(b), blk(b - 1)], inverses[b - 1]))
-
-
-def factor(core, mine, other):
+            v_ref[half, blk(0), blk(1)] = jnp.zeros((LANE, LANE), jnp.float32)
+            v_ref[half, blk(1), blk(0)] = -dot_nn(inverse, dot_nn(l_ref[blk(b), blk(b - 1)], inverses[b - 1]))
+    weights = [split(m) for m in (v_ref[0], l_ref[NB:, :NB], v_ref[1])]
+    for i, parts in enumerate(weights):
+        for j, part in enumerate(parts):
+            w_ref[i, j] = part
+    trd = r_ref.shape[2]
+    p0, p1 = (jnp.concatenate([r_ref[:, k, a].reshape(NB, NB) for a in range(trd)], 0) for k in range(2))
+    for k, parts in enumerate(solve(p0, p1, *weights)):
+        for j, part in enumerate(parts):
+            s_ref[j, :, k * NB : (k + 1) * NB] = part
+
+
+def factor(tiles, r):
     n = 2 * NB
+    trd = r.shape[1]
     vmem = pl.BlockSpec(memory_space=pltpu.VMEM)
     return pl.pallas_call(
         factor_kernel,
-        out_shape=[jax.ShapeDtypeStruct((n, n), jnp.float32), jax.ShapeDtypeStruct((2, NB, NB), jnp.float32)],
-        in_specs=[pl.BlockSpec(memory_space=pltpu.SMEM), vmem, vmem],
-        out_specs=[vmem, vmem],
-        scratch_shapes=[pltpu.VMEM((n, n), jnp.float32), pltpu.VMEM((2 * SUB * (SUB + 2), LANE), jnp.float32)],
-        compiler_params=pltpu.CompilerParams(vmem_limit_bytes=16 * 2**20),
+        out_shape=[
+            jax.ShapeDtypeStruct((n, n), jnp.float32),
+            jax.ShapeDtypeStruct((3, 3, NB, NB), jnp.bfloat16),
+            jax.ShapeDtypeStruct((3, trd * NB, n), jnp.bfloat16),
+        ],
+        in_specs=[vmem, vmem],
+        out_specs=[vmem, vmem, vmem],
+        scratch_shapes=[
+            pltpu.VMEM((n, n), jnp.float32),
+            pltpu.VMEM((2, NB, NB), jnp.float32),
+            pltpu.VMEM((2 * SUB * (SUB + 2), LANE), jnp.float32),
+        ],
+        compiler_params=pltpu.CompilerParams(vmem_limit_bytes=20 * 2**20),
         name="factor",
-    )(core, mine, other)
-
-
-def split(x):
-    hi = x.astype(jnp.bfloat16)
-    rest = x - hi.astype(jnp.float32)
-    mid = rest.astype(jnp.bfloat16)
-    return hi, mid, (rest - mid.astype(jnp.float32)).astype(jnp.bfloat16)
-
-
-def dot6(a, b):
-    out = None
-    for i in range(3):
-        for j in range(3 - i):
-            t = lax.dot_general(a[i], b[j], (((1,), (1,)), ((), ())), preferred_element_type=jnp.float32)
-            out = t if out is None else out + t
-    return out
-
-
-def update_kernel(place_ref, cov_hbm, r_ref, g_ref, w_ref, l_ref, out_ref, cov_ref, s_ref, sem):
+    )(tiles, r.reshape(Z, CORE, trd, PART, NB))
+
+
+def update_kernel(place_ref, cov_hbm, g_hbm, w_ref, l_ref, left_ref, out_ref, cov_ref, g_ref, s_ref, sems):
     trd, nb, tcd, _ = cov_ref.shape
-    copy = pltpu.make_async_copy(cov_hbm, cov_ref, sem)
-    copy.start()
-    w0, l10, w1 = split(w_ref[0]), split(l_ref[NB:, :NB]), split(w_ref[1])
-
-    def solve(p0, p1):
-        s0 = dot6(split(p0), w0)
-        a0 = split(s0)
-        s1 = dot6(split(p1 - dot6(a0, l10)), w1)
-        return s0, a0, s1, split(s1)
-
-    for b in range(0, tcd, 2):
+    copies = [pltpu.make_async_copy(g_hbm.at[:, :, a], g_ref.at[a], sems.at[a]) for a in range(2)]
+    copies.append(pltpu.make_async_copy(cov_hbm, cov_ref, sems.at[2]))
+    for copy in copies:
+        copy.start()
+    weights = [[w_ref[i, j] for j in range(3)] for i in range(3)]
+    for a in range(2):
+        copies[a].wait()
         p0, p1 = (
-            jnp.concatenate([g_ref[2 * h + k, :, b // 2].reshape(NB, NB) for h in range(2)], 0) for k in range(2)
+            jnp.concatenate([g_ref[a, :, 2 * h + k].reshape(NB, NB) for h in range(2)], 0) for k in range(2)
         )
-        _, a0, _, a1 = solve(p0, p1)
-        for j in range(3):
-            for h in range(2):
-                s_ref[j, b + h, :, :NB] = a0[j][h * NB : (h + 1) * NB]
-                s_ref[j, b + h, :, NB:] = a1[j][h * NB : (h + 1) * NB]
-    p0, p1 = (jnp.concatenate([r_ref[:, k, a].reshape(NB, NB) for a in range(trd)], 0) for k in range(2))
-    s0, a0, s1, a1 = solve(p0, p1)
-    left = [jnp.concatenate([u, v], 1) for u, v in zip(a0, a1)]
-    copy.wait()
+        for k, parts in enumerate(solve(p0, p1, *weights)):
+            for j, part in enumerate(parts):
+                for h in range(2):
+                    s_ref[j, 2 * a + h, :, k * NB : (k + 1) * NB] = part[h * NB : (h + 1) * NB]
+    left = [left_ref[j] for j in range(3)]
+    copies[2].wait()
     for b in range(tcd):
         u = dot6(left, [s_ref[j, b] for j in range(3)])
         for a in range(trd):
             out_ref[a, :, b, :] = cov_ref[a, :, b, :] - u[a * nb : (a + 1) * nb]
     row, col = place_ref[0], place_ref[1]
-    for k, s in enumerate((s0, s1)):
+    for k in range(2):
 
         @pl.when(col == k)
         def _():
+            s = sum(left_ref[j, :, k * NB : (k + 1) * NB].astype(jnp.float32) for j in (2, 1, 0))
             for a in range(trd):
                 out_ref[a, :, 0, :] = s[a * nb : (a + 1) * nb]
 
@@ -220,32 +232,38 @@
                         )
 
 
-def update(place, cov, r, g, w, lower):
+def update(place, cov, g, w, lower, left):
     trd, nb, tcd, _ = cov.shape
     vmem = pl.BlockSpec(memory_space=pltpu.VMEM)
+    hbm = pl.BlockSpec(memory_space=pl.ANY)
     return pl.pallas_call(
         update_kernel,
         out_shape=jax.ShapeDtypeStruct(cov.shape, jnp.float32),
-        in_specs=[pl.BlockSpec(memory_space=pltpu.SMEM), pl.BlockSpec(memory_space=pl.ANY), vmem, vmem, vmem, vmem],
+        in_specs=[pl.BlockSpec(memory_space=pltpu.SMEM), hbm, hbm, vmem, vmem, vmem],
         out_specs=vmem,
         scratch_shapes=[
             pltpu.VMEM(cov.shape, jnp.float32),
+            pltpu.VMEM((2, Y, X, PART, NB), jnp.float32),
             pltpu.VMEM((3, tcd, nb, 2 * nb), jnp.bfloat16),
-            pltpu.SemaphoreType.DMA,
+            pltpu.SemaphoreType.DMA((3,)),
         ],
-        compiler_params=pltpu.CompilerParams(vmem_limit_bytes=28 * 2**20),
+        compiler_params=pltpu.CompilerParams(vmem_limit_bytes=24 * 2**20),
         name="update",
-    )(place, cov, r.reshape(Z, CORE, trd, PART, nb), g, w, lower)
-
-
-def shared(block, groups):
+    )(place, cov, g, w, lower, left)
+
+
+def shared(block, axis, groups):
     many = jnp.broadcast_to(block[None], (len(groups[0]),) + block.shape)
-    return lax.all_to_all(many, "row", 0, 0, axis_index_groups=groups)
+    return lax.all_to_all(many, axis, 0, 0, axis_index_groups=groups)
 
 
 def on_device(cov):
     row, col = lax.axis_index("row"), lax.axis_index("col")
-    x, z, core = row // Y, col // CORE, col % CORE
+    y, z = row % Y, col // CORE
+    along_x = [[i * Y + j for i in range(X)] for j in range(Y)]
+    along_y = [[i * Y + j for j in range(Y)] for i in range(X)]
+    along_z = [[c * CORE + k for c in range(Z)] for k in range(CORE)]
+    chips = [[c * CORE + k for k in range(CORE)] for c in range(Z)]
     panel = cov[:, :, 0, :].reshape(2, Z, PART, NB)
 
     mine = jnp.where(z == 0, panel[:, 0], 0.0)
@@ -253,11 +271,6 @@
         pairs = [(p * N_COL + k, p * N_COL + s * CORE + k) for p in range(N_ROW) for k in range(CORE)]
         mine = mine + lax.ppermute(panel[:, s], BOTH, pairs)
     r = lax.all_gather(mine, "col")
-
-    head = jnp.where(x == 0, mine[0], 0.0)
-    for s in range(1, X):
-        pairs = [(device(0, y, c, k), device(s, y, c, k)) for c in range(Z) for y, k in ROOTS]
-        head = head + lax.ppermute(mine[0], BOTH, pairs)
 
     pairs = [
         (p * N_COL + c * CORE + k, device(2 * (p // N_COL) + k, c, (p % N_COL) // CORE, p % CORE))
@@ -265,15 +278,22 @@
         for c in range(Z)
         for k in range(CORE)
     ]
-    mine = lax.ppermute(mine, BOTH, pairs)
-    got = shared(jnp.concatenate([mine, head[None]]), [[i * Y + j for j in range(Y)] for i in range(X)])
-    g = lax.all_gather(got[:, :2], "row", axis_index_groups=[[i * Y + j for i in range(X)] for j in range(Y)])
-
-    many = jnp.broadcast_to(got[None, :2, 2], (Z, 2, PART, NB))
-    tiles = lax.all_to_all(many, "col", 0, 0, axis_index_groups=[[c * CORE + k for c in range(Z)] for k in range(CORE)])
-    other = lax.ppermute(tiles, "col", [(i, i ^ 1) for i in range(N_COL)])
-    lower, w = factor(core.astype(jnp.int32).reshape(1), tiles, other)
-    return update(jnp.stack([row, col]).astype(jnp.int32), cov, r, g, w, lower)
+    moved = lax.ppermute(mine, BOTH, pairs)
+
+    first = jnp.where(y == 0, mine[0], 0.0)
+    second = jnp.where(y == 1, mine[0], 0.0)
+    for s in range(1, Y):
+        pairs = [(device(0, j, c, k), device(0, (j + s) % Y, c, k)) for c in range(Z) for j, k in ROOTS]
+        came = lax.ppermute(mine[0], BOTH, pairs)
+        first = jnp.where(y == s, came, first)
+        second = jnp.where(y == (s + 1) % Y, came, second)
+    got = shared(jnp.concatenate([moved, first[None], second[None]]), "row", along_x)
+    g = lax.all_gather(got[:, :2], "row", axis_index_groups=along_y)
+
+    head = lax.all_gather(got[0, 2:], "col", axis_index_groups=chips)
+    tiles = shared(jnp.stack([head[0, 0], head[0, 1], head[1, 1]]), "col", along_z)
+    lower, w, left = factor(tiles, r)
+    return update(jnp.stack([row, col]).astype(jnp.int32), cov, g, w, lower, left)
 
 
 def solution(mesh):

time: 144 us -> 151 us (1.049)
  blocking collectives: 49.2 us -> 14.4 us
  waiting for transfers between devices: 9.45 us -> 37.7 us
  starting transfers between devices: 32.8 us -> 38.8 us
  local copies, waits for them, and re-layouts: 10.6 us -> 14.4 us
  Pallas kernels: 26.5 us -> 29.4 us
    all_to_all x2 -> x1, blocking collectives: 49.2 us -> 12.1 us  [shared(): return lax.all_to_all(many, axis, 0, 0, axis_index_groups=groups)]
    all_to_all x0 -> x1, waiting for transfers between devices: none -> 23.5 us  [shared(): return lax.all_to_all(many, axis, 0, 0, axis_index_groups=groups)]
    all_to_all x0 -> x1, starting transfers between devices: none -> 11.4 us  [shared(): return lax.all_to_all(many, axis, 0, 0, axis_index_groups=groups)]
    ppermute x5 -> x8, starting transfers between devices: 14.1 us -> 8.76 us  [the longest x7 5.26 us: on_device(): came = lax.ppermute(mine[0], BOTH, pairs)]
    ppermute x5 -> x8, waiting for transfers between devices: 7.74 us -> 12.5 us  [the longest x7 7.48 us: on_device(): came = lax.ppermute(mine[0], BOTH, pairs)]
    unnamed x15 -> x19, local copies, waits for them, and re-layouts: 6.88 us -> 9.93 us
    pallas_call x1, Pallas kernels: 14.6 us -> 17.5 us  [factor(): pl.pallas_call(factor_kernel, out_shape=[jax.ShapeDtypeStruct((n, n), jnp...]
    all_gather x0 -> x1, blocking collectives: none -> 2.23 us  [on_device(): head = lax.all_gather(got[0, 2:], 'col', axis_index_groups=chips)]
  transfers between devices with their start and end apart: 14 -> 18, of which waited for: 3 -> 4; matrix products, arithmetic and copies ran while one was open for 2% -> 2% of each run, Pallas kernels for 10% -> 12%
where the time goes in v3:
time: 151 us; the launch traced here: 150 us
  starting transfers between devices  38.8 us (26%)
  waiting for transfers between devices  37.7 us (25%)
  Pallas kernels  29.4 us (19%)
  local copies, waits for them, and re-layouts  14.4 us (10%)
  blocking collectives  14.4 us (10%)
  between operations  13.8 us (9%)
  other arithmetic  1.51 us (1%)
    all_to_all x1, waiting for transfers between devices, shared(): return lax.all_to_all(many, axis, 0, 0, axis_index_groups=groups)  23.5 us
    ppermute x7, starting transfers between devices, on_device(): mine = mine + lax.ppermute(panel[:, s], BOTH, pairs)  18.6 us
    pallas_call x1, Pallas kernels, factor(): pl.pallas_call(factor_kernel, out_shape=[jax.ShapeDtypeStruct((n, n), jnp...  17.5 us
    all_to_all x1, blocking collectives, shared(): return lax.all_to_all(many, axis, 0, 0, axis_index_groups=groups)  12.1 us
    pallas_call x1, Pallas kernels, update(): pl.pallas_call(update_kernel, out_shape=jax.ShapeDtypeStruct(cov.shape, j...  12 us
    all_to_all x1, starting transfers between devices, shared(): return lax.all_to_all(many, axis, 0, 0, axis_index_groups=groups)  11.4 us
    unnamed x19, local copies, waits for them, and re-layouts  9.93 us
    ppermute x7, waiting for transfers between devices, on_device(): came = lax.ppermute(mine[0], BOTH, pairs)  7.48 us
  transfers between devices with their start and end apart: 18, of which 4 were waited for; matrix products, arithmetic and copies ran while one was open for 2% of the time, Pallas kernels for 12%

profile of v3, /device:TPU:1, one launch (start us, length us, event | category | flops | bytes accessed | tf_op | source)
XLA Modules:
  0.0 150.0 jit_solution(5029998528973320566)
XLA Ops:
  6.5 0.0 all-gather.7.cloned.1.call-start
  6.5 2.0 %slice.53 = f32[2,256,1,256]{3,2,1,0:T(1,128)S(1)} slice(f32[2,256,4,256]{3,2,1,0:T(4,128)} %cov_hbm.1), slice={[0:2], [0:256], [0:1], [0:256]} | slice | bytes 1048576 | tf_op jit(solution)/shard_map/slice | solution.py:267
  8.6 4.8 %collective-permute-start = (f32[2,32,256]{2,1,0:T(8,128)S(1)}, f32[2,32,256]{2,1,0:T(8,128)S(1)}, u32[]{:S(2)}, u32[]{:S(2)}) collective-permute-start(f32[2,32,256]{2,1,0:T(8,128)S(1)} %get-tuple-element.11), channel_id=1, source_target_pairs={{0,2},{1,3},{16,18},{17,19},{32,34},{33,35},{48,50},{49,51},{64,66... | collective-permute-start | bytes 196616 | tf_op jit(solution)/shard_map/ppermute | solution.py:272
  13.4 7.3 %collective-permute-start.4 = (f32[2,32,256]{2,1,0:T(8,128)S(1)}, f32[2,32,256]{2,1,0:T(8,128)S(1)}, u32[]{:S(2)}, u32[]{:S(2)}) collective-permute-start(f32[2,32,256]{2,1,0:T(8,128)S(1)} %get-tuple-element.12), channel_id=1, source_target_pairs={{0,10},{1,11},{16,26},{17,27},{32,42},{33,43},{48,58},{49,59},{64,... | collective-permute-start | bytes 196616 | tf_op jit(solution)/shard_map/ppermute | solution.py:272
  20.7 1.3 collective-permute-start.3
  22.0 1.3 collective-permute-start.2
  23.3 1.3 collective-permute-start.1
  24.6 0.0 collective-permute-done
  24.6 1.3 collective-permute-start.6
  25.9 0.0 collective-permute-done.4
  26.0 1.3 collective-permute-start.5
  27.3 0.0 collective-permute-done.3
  27.3 0.0 collective-permute-done.2
  27.3 0.0 collective-permute-done.1
  27.3 0.0 collective-permute-done.6
  27.3 1.7 %collective-permute-done.5 = f32[2,32,256]{2,1,0:T(8,128)S(1)} collective-permute-done((f32[2,32,256]{2,1,0:T(8,128)S(1)}, f32[2,32,256]{2,1,0:T(8,128)S(1)}, u32[]{:S(2)}, u32[]{:S(2)}) %collective-permute-start.5) | collective-permute-done | bytes 65568 | tf_op jit(solution)/shard_map/ppermute | solution.py:272
  29.0 0.6 fusion.8
  29.6 0.0 all-gather.7.cloned.1.call-update
  29.6 0.0 all-gather.5.cloned.1.call-start
  29.7 0.8 slice_bitcast_fusion.11
  30.5 0.7 collective-permute-start.14
  31.1 0.7 collective-permute-start.13
  31.8 0.7 collective-permute-start.12
  32.5 0.7 collective-permute-start.11
  33.1 0.7 collective-permute-start.10
  33.8 0.0 collective-permute-done.14
  33.8 0.7 collective-permute-start.9
  34.5 0.0 collective-permute-done.13
  34.5 1.3 collective-permute-start.8
  35.8 0.0 collective-permute-done.12
  35.8 3.5 %collective-permute-start.7 = (f32[2,32,256]{2,1,0:T(8,128)}, f32[2,32,256]{2,1,0:T(8,128)S(1)}, u32[]{:S(2)}, u32[]{:S(2)}) collective-permute-start(f32[2,32,256]{2,1,0:T(8,128)} %fusion.8), channel_id=1, source_target_pairs={{0,0},{1,128},{2,16},{3,144},{4,32},{5,160},{6,48},{7,176},{8,64},... | collective-permute-start | bytes 196616 | tf_op jit(solution)/shard_map/ppermute | solution.py:281
  39.3 0.0 collective-permute-done.11
  39.3 0.0 collective-permute-done.10
  39.4 0.0 collective-permute-done.9
  39.4 7.5 %collective-permute-done.8 = f32[32,256]{1,0:T(8,128)S(1)} collective-permute-done((f32[32,256]{1,0:T(8,128)S(1)}, f32[32,256]{1,0:T(8,128)S(1)}, u32[]{:S(2)}, u32[]{:S(2)}) %collective-permute-start.8) | collective-permute-done | bytes 32800 | tf_op jit(solution)/shard_map/ppermute | solution.py:287
  46.8 0.8 select_bitcast_fusion.1
  47.6 5.0 %collective-permute-done.7 = f32[2,32,256]{2,1,0:T(8,128)S(1)} collective-permute-done((f32[2,32,256]{2,1,0:T(8,128)}, f32[2,32,256]{2,1,0:T(8,128)S(1)}, u32[]{:S(2)}, u32[]{:S(2)}) %collective-permute-start.7) | collective-permute-done | bytes 65568 | tf_op jit(solution)/shard_map/ppermute | solution.py:281
  52.7 12.1 %all_to_all.10 = f32[4,4,32,256]{3,2,1,0:T(8,128)S(1)} all-to-all(f32[4,4,32,256]{3,2,1,0:T(8,128)S(1)} %broadcast_in_dim.31), channel_id=1, replica_groups={{0,128,256,384},{16,144,272,400},{32,160,288,416},{48,176,304,432},{64,..., dimensions={0} | all-to-all | bytes 1048576 | tf_op jit(solution)/shard_map/all_to_all | solution.py:257
  64.8 0.7 slice.77
  65.5 0.0 all-gather.5.cloned.1.call-update
  65.6 2.2 %all_gather.17 = f32[2,2,32,256]{3,2,1,0:T(8,128)S(1)} all-gather(f32[1,2,32,256]{3,2,1,0:T(8,128)S(1)} %slice.78), channel_id=1, replica_groups={{0,1},{2,3},{4,5},{6,7},{8,9},{10,11},{12,13},{14,15},{16,17},{18,19},{..., dimensions={0}, use_global_device_ids=true | all-gather | bytes 196608 | tf_op jit(solution)/shard_map/all_gather | solution.py:293
  67.8 0.0 copy-start
  67.8 1.0 broadcast_in_dim.32
  68.8 11.4 %all-to-all-start.1 = ((f32[8,3,32,256]{3,2,1,0:T(8,128)}), f32[8,3,32,256]{3,2,1,0:T(8,128)S(1)}, u32[]{:S(2)}, u32[]{:S(2)}) async-start(f32[8,3,32,256]{3,2,1,0:T(8,128)} %broadcast_in_dim.32), calls=%async_computation.1 | async-start | bytes 1572864 | tf_op jit(solution)/shard_map/all_to_all | solution.py:257
  80.2 0.1 pad_add_fusion.place_ref
  80.3 23.5 %all-to-all-done.1.tiles_ref = f32[8,3,32,256]{3,2,1,0:T(8,128)S(1)} async-done(((f32[8,3,32,256]{3,2,1,0:T(8,128)}), f32[8,3,32,256]{3,2,1,0:T(8,128)S(1)}, u32[]{:S(2)}, u32[]{:S(2)}) %all-to-all-start.1) | async-done | bytes 786464 | tf_op jit(solution)/shard_map/all_to_all | solution.py:257
  103.8 0.0 all-gather.7.cloned.1.call-done
  103.8 0.0 copy-start.8
  103.8 1.2 copy-done.8
  105.0 17.5 %factor.1 = (f32[512,512]{1,0:T(8,128)S(1)}, bf16[3,3,256,256]{3,2,1,0:T(8,128)(2,1)S(1)}, bf16[3,512,512]{2,1,0:T(8,128)(2,1)S(1)}) custom-call(f32[8,3,32,256]{3,2,1,0:T(8,128)S(1)} %all-to-all-done.1.tiles_ref, f32[8,2,2,32,256]{4,3,2,1,0:T(8,128)S(1)} %bitcast.84), custom_call_target="tpu_custom_call" | custom-call | tf_op jit(solution)/shard_map/factor/pallas_call | solution.py:164
  122.5 0.0 copy-start.2
  122.5 1.1 copy-done.2
  123.6 1.0 copy-done.4
  124.7 0.0 copy-start.6
  124.7 1.0 copy-done.6
  125.7 0.0 all-gather.5.cloned.1.call-done
  125.7 0.0 copy-done
  125.7 0.0 copy-start.1
  125.7 1.6 %copy-done.1 = f32[32,2,32,256]{3,2,1,0:T(8,128)S(1)} copy-done((f32[32,2,32,256]{3,2,1,0:T(8,128)S(1)}, f32[32,2,32,256]{3,2,1,0:T(8,128)}, u32[]{:S(2)}) %copy-start.1) | copy-done | bytes 2097176
  127.3 0.0 copy-start.3
  127.3 1.4 copy-done.3
  128.7 1.3 copy-done.5
  130.0 1.2 copy-done.7
  131.2 12.0 %update.1 = f32[2,256,4,256]{3,2,1,0:T(4,128)} custom-call(s32[2]{0:T(128)S(1)} %pad_add_fusion.place_ref, f32[2,256,4,256]{3,2,1,0:T(4,128)S(1)} %copy-done, f32[8,4,2,32,256]{4,3,2,1,0:T(8,128)S(1)} %bitcast.83, bf16[3,3,256,256]{3,2,1,0:T(8,128)(2,1)S(1)} %copy-done.5, f32[512,512]{1,0:T(8,128)S(1)} %copy-done.7, bf16[3,512,512]{2,1,0:T(8,128)(2,1)S(1)} %copy-done.3), custom_call_target="tpu_custom_call" | custom-call | tf_op jit(solution)/shard_map/update/pallas_call | solution.py:239
  (10 shorter events, 0.1 us)
Async XLA Ops:
  6.5 97.3 %all-gather.7.cloned.1.call-start = ((), (), s32[]{:S(2)}) async-start(), calls=%async_computation.3 | async-start | bytes 1114112 | tf_op jit(solution)/shard_map/all_gather | solution.py:273
  8.6 16.1 %collective-permute-start = (f32[2,32,256]{2,1,0:T(8,128)S(1)}, f32[2,32,256]{2,1,0:T(8,128)S(1)}, u32[]{:S(2)}, u32[]{:S(2)}) collective-permute-start(f32[2,32,256]{2,1,0:T(8,128)S(1)} %get-tuple-element.11), channel_id=1, source_target_pairs={{0,2},{1,3},{16,18},{17,19},{32,34},{33,35},{48,50},{49,51},{64,66... | collective-permute-start | bytes 196616 | tf_op jit(solution)/shard_map/ppermute | solution.py:272
  13.4 12.5 %collective-permute-start.4 = (f32[2,32,256]{2,1,0:T(8,128)S(1)}, f32[2,32,256]{2,1,0:T(8,128)S(1)}, u32[]{:S(2)}, u32[]{:S(2)}) collective-permute-start(f32[2,32,256]{2,1,0:T(8,128)S(1)} %get-tuple-element.12), channel_id=1, source_target_pairs={{0,10},{1,11},{16,26},{17,27},{32,42},{33,43},{48,58},{49,59},{64,... | collective-permute-start | bytes 196616 | tf_op jit(solution)/shard_map/ppermute | solution.py:272
  20.7 6.5 %collective-permute-start.3 = (f32[2,32,256]{2,1,0:T(8,128)S(1)}, f32[2,32,256]{2,1,0:T(8,128)S(1)}, u32[]{:S(2)}, u32[]{:S(2)}) collective-permute-start(f32[2,32,256]{2,1,0:T(8,128)S(1)} %get-tuple-element.13), channel_id=1, source_target_pairs={{0,8},{1,9},{16,24},{17,25},{32,40},{33,41},{48,56},{49,57},{64,72... | collective-permute-start | bytes 196616 | tf_op jit(solution)/shard_map/ppermute | solution.py:272
  22.0 5.3 %collective-permute-start.2 = (f32[2,32,256]{2,1,0:T(8,128)S(1)}, f32[2,32,256]{2,1,0:T(8,128)S(1)}, u32[]{:S(2)}, u32[]{:S(2)}) collective-permute-start(f32[2,32,256]{2,1,0:T(8,128)S(1)} %get-tuple-element.14), channel_id=1, source_target_pairs={{0,6},{1,7},{16,22},{17,23},{32,38},{33,39},{48,54},{49,55},{64,70... | collective-permute-start | bytes 196616 | tf_op jit(solution)/shard_map/ppermute | solution.py:272
  23.3 4.0 %collective-permute-start.1 = (f32[2,32,256]{2,1,0:T(8,128)S(1)}, f32[2,32,256]{2,1,0:T(8,128)S(1)}, u32[]{:S(2)}, u32[]{:S(2)}) collective-permute-start(f32[2,32,256]{2,1,0:T(8,128)S(1)} %get-tuple-element.15), channel_id=1, source_target_pairs={{0,4},{1,5},{16,20},{17,21},{32,36},{33,37},{48,52},{49,53},{64,68... | collective-permute-start | bytes 196616 | tf_op jit(solution)/shard_map/ppermute | solution.py:272
  24.6 2.7 %collective-permute-start.6 = (f32[2,32,256]{2,1,0:T(8,128)S(1)}, f32[2,32,256]{2,1,0:T(8,128)S(1)}, u32[]{:S(2)}, u32[]{:S(2)}) collective-permute-start(f32[2,32,256]{2,1,0:T(8,128)S(1)} %get-tuple-element.16), channel_id=1, source_target_pairs={{0,14},{1,15},{16,30},{17,31},{32,46},{33,47},{48,62},{49,63},{64,... | collective-permute-start | bytes 196616 | tf_op jit(solution)/shard_map/ppermute | solution.py:272
  26.0 3.0 %collective-permute-start.5 = (f32[2,32,256]{2,1,0:T(8,128)S(1)}, f32[2,32,256]{2,1,0:T(8,128)S(1)}, u32[]{:S(2)}, u32[]{:S(2)}) collective-permute-start(f32[2,32,256]{2,1,0:T(8,128)S(1)} %get-tuple-element.17), channel_id=1, source_target_pairs={{0,12},{1,13},{16,28},{17,29},{32,44},{33,45},{48,60},{49,61},{64,... | collective-permute-start | bytes 196616 | tf_op jit(solution)/shard_map/ppermute | solution.py:272
  29.6 96.0 %all-gather.5.cloned.1.call-start = ((), (), s32[]{:S(2)}) async-start(), calls=%async_computation.2 | async-start | bytes 2359296 | tf_op jit(solution)/shard_map/all_gather | solution.py:291
  30.5 3.3 %collective-permute-start.14 = (f32[32,256]{1,0:T(8,128)S(1)}, f32[32,256]{1,0:T(8,128)S(1)}, u32[]{:S(2)}, u32[]{:S(2)}) collective-permute-start(f32[32,256]{1,0:T(8,128)S(1)} %slice_bitcast_fusion.11), channel_id=1, source_target_pairs={{0,16},{16,32},{17,33},{2,18},{18,34},{19,35},{4,20},{20,36},{21,3... | collective-permute-start | bytes 98312 | tf_op jit(solution)/shard_map/ppermute | solution.py:287
  31.1 3.4 %collective-permute-start.13 = (f32[32,256]{1,0:T(8,128)S(1)}, f32[32,256]{1,0:T(8,128)S(1)}, u32[]{:S(2)}, u32[]{:S(2)}) collective-permute-start(f32[32,256]{1,0:T(8,128)S(1)} %slice_bitcast_fusion.11), channel_id=1, source_target_pairs={{0,32},{16,48},{17,49},{2,34},{18,50},{19,51},{4,36},{20,52},{21,5... | collective-permute-start | bytes 98312 | tf_op jit(solution)/shard_map/ppermute | solution.py:287
  31.8 4.0 %collective-permute-start.12 = (f32[32,256]{1,0:T(8,128)S(1)}, f32[32,256]{1,0:T(8,128)S(1)}, u32[]{:S(2)}, u32[]{:S(2)}) collective-permute-start(f32[32,256]{1,0:T(8,128)S(1)} %slice_bitcast_fusion.11), channel_id=1, source_target_pairs={{0,48},{16,64},{17,65},{2,50},{18,66},{19,67},{4,52},{20,68},{21,6... | collective-permute-start | bytes 98312 | tf_op jit(solution)/shard_map/ppermute | solution.py:287
  32.5 6.9 %collective-permute-start.11 = (f32[32,256]{1,0:T(8,128)S(1)}, f32[32,256]{1,0:T(8,128)S(1)}, u32[]{:S(2)}, u32[]{:S(2)}) collective-permute-start(f32[32,256]{1,0:T(8,128)S(1)} %slice_bitcast_fusion.11), channel_id=1, source_target_pairs={{0,64},{16,80},{17,81},{2,66},{18,82},{19,83},{4,68},{20,84},{21,8... | collective-permute-start | bytes 98312 | tf_op jit(solution)/shard_map/ppermute | solution.py:287
  33.1 6.2 %collective-permute-start.10 = (f32[32,256]{1,0:T(8,128)S(1)}, f32[32,256]{1,0:T(8,128)S(1)}, u32[]{:S(2)}, u32[]{:S(2)}) collective-permute-start(f32[32,256]{1,0:T(8,128)S(1)} %slice_bitcast_fusion.11), channel_id=1, source_target_pairs={{0,80},{16,96},{17,97},{2,82},{18,98},{19,99},{4,84},{20,100},{21,... | collective-permute-start | bytes 98312 | tf_op jit(solution)/shard_map/ppermute | solution.py:287
  33.8 5.5 %collective-permute-start.9 = (f32[32,256]{1,0:T(8,128)S(1)}, f32[32,256]{1,0:T(8,128)S(1)}, u32[]{:S(2)}, u32[]{:S(2)}) collective-permute-start(f32[32,256]{1,0:T(8,128)S(1)} %slice_bitcast_fusion.11), channel_id=1, source_target_pairs={{0,96},{16,112},{17,113},{2,98},{18,114},{19,115},{4,100},{20,116}... | collective-permute-start | bytes 98312 | tf_op jit(solution)/shard_map/ppermute | solution.py:287
  34.5 12.3 %collective-permute-start.8 = (f32[32,256]{1,0:T(8,128)S(1)}, f32[32,256]{1,0:T(8,128)S(1)}, u32[]{:S(2)}, u32[]{:S(2)}) collective-permute-start(f32[32,256]{1,0:T(8,128)S(1)} %slice_bitcast_fusion.11), channel_id=1, source_target_pairs={{0,112},{16,0},{17,1},{2,114},{18,2},{19,3},{4,116},{20,4},{21,5},... | collective-permute-start | bytes 98312 | tf_op jit(solution)/shard_map/ppermute | solution.py:287
  35.8 16.8 %collective-permute-start.7 = (f32[2,32,256]{2,1,0:T(8,128)}, f32[2,32,256]{2,1,0:T(8,128)S(1)}, u32[]{:S(2)}, u32[]{:S(2)}) collective-permute-start(f32[2,32,256]{2,1,0:T(8,128)} %fusion.8), channel_id=1, source_target_pairs={{0,0},{1,128},{2,16},{3,144},{4,32},{5,160},{6,48},{7,176},{8,64},... | collective-permute-start | bytes 196616 | tf_op jit(solution)/shard_map/ppermute | solution.py:281
  67.8 57.8 %copy-start = (f32[2,256,4,256]{3,2,1,0:T(4,128)S(1)}, f32[2,256,4,256]{3,2,1,0:T(4,128)}, u32[]{:S(2)}) copy-start(f32[2,256,4,256]{3,2,1,0:T(4,128)} %cov_hbm.1) | copy-start | bytes 6291460
  68.8 35.0 %all-to-all-start.1 = ((f32[8,3,32,256]{3,2,1,0:T(8,128)}), f32[8,3,32,256]{3,2,1,0:T(8,128)S(1)}, u32[]{:S(2)}, u32[]{:S(2)}) async-start(f32[8,3,32,256]{3,2,1,0:T(8,128)} %broadcast_in_dim.32), calls=%async_computation.1 | async-start | bytes 1572864 | tf_op jit(solution)/shard_map/all_to_all | solution.py:257
  103.8 1.2 copy-start.8
  122.5 1.1 copy-start.2
  123.6 1.0 copy-start.4
  124.7 1.0 copy-start.6
  125.7 1.6 %copy-start.1 = (f32[32,2,32,256]{3,2,1,0:T(8,128)S(1)}, f32[32,2,32,256]{3,2,1,0:T(8,128)}, u32[]{:S(2)}) copy-start(f32[32,2,32,256]{3,2,1,0:T(8,128)} %all-gather.5.cloned.1.call-done) | copy-start | bytes 6291460
  127.3 1.4 copy-start.3
  128.7 1.3 copy-start.5
  130.0 1.2 copy-start.7
Sparse Core Ops, SparseCore 0:
  29.8 43.0 all-gather.6
  74.9 39.6 all-gather.4

commit v4 on v3

--- a/solution.py
+++ b/solution.py
@@ -120,9 +120,12 @@
     return a0, split(dot6(split(p1 - dot6(a0, l10)), w1))
 
 
-def factor_kernel(tiles_ref, r_ref, l_ref, w_ref, s_ref, a_ref, v_ref, spread_ref):
+def factor_kernel(tiles_ref, r_hbm, l_hbm, w_hbm, s_hbm, a_ref, l_ref, w_ref, r_ref, s_ref, spread_ref, sems):
     n = a_ref.shape[0]
     nb = n // LANE
+    trd = r_ref.shape[2]
+    fetch = pltpu.make_async_copy(r_hbm, r_ref, sems.at[0])
+    fetch.start()
     a_ref[:NB, :NB] = tiles_ref[:, 0].reshape(NB, NB)
     a_ref[NB:, :NB] = tiles_ref[:, 1].reshape(NB, NB)
     a_ref[NB:, NB:] = tiles_ref[:, 2].reshape(NB, NB)
@@ -142,62 +145,78 @@
             for j in range(b + 1, i + 1):
                 a_ref[blk(i), blk(j)] = a_ref[blk(i), blk(j)] - dot_nt(panel, l_ref[blk(j), blk(b)])
         half, odd = divmod(b, 2)
-        v_ref[half, blk(odd), blk(odd)] = inverse
+        w_ref[2 * half, blk(odd), blk(odd)] = inverse
         if odd:
-            v_ref[half, blk(0), blk(1)] = jnp.zeros((LANE, LANE), jnp.float32)
-            v_ref[half, blk(1), blk(0)] = -dot_nn(inverse, dot_nn(l_ref[blk(b), blk(b - 1)], inverses[b - 1]))
-    weights = [split(m) for m in (v_ref[0], l_ref[NB:, :NB], v_ref[1])]
-    for i, parts in enumerate(weights):
-        for j, part in enumerate(parts):
-            w_ref[i, j] = part
-    trd = r_ref.shape[2]
-    p0, p1 = (jnp.concatenate([r_ref[:, k, a].reshape(NB, NB) for a in range(trd)], 0) for k in range(2))
-    for k, parts in enumerate(solve(p0, p1, *weights)):
-        for j, part in enumerate(parts):
-            s_ref[j, :, k * NB : (k + 1) * NB] = part
+            w_ref[2 * half, blk(0), blk(1)] = jnp.zeros((LANE, LANE), jnp.float32)
+            w_ref[2 * half, blk(1), blk(0)] = -dot_nn(inverse, dot_nn(l_ref[blk(b), blk(b - 1)], inverses[b - 1]))
+        if b == 1:
+            w_ref[1] = l_ref[NB:, :NB]
+            fetch.wait()
+            p0, p1 = (jnp.concatenate([r_ref[:, k, a].reshape(NB, NB) for a in range(trd)], 0) for k in range(2))
+            s0 = dot6(split(p0), split(w_ref[0]))
+            rest = p1 - dot6(split(s0), split(w_ref[1]))
+            s_ref[:, :NB] = s0
+    stores = [
+        pltpu.make_async_copy(l_ref, l_hbm, sems.at[1]),
+        pltpu.make_async_copy(w_ref, w_hbm, sems.at[2]),
+        pltpu.make_async_copy(s_ref, s_hbm, sems.at[3]),
+    ]
+    for store in stores[:2]:
+        store.start()
+    s_ref[:, NB:] = dot6(split(rest), split(w_ref[2]))
+    stores[2].start()
+    for store in stores:
+        store.wait()
 
 
 def factor(tiles, r):
     n = 2 * NB
     trd = r.shape[1]
-    vmem = pl.BlockSpec(memory_space=pltpu.VMEM)
+    hbm = pl.BlockSpec(memory_space=pltpu.HBM)
+    r = r.reshape(Z, CORE, trd, PART, NB)
+    shapes = [(n, n), (3, NB, NB), (trd * NB, n)]
     return pl.pallas_call(
         factor_kernel,
-        out_shape=[
-            jax.ShapeDtypeStruct((n, n), jnp.float32),
-            jax.ShapeDtypeStruct((3, 3, NB, NB), jnp.bfloat16),
-            jax.ShapeDtypeStruct((3, trd * NB, n), jnp.bfloat16),
-        ],
-        in_specs=[vmem, vmem],
-        out_specs=[vmem, vmem, vmem],
+        out_shape=[jax.ShapeDtypeStruct(shape, jnp.float32) for shape in shapes],
+        in_specs=[pl.BlockSpec(memory_space=pltpu.VMEM), hbm],
+        out_specs=[hbm] * 3,
         scratch_shapes=[
             pltpu.VMEM((n, n), jnp.float32),
-            pltpu.VMEM((2, NB, NB), jnp.float32),
+            pltpu.VMEM(shapes[0], jnp.float32),
+            pltpu.VMEM(shapes[1], jnp.float32),
+            pltpu.VMEM(r.shape, jnp.float32),
+            pltpu.VMEM(shapes[2], jnp.float32),
             pltpu.VMEM((2 * SUB * (SUB + 2), LANE), jnp.float32),
+            pltpu.SemaphoreType.DMA((4,)),
         ],
         compiler_params=pltpu.CompilerParams(vmem_limit_bytes=20 * 2**20),
         name="factor",
-    )(tiles, r.reshape(Z, CORE, trd, PART, NB))
-
-
-def update_kernel(place_ref, cov_hbm, g_hbm, w_ref, l_ref, left_ref, out_ref, cov_ref, g_ref, s_ref, sems):
+    )(tiles, r)
+
+
+def update_kernel(
+    place_ref, cov_hbm, g_hbm, w_hbm, l_hbm, left_hbm, out_ref, cov_ref, g_ref, w_ref, l_ref, left_ref, s_ref, sems
+):
     trd, nb, tcd, _ = cov_ref.shape
-    copies = [pltpu.make_async_copy(g_hbm.at[:, :, a], g_ref.at[a], sems.at[a]) for a in range(2)]
-    copies.append(pltpu.make_async_copy(cov_hbm, cov_ref, sems.at[2]))
-    for copy in copies:
-        copy.start()
-    weights = [[w_ref[i, j] for j in range(3)] for i in range(3)]
+    fetches = [pltpu.make_async_copy(w_hbm, w_ref, sems.at[0])]
+    fetches += [pltpu.make_async_copy(g_hbm.at[:, :, a], g_ref.at[a], sems.at[1 + a]) for a in range(2)]
+    fetches += [pltpu.make_async_copy(left_hbm, left_ref, sems.at[3]), pltpu.make_async_copy(cov_hbm, cov_ref, sems.at[4])]
+    for fetch in fetches:
+        fetch.start()
+    fetches[0].wait()
+    weights = [split(w_ref[i]) for i in range(3)]
     for a in range(2):
-        copies[a].wait()
+        fetches[1 + a].wait()
         p0, p1 = (
-            jnp.concatenate([g_ref[a, :, 2 * h + k].reshape(NB, NB) for h in range(2)], 0) for k in range(2)
+            jnp.concatenate([g_ref[a, 2 * h + k].reshape(NB, NB) for h in range(2)], 0) for k in range(2)
         )
         for k, parts in enumerate(solve(p0, p1, *weights)):
             for j, part in enumerate(parts):
                 for h in range(2):
                     s_ref[j, 2 * a + h, :, k * NB : (k + 1) * NB] = part[h * NB : (h + 1) * NB]
-    left = [left_ref[j] for j in range(3)]
-    copies[2].wait()
+    fetches[3].wait()
+    left = split(left_ref[...])
+    fetches[4].wait()
     for b in range(tcd):
         u = dot6(left, [s_ref[j, b] for j in range(3)])
         for a in range(trd):
@@ -207,9 +226,8 @@
 
         @pl.when(col == k)
         def _():
-            s = sum(left_ref[j, :, k * NB : (k + 1) * NB].astype(jnp.float32) for j in (2, 1, 0))
             for a in range(trd):
-                out_ref[a, :, 0, :] = s[a * nb : (a + 1) * nb]
+                out_ref[a, :, 0, :] = left_ref[a * nb : (a + 1) * nb, k * NB : (k + 1) * NB]
 
     @pl.when(row < 2)
     def _():
@@ -220,13 +238,16 @@
 
             @pl.when(jnp.logical_and(row == i, col == j))
             def _():
+                fetch = pltpu.make_async_copy(
+                    l_hbm.at[i * NB : (i + 1) * NB, j * NB : (j + 1) * NB], l_ref, sems.at[5]
+                )
+                fetch.start()
+                fetch.wait()
                 for u in range(2):
                     for v in range(2):
                         if i == j and u < v:
                             continue
-                        block = l_ref[
-                            i * NB + u * LANE : i * NB + (u + 1) * LANE, j * NB + v * LANE : j * NB + (v + 1) * LANE
-                        ]
+                        block = l_ref[u * LANE : (u + 1) * LANE, v * LANE : (v + 1) * LANE]
                         out_ref[0, u * LANE : (u + 1) * LANE, 0, v * LANE : (v + 1) * LANE] = (
                             block.T if i == j and u == v else block
                         )
@@ -234,42 +255,50 @@
 
 def update(place, cov, g, w, lower, left):
     trd, nb, tcd, _ = cov.shape
-    vmem = pl.BlockSpec(memory_space=pltpu.VMEM)
-    hbm = pl.BlockSpec(memory_space=pl.ANY)
+    hbm = pl.BlockSpec(memory_space=pltpu.HBM)
     return pl.pallas_call(
         update_kernel,
         out_shape=jax.ShapeDtypeStruct(cov.shape, jnp.float32),
-        in_specs=[pl.BlockSpec(memory_space=pltpu.SMEM), hbm, hbm, vmem, vmem, vmem],
-        out_specs=vmem,
+        in_specs=[pl.BlockSpec(memory_space=pltpu.SMEM)] + [hbm] * 5,
+        out_specs=pl.BlockSpec(memory_space=pltpu.VMEM),
         scratch_shapes=[
             pltpu.VMEM(cov.shape, jnp.float32),
-            pltpu.VMEM((2, Y, X, PART, NB), jnp.float32),
+            pltpu.VMEM((2, X, Y, PART, NB), jnp.float32),
+            pltpu.VMEM(w.shape, jnp.float32),
+            pltpu.VMEM((NB, NB), jnp.float32),
+            pltpu.VMEM(left.shape, jnp.float32),
             pltpu.VMEM((3, tcd, nb, 2 * nb), jnp.bfloat16),
-            pltpu.SemaphoreType.DMA((3,)),
+            pltpu.SemaphoreType.DMA((6,)),
         ],
         compiler_params=pltpu.CompilerParams(vmem_limit_bytes=24 * 2**20),
         name="update",
     )(place, cov, g, w, lower, left)
 
 
-def shared(block, axis, groups):
+def shared(block, groups):
     many = jnp.broadcast_to(block[None], (len(groups[0]),) + block.shape)
-    return lax.all_to_all(many, axis, 0, 0, axis_index_groups=groups)
+    return lax.all_to_all(many, "row", 0, 0, axis_index_groups=groups)
 
 
 def on_device(cov):
     row, col = lax.axis_index("row"), lax.axis_index("col")
-    y, z = row % Y, col // CORE
+    x, y, z = row // Y, row % Y, col // CORE
     along_x = [[i * Y + j for i in range(X)] for j in range(Y)]
     along_y = [[i * Y + j for j in range(Y)] for i in range(X)]
-    along_z = [[c * CORE + k for c in range(Z)] for k in range(CORE)]
     chips = [[c * CORE + k for k in range(CORE)] for c in range(Z)]
-    panel = cov[:, :, 0, :].reshape(2, Z, PART, NB)
-
-    mine = jnp.where(z == 0, panel[:, 0], 0.0)
+    panel = cov[:, :, 0, :]
+
+    tile = panel[0].reshape(X, NB // X, NB)
+    head = jnp.where(x == 0, tile[0], 0.0)
+    for s in range(1, X):
+        pairs = [(device(0, j, 0, k), device(s, j, 0, k)) for j, k in ROOTS]
+        head = head + lax.ppermute(tile[s], BOTH, pairs)
+
+    parts = panel.reshape(2, Z, PART, NB)
+    mine = jnp.where(z == 0, parts[:, 0], 0.0)
     for s in range(1, Z):
         pairs = [(p * N_COL + k, p * N_COL + s * CORE + k) for p in range(N_ROW) for k in range(CORE)]
-        mine = mine + lax.ppermute(panel[:, s], BOTH, pairs)
+        mine = mine + lax.ppermute(parts[:, s], BOTH, pairs)
     r = lax.all_gather(mine, "col")
 
     pairs = [
@@ -280,18 +309,25 @@
     ]
     moved = lax.ppermute(mine, BOTH, pairs)
 
-    first = jnp.where(y == 0, mine[0], 0.0)
-    second = jnp.where(y == 1, mine[0], 0.0)
+    first = jnp.where(y == 0, head, 0.0)
+    second = jnp.where(y == 1, head, 0.0)
     for s in range(1, Y):
-        pairs = [(device(0, j, c, k), device(0, (j + s) % Y, c, k)) for c in range(Z) for j, k in ROOTS]
-        came = lax.ppermute(mine[0], BOTH, pairs)
+        pairs = [(device(i, j, 0, k), device(i, (j + s) % Y, 0, k)) for i in range(X) for j, k in ROOTS]
+        came = lax.ppermute(head, BOTH, pairs)
         first = jnp.where(y == s, came, first)
         second = jnp.where(y == (s + 1) % Y, came, second)
-    got = shared(jnp.concatenate([moved, first[None], second[None]]), "row", along_x)
-    g = lax.all_gather(got[:, :2], "row", axis_index_groups=along_y)
-
-    head = lax.all_gather(got[0, 2:], "col", axis_index_groups=chips)
-    tiles = shared(jnp.stack([head[0, 0], head[0, 1], head[1, 1]]), "col", along_z)
+    here = jnp.stack([first, second])
+    moved, here = lax.optimization_barrier((moved, here))
+    head = jnp.where(z == 0, here, 0.0)
+    for s in range(1, Z):
+        pairs = [(device(i, j, 0, k), device(i, j, s, k)) for i in range(X) for j in range(Y) for k in range(CORE)]
+        head = head + lax.ppermute(here, BOTH, pairs)
+
+    got = shared(moved, along_y)
+    g = lax.all_gather(got, "row", axis_index_groups=along_x)
+
+    head = lax.all_gather(head, "col", axis_index_groups=chips)
+    tiles = shared(jnp.stack([head[0, 0], head[0, 1], head[1, 1]]), along_x)
     lower, w, left = factor(tiles, r)
     return update(jnp.stack([row, col]).astype(jnp.int32), cov, g, w, lower, left)
 

time: 151 us -> 167 us (1.11)
  starting transfers between devices: 38.8 us -> 64.3 us
  waiting for transfers between devices: 37.7 us -> 22.3 us
  blocking collectives: 14.4 us -> 22.3 us
  local copies, waits for them, and re-layouts: 14.4 us -> 12.6 us
    ppermute x14 -> x24, starting transfers between devices: 23.9 us -> 42.1 us  [the longest x7 18.6 us: on_device(): mine = mine + lax.ppermute(parts[:, s], BOTH, pairs)]
    ppermute x1, starting transfers between devices: 3.5 us -> 18.7 us  [on_device(): moved = lax.ppermute(mine, BOTH, pairs)]
    all_to_all x1, waiting for transfers between devices: 23.5 us -> 11.9 us  [shared(): return lax.all_to_all(many, 'row', 0, 0, axis_index_groups=groups)]
    all_to_all x1, starting transfers between devices: 11.4 us -> 3.49 us  [shared(): return lax.all_to_all(many, 'row', 0, 0, axis_index_groups=groups)]
    all_to_all x1, blocking collectives: 12.1 us -> 19.5 us  [shared(): return lax.all_to_all(many, 'row', 0, 0, axis_index_groups=groups)]
    ppermute x1, waiting for transfers between devices: 5 us -> 1.69 us  [on_device(): moved = lax.ppermute(mine, BOTH, pairs)]
    unnamed x19 -> x22, local copies, waits for them, and re-layouts: 9.93 us -> 9.27 us
    ppermute x14 -> x24, waiting for transfers between devices: 9.15 us -> 8.63 us  [the longest x7 6.94 us: on_device(): head = head + lax.ppermute(here, BOTH, pairs)]
  transfers between devices with their start and end apart: 18 -> 28, of which waited for: 4 -> 6; matrix products, arithmetic and copies ran while one was open for 2% -> 1% of each run, Pallas kernels for 12% -> 11%
where the time goes in v4:
time: 167 us; the launch traced here: 166 us
  starting transfers between devices  64.3 us (39%)
  Pallas kernels  30.1 us (18%)
  waiting for transfers between devices  22.3 us (13%)
  blocking collectives  22.3 us (13%)
  between operations  14 us (8%)
  local copies, waits for them, and re-layouts  12.6 us (8%)
    all_to_all x1, blocking collectives, shared(): return lax.all_to_all(many, 'row', 0, 0, axis_index_groups=groups)  19.5 us
    ppermute x1, starting transfers between devices, on_device(): moved = lax.ppermute(mine, BOTH, pairs)  18.7 us
    ppermute x7, starting transfers between devices, on_device(): mine = mine + lax.ppermute(parts[:, s], BOTH, pairs)  18.6 us
    pallas_call x1, Pallas kernels, factor(): pl.pallas_call(factor_kernel, out_shape=[jax.ShapeDtypeStruct(shape, jnp....  17.6 us
    ppermute x7, starting transfers between devices, on_device(): head = head + lax.ppermute(here, BOTH, pairs)  16.2 us
    pallas_call x1, Pallas kernels, update(): pl.pallas_call(update_kernel, out_shape=jax.ShapeDtypeStruct(cov.shape, j...  12.5 us
    all_to_all x1, waiting for transfers between devices, shared(): return lax.all_to_all(many, 'row', 0, 0, axis_index_groups=groups)  11.9 us
    unnamed x22, local copies, waits for them, and re-layouts  9.27 us
  transfers between devices with their start and end apart: 28, of which 6 were waited for; matrix products, arithmetic and copies ran while one was open for 1% of the time, Pallas kernels for 11%

profile of v4, /device:TPU:1, one launch (start us, length us, event | category | flops | bytes accessed | tf_op | source)
XLA Modules:
  0.0 166.5 jit_solution(5332109176426732656)
XLA Ops:
  6.5 2.1 %slice.59 = f32[2,256,1,256]{3,2,1,0:T(1,128)S(1)} slice(f32[2,256,4,256]{3,2,1,0:T(4,128)} %cov_hbm.1), slice={[0:2], [0:256], [0:1], [0:256]} | slice | bytes 1048576 | tf_op jit(solution)/shard_map/slice | solution.py:289
  8.7 4.8 %collective-permute-start = (f32[2,32,256]{2,1,0:T(8,128)S(1)}, f32[2,32,256]{2,1,0:T(8,128)S(1)}, u32[]{:S(2)}, u32[]{:S(2)}) collective-permute-start(f32[2,32,256]{2,1,0:T(8,128)S(1)} %get-tuple-element.21), channel_id=1, source_target_pairs={{0,2},{1,3},{16,18},{17,19},{32,34},{33,35},{48,50},{49,51},{64,66... | collective-permute-start | bytes 196616 | tf_op jit(solution)/shard_map/ppermute | solution.py:301
  13.6 7.3 %collective-permute-start.4 = (f32[2,32,256]{2,1,0:T(8,128)S(1)}, f32[2,32,256]{2,1,0:T(8,128)S(1)}, u32[]{:S(2)}, u32[]{:S(2)}) collective-permute-start(f32[2,32,256]{2,1,0:T(8,128)S(1)} %get-tuple-element.22), channel_id=1, source_target_pairs={{0,10},{1,11},{16,26},{17,27},{32,42},{33,43},{48,58},{49,59},{64,... | collective-permute-start | bytes 196616 | tf_op jit(solution)/shard_map/ppermute | solution.py:301
  20.9 1.3 collective-permute-start.3
  22.2 1.3 collective-permute-start.2
  23.5 1.3 collective-permute-start.1
  24.8 1.3 collective-permute-start.6
  26.1 0.0 collective-permute-done.4
  26.1 1.3 collective-permute-start.5
  27.4 0.0 collective-permute-done.3
  27.5 0.0 collective-permute-done.6
  27.5 1.7 collective-permute-done.5
  29.1 0.7 fusion.8
  29.8 0.0 all-gather.8.cloned.1.call-update
  29.8 0.0 all-gather.6.cloned.1.call-start
  29.9 0.2 fusion.13
  30.1 0.7 collective-permute-start.10
  30.8 0.7 collective-permute-start.9
  31.4 0.7 collective-permute-start.8
  32.2 0.0 collective-permute-done.8
  32.2 0.7 collective-permute-start.17
  32.9 0.7 collective-permute-start.16
  33.5 0.7 collective-permute-start.15
  34.2 0.7 collective-permute-start.14
  34.9 0.7 collective-permute-start.13
  35.6 0.0 collective-permute-done.17
  35.6 0.7 collective-permute-start.12
  36.2 0.0 collective-permute-done.16
  36.3 1.3 collective-permute-start.11
  37.6 0.0 collective-permute-done.15
  37.6 18.7 %collective-permute-start.7 = (f32[2,32,256]{2,1,0:T(8,128)}, f32[2,32,256]{2,1,0:T(8,128)S(1)}, u32[]{:S(2)}, u32[]{:S(2)}) collective-permute-start(f32[2,32,256]{2,1,0:T(8,128)} %fusion.8), channel_id=1, source_target_pairs={{0,0},{1,128},{2,16},{3,144},{4,32},{5,160},{6,48},{7,176},{8,64},... | collective-permute-start | bytes 196616 | tf_op jit(solution)/shard_map/ppermute | solution.py:310
  56.3 0.0 collective-permute-done.14
  56.3 0.0 collective-permute-done.13
  56.3 0.0 collective-permute-done.11
  56.4 1.7 %collective-permute-done.7 = f32[2,32,256]{2,1,0:T(8,128)S(1)} collective-permute-done((f32[2,32,256]{2,1,0:T(8,128)}, f32[2,32,256]{2,1,0:T(8,128)S(1)}, u32[]{:S(2)}, u32[]{:S(2)}) %collective-permute-start.7) | collective-permute-done | bytes 65568 | tf_op jit(solution)/shard_map/ppermute | solution.py:310
  58.1 19.5 %all_to_all.10 = f32[8,2,32,256]{3,2,1,0:T(8,128)} all-to-all(f32[8,2,32,256]{3,2,1,0:T(8,128)S(1)} %broadcast_in_dim.31), channel_id=1, replica_groups={{0,16,32,48,64,80,96,112},{128,144,160,176,192,208,224,240},{256,272,28..., dimensions={0} | all-to-all | bytes 1048576 | tf_op jit(solution)/shard_map/all_to_all | solution.py:280
  77.6 0.0 all-gather.6.cloned.1.call-update
  77.6 1.3 collective-permute-start.24
  78.9 1.3 collective-permute-start.23
  80.2 6.3 %collective-permute-start.22 = (f32[2,64,256]{2,1,0:T(8,128)S(1)}, f32[2,64,256]{2,1,0:T(8,128)S(1)}, u32[]{:S(2)}, u32[]{:S(2)}) collective-permute-start(f32[2,64,256]{2,1,0:T(8,128)S(1)} %pad_maximum_fusion.1), channel_id=1, source_target_pairs={{0,10},{1,11},{16,26},{17,27},{32,42},{33,43},{48,58},{49,59},{64,... | collective-permute-start | bytes 393224 | tf_op jit(solution)/shard_map/ppermute | solution.py:324
  86.6 3.4 %collective-permute-start.21 = (f32[2,64,256]{2,1,0:T(8,128)S(1)}, f32[2,64,256]{2,1,0:T(8,128)S(1)}, u32[]{:S(2)}, u32[]{:S(2)}) collective-permute-start(f32[2,64,256]{2,1,0:T(8,128)S(1)} %pad_maximum_fusion.1), channel_id=1, source_target_pairs={{0,8},{1,9},{16,24},{17,25},{32,40},{33,41},{48,56},{49,57},{64,72... | collective-permute-start | bytes 393224 | tf_op jit(solution)/shard_map/ppermute | solution.py:324
  89.9 1.3 collective-permute-start.20
  91.3 1.3 collective-permute-start.19
  92.6 1.3 collective-permute-start.18
  93.9 1.3 collective-permute-done.20
  95.2 2.8 %collective-permute-done.19 = f32[2,64,256]{2,1,0:T(8,128)S(1)} collective-permute-done((f32[2,64,256]{2,1,0:T(8,128)S(1)}, f32[2,64,256]{2,1,0:T(8,128)S(1)}, u32[]{:S(2)}, u32[]{:S(2)}) %collective-permute-start.19) | collective-permute-done | bytes 131104 | tf_op jit(solution)/shard_map/ppermute | solution.py:324
  98.0 2.8 %collective-permute-done.18 = f32[2,64,256]{2,1,0:T(8,128)S(1)} collective-permute-done((f32[2,64,256]{2,1,0:T(8,128)S(1)}, f32[2,64,256]{2,1,0:T(8,128)S(1)}, u32[]{:S(2)}, u32[]{:S(2)}) %collective-permute-start.18) | collective-permute-done | bytes 131104 | tf_op jit(solution)/shard_map/ppermute | solution.py:324
  100.8 0.1 add_add_fusion
  100.9 2.9 %all-gather.1 = f32[4,64,256]{2,1,0:T(8,128)S(1)} all-gather(f32[2,64,256]{2,1,0:T(8,128)S(1)} %add_add_fusion), channel_id=3, replica_groups={{0,1},{2,3},{4,5},{6,7},{8,9},{10,11},{12,13},{14,15},{16,17},{18,19},{..., dimensions={0}, use_global_device_ids=true | all-gather | bytes 393216 | tf_op jit(solution)/shard_map/all_gather | solution.py:329
  103.8 0.9 broadcast_in_dim.33
  104.8 3.5 %all-to-all-start.1 = ((f32[4,3,64,256]{3,2,1,0:T(8,128)}), f32[4,3,64,256]{3,2,1,0:T(8,128)S(1)}, u32[]{:S(2)}, u32[]{:S(2)}) async-start(f32[4,3,64,256]{3,2,1,0:T(8,128)} %broadcast_in_dim.33), calls=%async_computation.1 | async-start | bytes 1572864 | tf_op jit(solution)/shard_map/all_to_all | solution.py:280
  108.3 0.1 pad_add_fusion.place_ref
  108.3 11.9 %all-to-all-done.1.tiles_ref = f32[4,3,64,256]{3,2,1,0:T(8,128)S(1)} async-done(((f32[4,3,64,256]{3,2,1,0:T(8,128)}), f32[4,3,64,256]{3,2,1,0:T(8,128)S(1)}, u32[]{:S(2)}, u32[]{:S(2)}) %all-to-all-start.1) | async-done | bytes 786464 | tf_op jit(solution)/shard_map/all_to_all | solution.py:280
  120.3 1.2 copy-done.6
  121.5 17.6 %factor.1 = (f32[512,512]{1,0:T(8,128)S(1)}, f32[3,256,256]{2,1,0:T(8,128)S(1)}, f32[512,512]{1,0:T(8,128)S(1)}) custom-call(f32[4,3,64,256]{3,2,1,0:T(8,128)S(1)} %all-to-all-done.1.tiles_ref, f32[8,2,2,32,256]{4,3,2,1,0:T(8,128)S(1)} %bitcast.96), custom_call_target="tpu_custom_call" | custom-call | tf_op jit(solution)/shard_map/factor/pallas_call | solution.py:178
  139.1 0.0 copy-start.2
  139.1 1.0 copy-done.2
  140.1 1.0 copy-done.4
  141.1 0.9 copy-done.7
  142.0 1.6 copy-done.1
  143.6 1.2 copy-done.3
  144.8 1.2 copy-done.5
  146.0 1.1 copy-done.8
  147.1 12.5 %update.1 = f32[2,256,4,256]{3,2,1,0:T(4,128)} custom-call(s32[2]{0:T(128)S(1)} %pad_add_fusion.place_ref, f32[2,256,4,256]{3,2,1,0:T(4,128)S(1)} %copy-done, f32[4,8,2,32,256]{4,3,2,1,0:T(8,128)S(1)} %bitcast.95, f32[3,256,256]{2,1,0:T(8,128)S(1)} %copy-done.8, f32[512,512]{1,0:T(8,128)S(1)} %copy-done.3, f32[512,512]{1,0:T(8,128)S(1)} %copy-done.5), custom_call_target="tpu_custom_call" | custom-call | tf_op jit(solution)/shard_map/update/pallas_call | solution.py:259
  (33 shorter events, 0.3 us)
Async XLA Ops:
  6.5 23.3 %copy-start = (f32[2,256,4,256]{3,2,1,0:T(4,128)S(1)}, f32[2,256,4,256]{3,2,1,0:T(4,128)}, u32[]{:S(2)}) copy-start(f32[2,256,4,256]{3,2,1,0:T(4,128)} %cov_hbm.1) | copy-start | bytes 6291460
  6.5 113.7 %all-gather.8.cloned.1.call-start = ((), (), s32[]{:S(2)}) async-start(), calls=%async_computation.3 | async-start | bytes 1114112 | tf_op jit(solution)/shard_map/all_gather | solution.py:302
  8.7 16.1 %collective-permute-start = (f32[2,32,256]{2,1,0:T(8,128)S(1)}, f32[2,32,256]{2,1,0:T(8,128)S(1)}, u32[]{:S(2)}, u32[]{:S(2)}) collective-permute-start(f32[2,32,256]{2,1,0:T(8,128)S(1)} %get-tuple-element.21), channel_id=1, source_target_pairs={{0,2},{1,3},{16,18},{17,19},{32,34},{33,35},{48,50},{49,51},{64,66... | collective-permute-start | bytes 196616 | tf_op jit(solution)/shard_map/ppermute | solution.py:301
  13.6 12.5 %collective-permute-start.4 = (f32[2,32,256]{2,1,0:T(8,128)S(1)}, f32[2,32,256]{2,1,0:T(8,128)S(1)}, u32[]{:S(2)}, u32[]{:S(2)}) collective-permute-start(f32[2,32,256]{2,1,0:T(8,128)S(1)} %get-tuple-element.22), channel_id=1, source_target_pairs={{0,10},{1,11},{16,26},{17,27},{32,42},{33,43},{48,58},{49,59},{64,... | collective-permute-start | bytes 196616 | tf_op jit(solution)/shard_map/ppermute | solution.py:301
  20.9 6.5 %collective-permute-start.3 = (f32[2,32,256]{2,1,0:T(8,128)S(1)}, f32[2,32,256]{2,1,0:T(8,128)S(1)}, u32[]{:S(2)}, u32[]{:S(2)}) collective-permute-start(f32[2,32,256]{2,1,0:T(8,128)S(1)} %get-tuple-element.23), channel_id=1, source_target_pairs={{0,8},{1,9},{16,24},{17,25},{32,40},{33,41},{48,56},{49,57},{64,72... | collective-permute-start | bytes 196616 | tf_op jit(solution)/shard_map/ppermute | solution.py:301
  22.2 5.3 %collective-permute-start.2 = (f32[2,32,256]{2,1,0:T(8,128)S(1)}, f32[2,32,256]{2,1,0:T(8,128)S(1)}, u32[]{:S(2)}, u32[]{:S(2)}) collective-permute-start(f32[2,32,256]{2,1,0:T(8,128)S(1)} %get-tuple-element.24), channel_id=1, source_target_pairs={{0,6},{1,7},{16,22},{17,23},{32,38},{33,39},{48,54},{49,55},{64,70... | collective-permute-start | bytes 196616 | tf_op jit(solution)/shard_map/ppermute | solution.py:301
  23.5 4.0 %collective-permute-start.1 = (f32[2,32,256]{2,1,0:T(8,128)S(1)}, f32[2,32,256]{2,1,0:T(8,128)S(1)}, u32[]{:S(2)}, u32[]{:S(2)}) collective-permute-start(f32[2,32,256]{2,1,0:T(8,128)S(1)} %get-tuple-element.25), channel_id=1, source_target_pairs={{0,4},{1,5},{16,20},{17,21},{32,36},{33,37},{48,52},{49,53},{64,68... | collective-permute-start | bytes 196616 | tf_op jit(solution)/shard_map/ppermute | solution.py:301
  24.8 2.7 %collective-permute-start.6 = (f32[2,32,256]{2,1,0:T(8,128)S(1)}, f32[2,32,256]{2,1,0:T(8,128)S(1)}, u32[]{:S(2)}, u32[]{:S(2)}) collective-permute-start(f32[2,32,256]{2,1,0:T(8,128)S(1)} %get-tuple-element.26), channel_id=1, source_target_pairs={{0,14},{1,15},{16,30},{17,31},{32,46},{33,47},{48,62},{49,63},{64,... | collective-permute-start | bytes 196616 | tf_op jit(solution)/shard_map/ppermute | solution.py:301
  26.1 3.0 %collective-permute-start.5 = (f32[2,32,256]{2,1,0:T(8,128)S(1)}, f32[2,32,256]{2,1,0:T(8,128)S(1)}, u32[]{:S(2)}, u32[]{:S(2)}) collective-permute-start(f32[2,32,256]{2,1,0:T(8,128)S(1)} %get-tuple-element.27), channel_id=1, source_target_pairs={{0,12},{1,13},{16,28},{17,29},{32,44},{33,45},{48,60},{49,61},{64,... | collective-permute-start | bytes 196616 | tf_op jit(solution)/shard_map/ppermute | solution.py:301
  29.8 112.2 %all-gather.6.cloned.1.call-start = ((), (), s32[]{:S(2)}) async-start(), calls=%async_computation.2 | async-start | bytes 2621440 | tf_op jit(solution)/shard_map/all_gather | solution.py:327
  30.1 2.1 %collective-permute-start.10 = (f32[64,256]{1,0:T(8,128)S(1)}, f32[64,256]{1,0:T(8,128)S(1)}, u32[]{:S(2)}, u32[]{:S(2)}) collective-permute-start(f32[64,256]{1,0:T(8,128)S(1)} %bitcast.100), channel_id=1, source_target_pairs={{0,384},{16,400},{17,401}} | collective-permute-start | bytes 196616 | tf_op jit(solution)/shard_map/ppermute | solution.py:295
  30.8 1.4 collective-permute-start.9
  31.4 0.7 collective-permute-start.8
  32.2 3.4 %collective-permute-start.17 = (f32[64,256]{1,0:T(8,128)S(1)}, f32[64,256]{1,0:T(8,128)S(1)}, u32[]{:S(2)}, u32[]{:S(2)}) collective-permute-start(f32[64,256]{1,0:T(8,128)S(1)} %fusion.12), channel_id=1, source_target_pairs={{0,16},{16,32},{17,33},{128,144},{144,160},{145,161},{256,272},{27... | collective-permute-start | bytes 196616 | tf_op jit(solution)/shard_map/ppermute | solution.py:316
  32.9 3.4 %collective-permute-start.16 = (f32[64,256]{1,0:T(8,128)S(1)}, f32[64,256]{1,0:T(8,128)S(1)}, u32[]{:S(2)}, u32[]{:S(2)}) collective-permute-start(f32[64,256]{1,0:T(8,128)S(1)} %fusion.12), channel_id=1, source_target_pairs={{0,32},{16,48},{17,49},{128,160},{144,176},{145,177},{256,288},{27... | collective-permute-start | bytes 196616 | tf_op jit(solution)/shard_map/ppermute | solution.py:316
  33.5 4.0 %collective-permute-start.15 = (f32[64,256]{1,0:T(8,128)S(1)}, f32[64,256]{1,0:T(8,128)S(1)}, u32[]{:S(2)}, u32[]{:S(2)}) collective-permute-start(f32[64,256]{1,0:T(8,128)S(1)} %fusion.12), channel_id=1, source_target_pairs={{0,48},{16,64},{17,65},{128,176},{144,192},{145,193},{256,304},{27... | collective-permute-start | bytes 196616 | tf_op jit(solution)/shard_map/ppermute | solution.py:316
  34.2 22.1 %collective-permute-start.14 = (f32[64,256]{1,0:T(8,128)S(1)}, f32[64,256]{1,0:T(8,128)S(1)}, u32[]{:S(2)}, u32[]{:S(2)}) collective-permute-start(f32[64,256]{1,0:T(8,128)S(1)} %fusion.12), channel_id=1, source_target_pairs={{0,64},{16,80},{17,81},{128,192},{144,208},{145,209},{256,320},{27... | collective-permute-start | bytes 196616 | tf_op jit(solution)/shard_map/ppermute | solution.py:316
  34.9 21.4 %collective-permute-start.13 = (f32[64,256]{1,0:T(8,128)S(1)}, f32[64,256]{1,0:T(8,128)S(1)}, u32[]{:S(2)}, u32[]{:S(2)}) collective-permute-start(f32[64,256]{1,0:T(8,128)S(1)} %fusion.12), channel_id=1, source_target_pairs={{0,80},{16,96},{17,97},{128,208},{144,224},{145,225},{256,336},{27... | collective-permute-start | bytes 196616 | tf_op jit(solution)/shard_map/ppermute | solution.py:316
  35.6 20.7 %collective-permute-start.12 = (f32[64,256]{1,0:T(8,128)S(1)}, f32[64,256]{1,0:T(8,128)S(1)}, u32[]{:S(2)}, u32[]{:S(2)}) collective-permute-start(f32[64,256]{1,0:T(8,128)S(1)} %fusion.12), channel_id=1, source_target_pairs={{0,96},{16,112},{17,113},{128,224},{144,240},{145,241},{256,352},{... | collective-permute-start | bytes 196616 | tf_op jit(solution)/shard_map/ppermute | solution.py:316
  36.3 20.1 %collective-permute-start.11 = (f32[64,256]{1,0:T(8,128)S(1)}, f32[64,256]{1,0:T(8,128)S(1)}, u32[]{:S(2)}, u32[]{:S(2)}) collective-permute-start(f32[64,256]{1,0:T(8,128)S(1)} %fusion.12), channel_id=1, source_target_pairs={{0,112},{16,0},{17,1},{128,240},{144,128},{145,129},{256,368},{272... | collective-permute-start | bytes 196616 | tf_op jit(solution)/shard_map/ppermute | solution.py:316
  37.6 20.5 %collective-permute-start.7 = (f32[2,32,256]{2,1,0:T(8,128)}, f32[2,32,256]{2,1,0:T(8,128)S(1)}, u32[]{:S(2)}, u32[]{:S(2)}) collective-permute-start(f32[2,32,256]{2,1,0:T(8,128)} %fusion.8), channel_id=1, source_target_pairs={{0,0},{1,128},{2,16},{3,144},{4,32},{5,160},{6,48},{7,176},{8,64},... | collective-permute-start | bytes 196616 | tf_op jit(solution)/shard_map/ppermute | solution.py:310
  77.6 13.6 %collective-permute-start.24 = (f32[2,64,256]{2,1,0:T(8,128)S(1)}, f32[2,64,256]{2,1,0:T(8,128)S(1)}, u32[]{:S(2)}, u32[]{:S(2)}) collective-permute-start(f32[2,64,256]{2,1,0:T(8,128)S(1)} %pad_maximum_fusion.1), channel_id=1, source_target_pairs={{0,14},{1,15},{16,30},{17,31},{32,46},{33,47},{48,62},{49,63},{64,... | collective-permute-start | bytes 393224 | tf_op jit(solution)/shard_map/ppermute | solution.py:324
  78.9 13.6 %collective-permute-start.23 = (f32[2,64,256]{2,1,0:T(8,128)S(1)}, f32[2,64,256]{2,1,0:T(8,128)S(1)}, u32[]{:S(2)}, u32[]{:S(2)}) collective-permute-start(f32[2,64,256]{2,1,0:T(8,128)S(1)} %pad_maximum_fusion.1), channel_id=1, source_target_pairs={{0,12},{1,13},{16,28},{17,29},{32,44},{33,45},{48,60},{49,61},{64,... | collective-permute-start | bytes 393224 | tf_op jit(solution)/shard_map/ppermute | solution.py:324
  80.2 13.6 %collective-permute-start.22 = (f32[2,64,256]{2,1,0:T(8,128)S(1)}, f32[2,64,256]{2,1,0:T(8,128)S(1)}, u32[]{:S(2)}, u32[]{:S(2)}) collective-permute-start(f32[2,64,256]{2,1,0:T(8,128)S(1)} %pad_maximum_fusion.1), channel_id=1, source_target_pairs={{0,10},{1,11},{16,26},{17,27},{32,42},{33,43},{48,58},{49,59},{64,... | collective-permute-start | bytes 393224 | tf_op jit(solution)/shard_map/ppermute | solution.py:324
  86.6 7.3 %collective-permute-start.21 = (f32[2,64,256]{2,1,0:T(8,128)S(1)}, f32[2,64,256]{2,1,0:T(8,128)S(1)}, u32[]{:S(2)}, u32[]{:S(2)}) collective-permute-start(f32[2,64,256]{2,1,0:T(8,128)S(1)} %pad_maximum_fusion.1), channel_id=1, source_target_pairs={{0,8},{1,9},{16,24},{17,25},{32,40},{33,41},{48,56},{49,57},{64,72... | collective-permute-start | bytes 393224 | tf_op jit(solution)/shard_map/ppermute | solution.py:324
  89.9 5.3 %collective-permute-start.20 = (f32[2,64,256]{2,1,0:T(8,128)S(1)}, f32[2,64,256]{2,1,0:T(8,128)S(1)}, u32[]{:S(2)}, u32[]{:S(2)}) collective-permute-start(f32[2,64,256]{2,1,0:T(8,128)S(1)} %pad_maximum_fusion.1), channel_id=1, source_target_pairs={{0,6},{1,7},{16,22},{17,23},{32,38},{33,39},{48,54},{49,55},{64,70... | collective-permute-start | bytes 393224 | tf_op jit(solution)/shard_map/ppermute | solution.py:324
  91.3 6.8 %collective-permute-start.19 = (f32[2,64,256]{2,1,0:T(8,128)S(1)}, f32[2,64,256]{2,1,0:T(8,128)S(1)}, u32[]{:S(2)}, u32[]{:S(2)}) collective-permute-start(f32[2,64,256]{2,1,0:T(8,128)S(1)} %pad_maximum_fusion.1), channel_id=1, source_target_pairs={{0,4},{1,5},{16,20},{17,21},{32,36},{33,37},{48,52},{49,53},{64,68... | collective-permute-start | bytes 393224 | tf_op jit(solution)/shard_map/ppermute | solution.py:324
  92.6 8.3 %collective-permute-start.18 = (f32[2,64,256]{2,1,0:T(8,128)S(1)}, f32[2,64,256]{2,1,0:T(8,128)S(1)}, u32[]{:S(2)}, u32[]{:S(2)}) collective-permute-start(f32[2,64,256]{2,1,0:T(8,128)S(1)} %pad_maximum_fusion.1), channel_id=1, source_target_pairs={{0,2},{1,3},{16,18},{17,19},{32,34},{33,35},{48,50},{49,51},{64,66... | collective-permute-start | bytes 393224 | tf_op jit(solution)/shard_map/ppermute | solution.py:324
  104.8 15.5 %all-to-all-start.1 = ((f32[4,3,64,256]{3,2,1,0:T(8,128)}), f32[4,3,64,256]{3,2,1,0:T(8,128)S(1)}, u32[]{:S(2)}, u32[]{:S(2)}) async-start(f32[4,3,64,256]{3,2,1,0:T(8,128)} %broadcast_in_dim.33), calls=%async_computation.1 | async-start | bytes 1572864 | tf_op jit(solution)/shard_map/all_to_all | solution.py:280
  120.3 1.2 copy-start.6
  139.1 1.0 copy-start.2
  140.1 1.0 copy-start.4
  141.1 0.9 copy-start.7
  142.0 1.6 copy-start.1
  143.6 1.2 copy-start.3
  144.8 1.2 copy-start.5
  146.0 1.1 copy-start.8
Sparse Core Ops, SparseCore 0:
  29.9 43.0 all-gather.7
  77.7 33.5 all-gather.5

commit v5 on v4

--- a/solution.py
+++ b/solution.py
@@ -12,6 +12,7 @@
 NB = 256
 PART = NB // Z
 BOTH = ("row", "col")
+VMEM_LIMIT = 24 * 2**20
 ROOTS = ((0, 0), (1, 0), (1, 1))
 
 
@@ -120,11 +121,11 @@
     return a0, split(dot6(split(p1 - dot6(a0, l10)), w1))
 
 
-def factor_kernel(tiles_ref, r_hbm, l_hbm, w_hbm, s_hbm, a_ref, l_ref, w_ref, r_ref, s_ref, spread_ref, sems):
+def factor_kernel(tiles_ref, r_hbm, l_ref, w_ref, s_ref, a_ref, r_ref, spread_ref, sem):
     n = a_ref.shape[0]
     nb = n // LANE
     trd = r_ref.shape[2]
-    fetch = pltpu.make_async_copy(r_hbm, r_ref, sems.at[0])
+    fetch = pltpu.make_async_copy(r_hbm, r_ref, sem)
     fetch.start()
     a_ref[:NB, :NB] = tiles_ref[:, 0].reshape(NB, NB)
     a_ref[NB:, :NB] = tiles_ref[:, 1].reshape(NB, NB)
@@ -156,51 +157,38 @@
             s0 = dot6(split(p0), split(w_ref[0]))
             rest = p1 - dot6(split(s0), split(w_ref[1]))
             s_ref[:, :NB] = s0
-    stores = [
-        pltpu.make_async_copy(l_ref, l_hbm, sems.at[1]),
-        pltpu.make_async_copy(w_ref, w_hbm, sems.at[2]),
-        pltpu.make_async_copy(s_ref, s_hbm, sems.at[3]),
-    ]
-    for store in stores[:2]:
-        store.start()
     s_ref[:, NB:] = dot6(split(rest), split(w_ref[2]))
-    stores[2].start()
-    for store in stores:
-        store.wait()
 
 
 def factor(tiles, r):
     n = 2 * NB
     trd = r.shape[1]
-    hbm = pl.BlockSpec(memory_space=pltpu.HBM)
-    r = r.reshape(Z, CORE, trd, PART, NB)
+    vmem = pl.BlockSpec(memory_space=pltpu.VMEM)
+    r = pltpu.with_memory_space_constraint(r.reshape(Z, CORE, trd, PART, NB), pltpu.HBM)
     shapes = [(n, n), (3, NB, NB), (trd * NB, n)]
     return pl.pallas_call(
         factor_kernel,
         out_shape=[jax.ShapeDtypeStruct(shape, jnp.float32) for shape in shapes],
-        in_specs=[pl.BlockSpec(memory_space=pltpu.VMEM), hbm],
-        out_specs=[hbm] * 3,
+        in_specs=[vmem, pl.BlockSpec(memory_space=pltpu.HBM)],
+        out_specs=[vmem] * 3,
         scratch_shapes=[
             pltpu.VMEM((n, n), jnp.float32),
-            pltpu.VMEM(shapes[0], jnp.float32),
-            pltpu.VMEM(shapes[1], jnp.float32),
             pltpu.VMEM(r.shape, jnp.float32),
-            pltpu.VMEM(shapes[2], jnp.float32),
             pltpu.VMEM((2 * SUB * (SUB + 2), LANE), jnp.float32),
-            pltpu.SemaphoreType.DMA((4,)),
+            pltpu.SemaphoreType.DMA,
         ],
-        compiler_params=pltpu.CompilerParams(vmem_limit_bytes=20 * 2**20),
+        compiler_params=pltpu.CompilerParams(vmem_limit_bytes=VMEM_LIMIT),
         name="factor",
     )(tiles, r)
 
 
 def update_kernel(
-    place_ref, cov_hbm, g_hbm, w_hbm, l_hbm, left_hbm, out_ref, cov_ref, g_ref, w_ref, l_ref, left_ref, s_ref, sems
+    place_ref, cov_ref, g_hbm, w_hbm, l_hbm, left_hbm, out_ref, g_ref, w_ref, l_ref, left_ref, s_ref, sems
 ):
     trd, nb, tcd, _ = cov_ref.shape
     fetches = [pltpu.make_async_copy(w_hbm, w_ref, sems.at[0])]
     fetches += [pltpu.make_async_copy(g_hbm.at[:, :, a], g_ref.at[a], sems.at[1 + a]) for a in range(2)]
-    fetches += [pltpu.make_async_copy(left_hbm, left_ref, sems.at[3]), pltpu.make_async_copy(cov_hbm, cov_ref, sems.at[4])]
+    fetches.append(pltpu.make_async_copy(left_hbm, left_ref, sems.at[3]))
     for fetch in fetches:
         fetch.start()
     fetches[0].wait()
@@ -216,7 +204,6 @@
                     s_ref[j, 2 * a + h, :, k * NB : (k + 1) * NB] = part[h * NB : (h + 1) * NB]
     fetches[3].wait()
     left = split(left_ref[...])
-    fetches[4].wait()
     for b in range(tcd):
         u = dot6(left, [s_ref[j, b] for j in range(3)])
         for a in range(trd):
@@ -239,7 +226,7 @@
             @pl.when(jnp.logical_and(row == i, col == j))
             def _():
                 fetch = pltpu.make_async_copy(
-                    l_hbm.at[i * NB : (i + 1) * NB, j * NB : (j + 1) * NB], l_ref, sems.at[5]
+                    l_hbm.at[i * NB : (i + 1) * NB, j * NB : (j + 1) * NB], l_ref, sems.at[4]
                 )
                 fetch.start()
                 fetch.wait()
@@ -253,31 +240,32 @@
                         )
 
 
-def update(place, cov, g, w, lower, left):
+def update(place, cov, *rest):
     trd, nb, tcd, _ = cov.shape
-    hbm = pl.BlockSpec(memory_space=pltpu.HBM)
+    vmem, hbm = (pl.BlockSpec(memory_space=space) for space in (pltpu.VMEM, pltpu.HBM))
+    rest = [pltpu.with_memory_space_constraint(array, pltpu.HBM) for array in rest]
+    g, w, _, left = rest
     return pl.pallas_call(
         update_kernel,
         out_shape=jax.ShapeDtypeStruct(cov.shape, jnp.float32),
-        in_specs=[pl.BlockSpec(memory_space=pltpu.SMEM)] + [hbm] * 5,
-        out_specs=pl.BlockSpec(memory_space=pltpu.VMEM),
+        in_specs=[pl.BlockSpec(memory_space=pltpu.SMEM), vmem] + [hbm] * len(rest),
+        out_specs=vmem,
         scratch_shapes=[
-            pltpu.VMEM(cov.shape, jnp.float32),
             pltpu.VMEM((2, X, Y, PART, NB), jnp.float32),
             pltpu.VMEM(w.shape, jnp.float32),
             pltpu.VMEM((NB, NB), jnp.float32),
             pltpu.VMEM(left.shape, jnp.float32),
             pltpu.VMEM((3, tcd, nb, 2 * nb), jnp.bfloat16),
-            pltpu.SemaphoreType.DMA((6,)),
+            pltpu.SemaphoreType.DMA((5,)),
         ],
-        compiler_params=pltpu.CompilerParams(vmem_limit_bytes=24 * 2**20),
+        compiler_params=pltpu.CompilerParams(vmem_limit_bytes=VMEM_LIMIT),
         name="update",
-    )(place, cov, g, w, lower, left)
-
-
-def shared(block, groups):
+    )(place, cov, *rest)
+
+
+def shared(block, axis, groups):
     many = jnp.broadcast_to(block[None], (len(groups[0]),) + block.shape)
-    return lax.all_to_all(many, "row", 0, 0, axis_index_groups=groups)
+    return lax.all_to_all(many, axis, 0, 0, axis_index_groups=groups)
 
 
 def on_device(cov):
@@ -285,20 +273,14 @@
     x, y, z = row // Y, row % Y, col // CORE
     along_x = [[i * Y + j for i in range(X)] for j in range(Y)]
     along_y = [[i * Y + j for j in range(Y)] for i in range(X)]
+    along_z = [[c * CORE + k for c in range(Z)] for k in range(CORE)]
     chips = [[c * CORE + k for k in range(CORE)] for c in range(Z)]
-    panel = cov[:, :, 0, :]
-
-    tile = panel[0].reshape(X, NB // X, NB)
-    head = jnp.where(x == 0, tile[0], 0.0)
-    for s in range(1, X):
-        pairs = [(device(0, j, 0, k), device(s, j, 0, k)) for j, k in ROOTS]
-        head = head + lax.ppermute(tile[s], BOTH, pairs)
-
-    parts = panel.reshape(2, Z, PART, NB)
-    mine = jnp.where(z == 0, parts[:, 0], 0.0)
+    panel = cov[:, :, 0, :].reshape(2, Z, PART, NB)
+
+    mine = jnp.where(z == 0, panel[:, 0], 0.0)
     for s in range(1, Z):
         pairs = [(p * N_COL + k, p * N_COL + s * CORE + k) for p in range(N_ROW) for k in range(CORE)]
-        mine = mine + lax.ppermute(parts[:, s], BOTH, pairs)
+        mine = mine + lax.ppermute(panel[:, s], BOTH, pairs)
     r = lax.all_gather(mine, "col")
 
     pairs = [
@@ -308,26 +290,26 @@
         for k in range(CORE)
     ]
     moved = lax.ppermute(mine, BOTH, pairs)
-
+    got = shared(moved, "row", along_y)
+
+    head = jnp.where(x == 0, mine[0], 0.0)
+    for s in range(1, X):
+        pairs = [(device(0, j, c, k), device(s, j, c, k)) for c in range(Z) for j, k in ROOTS]
+        head = head + lax.ppermute(mine[0], BOTH, pairs)
     first = jnp.where(y == 0, head, 0.0)
     second = jnp.where(y == 1, head, 0.0)
     for s in range(1, Y):
-        pairs = [(device(i, j, 0, k), device(i, (j + s) % Y, 0, k)) for i in range(X) for j, k in ROOTS]
+        pairs = [
+            (device(i, j, c, k), device(i, (j + s) % Y, c, k)) for i in range(X) for c in range(Z) for j, k in ROOTS
+        ]
         came = lax.ppermute(head, BOTH, pairs)
         first = jnp.where(y == s, came, first)
         second = jnp.where(y == (s + 1) % Y, came, second)
-    here = jnp.stack([first, second])
-    moved, here = lax.optimization_barrier((moved, here))
-    head = jnp.where(z == 0, here, 0.0)
-    for s in range(1, Z):
-        pairs = [(device(i, j, 0, k), device(i, j, s, k)) for i in range(X) for j in range(Y) for k in range(CORE)]
-        head = head + lax.ppermute(here, BOTH, pairs)
-
-    got = shared(moved, along_y)
+
+    head = lax.all_gather(jnp.stack([first, second]), "col", axis_index_groups=chips)
+    tiles = shared(jnp.stack([head[0, 0], head[0, 1], head[1, 1]]), "col", along_z)
+    got, tiles = lax.optimization_barrier((got, tiles))
     g = lax.all_gather(got, "row", axis_index_groups=along_x)
-
-    head = lax.all_gather(head, "col", axis_index_groups=chips)
-    tiles = shared(jnp.stack([head[0, 0], head[0, 1], head[1, 1]]), along_x)
     lower, w, left = factor(tiles, r)
     return update(jnp.stack([row, col]).astype(jnp.int32), cov, g, w, lower, left)
 

time: 167 us -> 165 us (0.988)
  starting transfers between devices: 64.3 us -> 41.4 us
  blocking collectives: 22.3 us -> 37.6 us
  waiting for transfers between devices: 22.3 us -> 34.3 us
  local copies, waits for them, and re-layouts: 12.6 us -> 5.81 us
    ppermute x17 -> x10, starting transfers between devices: 36.8 us -> 20.6 us  [the longest x7 18.6 us: on_device(): mine = mine + lax.ppermute(panel[:, s], BOTH, pairs)]
    all_gather x1, waiting for transfers between devices: 0.01 us -> 15.5 us  [on_device(): g = lax.all_gather(got, 'row', axis_index_groups=along_x)]
    ppermute x1, starting transfers between devices: 18.7 us -> 4.13 us  [on_device(): moved = lax.ppermute(mine, BOTH, pairs)]
    all_to_all x1, waiting for transfers between devices: 11.9 us -> 0.01 us  [shared(): return lax.all_to_all(many, axis, 0, 0, axis_index_groups=groups)]
    all_to_all x1, blocking collectives: 19.5 us -> 30.1 us  [shared(): return lax.all_to_all(many, axis, 0, 0, axis_index_groups=groups)]
    ppermute x7, waiting for transfers between devices: 0.02 us -> 10.3 us  [on_device(): came = lax.ppermute(head, BOTH, pairs)]
    all_to_all x1, starting transfers between devices: 3.49 us -> 11.3 us  [shared(): return lax.all_to_all(many, axis, 0, 0, axis_index_groups=groups)]
    ppermute x17 -> x10, waiting for transfers between devices: 8.62 us -> 1.68 us  [the longest x7 1.67 us: on_device(): mine = mine + lax.ppermute(panel[:, s], BOTH, pairs)]
  transfers between devices with their start and end apart: 28 -> 21, of which waited for: 6 -> 5; matrix products, arithmetic and copies ran while one was open for 1% -> 1% of each run, Pallas kernels for 11% -> 11%
where the time goes in v5:
time: 165 us
  starting transfers between devices  41.4 us (25%)
  blocking collectives  37.6 us (23%)
  waiting for transfers between devices  34.3 us (21%)
  Pallas kernels  31.5 us (19%)
  between operations  13.9 us (8%)
  local copies, waits for them, and re-layouts  5.81 us (4%)
    all_to_all x1, blocking collectives, shared(): return lax.all_to_all(many, axis, 0, 0, axis_index_groups=groups)  30.1 us
    ppermute x7, starting transfers between devices, on_device(): mine = mine + lax.ppermute(panel[:, s], BOTH, pairs)  18.6 us
    pallas_call x1, Pallas kernels, factor(): pl.pallas_call(factor_kernel, out_shape=[jax.ShapeDtypeStruct(shape, jnp....  18.5 us
    all_gather x1, waiting for transfers between devices, on_device(): g = lax.all_gather(got, 'row', axis_index_groups=along_x)  15.5 us
    pallas_call x1, Pallas kernels, update(): pl.pallas_call(update_kernel, out_shape=jax.ShapeDtypeStruct(cov.shape, j...  13 us
    all_to_all x1, starting transfers between devices, shared(): return lax.all_to_all(many, axis, 0, 0, axis_index_groups=groups)  11.3 us
    ppermute x7, waiting for transfers between devices, on_device(): came = lax.ppermute(head, BOTH, pairs)  10.3 us
    all_gather x1, blocking collectives, on_device(): lax.all_gather(jnp.stack([first, second]), 'col', axis_index_groups=chips)  7.49 us
  transfers between devices with their start and end apart: 21, of which 5 were waited for; matrix products, arithmetic and copies ran while one was open for 1% of the time, Pallas kernels for 11%

profile of v5, /device:TPU:1, one launch (start us, length us, event | category | flops | bytes accessed | tf_op | source)
XLA Modules:
  0.0 164.6 jit_solution(14310206608793526652)
XLA Ops:
  6.5 2.0 %slice.42 = f32[2,256,1,256]{3,2,1,0:T(1,128)S(1)} slice(f32[2,256,4,256]{3,2,1,0:T(4,128)} %cov_ref.1), slice={[0:2], [0:256], [0:1], [0:256]} | slice | bytes 1048576 | tf_op jit(solution)/shard_map/slice | solution.py:278
  8.6 4.8 %collective-permute-start = (f32[2,32,256]{2,1,0:T(8,128)S(1)}, f32[2,32,256]{2,1,0:T(8,128)S(1)}, u32[]{:S(2)}, u32[]{:S(2)}) collective-permute-start(f32[2,32,256]{2,1,0:T(8,128)S(1)} %get-tuple-element.15), channel_id=1, source_target_pairs={{0,2},{1,3},{16,18},{17,19},{32,34},{33,35},{48,50},{49,51},{64,66... | collective-permute-start | bytes 196616 | tf_op jit(solution)/shard_map/ppermute | solution.py:283
  13.4 7.3 %collective-permute-start.4 = (f32[2,32,256]{2,1,0:T(8,128)S(1)}, f32[2,32,256]{2,1,0:T(8,128)S(1)}, u32[]{:S(2)}, u32[]{:S(2)}) collective-permute-start(f32[2,32,256]{2,1,0:T(8,128)S(1)} %get-tuple-element.16), channel_id=1, source_target_pairs={{0,10},{1,11},{16,26},{17,27},{32,42},{33,43},{48,58},{49,59},{64,... | collective-permute-start | bytes 196616 | tf_op jit(solution)/shard_map/ppermute | solution.py:283
  20.7 1.3 collective-permute-start.3
  22.0 1.3 collective-permute-start.2
  23.3 1.3 collective-permute-start.1
  24.6 0.0 collective-permute-done
  24.6 1.3 collective-permute-start.6
  25.9 0.0 collective-permute-done.4
  26.0 1.3 collective-permute-start.5
  27.3 0.0 collective-permute-done.3
  27.3 0.0 collective-permute-done.2
  27.3 0.0 collective-permute-done.1
  27.3 0.0 collective-permute-done.6
  27.3 1.7 %collective-permute-done.5 = f32[2,32,256]{2,1,0:T(8,128)S(1)} collective-permute-done((f32[2,32,256]{2,1,0:T(8,128)S(1)}, f32[2,32,256]{2,1,0:T(8,128)S(1)}, u32[]{:S(2)}, u32[]{:S(2)}) %collective-permute-start.5) | collective-permute-done | bytes 65568 | tf_op jit(solution)/shard_map/ppermute | solution.py:283
  29.0 0.0 copy-start.5
  29.0 4.1 %collective-permute-start.7 = (f32[2,32,256]{2,1,0:T(8,128)S(1)}, f32[2,32,256]{2,1,0:T(8,128)S(1)}, u32[]{:S(2)}, u32[]{:S(2)}) collective-permute-start(f32[2,32,256]{2,1,0:T(8,128)S(1)} %fusion.8), channel_id=1, source_target_pairs={{0,0},{1,128},{2,16},{3,144},{4,32},{5,160},{6,48},{7,176},{8,64},... | collective-permute-start | bytes 196616 | tf_op jit(solution)/shard_map/ppermute | solution.py:292
  33.2 0.7 collective-permute-start.9
  33.8 0.7 collective-permute-start.8
  34.5 0.7 collective-permute-start.10
  35.2 3.2 %collective-permute-done.7 = f32[2,32,256]{2,1,0:T(8,128)S(1)} collective-permute-done((f32[2,32,256]{2,1,0:T(8,128)S(1)}, f32[2,32,256]{2,1,0:T(8,128)S(1)}, u32[]{:S(2)}, u32[]{:S(2)}) %collective-permute-start.7) | collective-permute-done | bytes 65568 | tf_op jit(solution)/shard_map/ppermute | solution.py:292
  38.4 0.8 broadcast_in_dim.23
  39.2 11.3 %all-to-all-start = ((f32[8,2,32,256]{3,2,1,0:T(8,128)}), f32[8,2,32,256]{3,2,1,0:T(8,128)S(1)}, u32[]{:S(2)}, u32[]{:S(2)}) async-start(f32[8,2,32,256]{3,2,1,0:T(8,128)} %broadcast_in_dim.23), calls=%async_computation | async-start | bytes 1048576 | tf_op jit(solution)/shard_map/all_to_all | solution.py:268
  50.5 0.0 all-gather.8.cloned.1.call-start
  50.6 0.0 collective-permute-done.9
  50.6 0.0 collective-permute-done.8
  50.6 0.0 collective-permute-done.10
  50.6 0.7 collective-permute-start.17
  51.3 0.7 collective-permute-start.16
  52.0 0.7 collective-permute-start.15
  52.6 0.7 collective-permute-start.14
  53.3 0.7 collective-permute-start.13
  54.0 0.0 collective-permute-done.17
  54.0 0.7 collective-permute-start.12
  54.7 0.0 collective-permute-done.16
  54.7 1.3 collective-permute-start.11
  56.0 0.0 copy-done.5
  56.0 0.0 all-gather.8.cloned.1.call-update
  56.0 0.0 all-gather.6.cloned.1.call-start
  56.1 0.0 collective-permute-done.15
  56.1 0.0 collective-permute-done.14
  56.1 0.0 collective-permute-done.13
  56.1 0.0 collective-permute-done.12
  56.1 10.3 %collective-permute-done.11 = f32[32,256]{1,0:T(8,128)S(1)} collective-permute-done((f32[32,256]{1,0:T(8,128)S(1)}, f32[32,256]{1,0:T(8,128)S(1)}, u32[]{:S(2)}, u32[]{:S(2)}) %collective-permute-start.11) | collective-permute-done | bytes 32800 | tf_op jit(solution)/shard_map/ppermute | solution.py:305
  66.5 7.5 %all-gather = f32[4,32,256]{2,1,0:T(8,128)S(1)} all-gather(f32[2,32,256]{2,1,0:T(8,128)S(1)} %pad_maximum_fusion.1), channel_id=2, replica_groups={{0,1},{2,3},{4,5},{6,7},{8,9},{10,11},{12,13},{14,15},{16,17},{18,19},{..., dimensions={0}, use_global_device_ids=true | all-gather | bytes 196608 | tf_op jit(solution)/shard_map/all_gather | solution.py:309
  74.0 0.0 all-to-all-done
  74.0 0.0 copy-start.4
  74.0 0.1 broadcast_in_dim.25
  74.1 0.0 copy-start
  74.1 30.1 %all_to_all.10.tiles_ref = f32[8,3,32,256]{3,2,1,0:T(8,128)S(1)} all-to-all(f32[8,3,32,256]{3,2,1,0:T(8,128)S(1)} %broadcast_in_dim.25), channel_id=1, replica_groups={{0,2,4,6,8,10,12,14},{1,3,5,7,9,11,13,15},{16,18,20,22,24,26,28,30},{17..., dimensions={0} | all-to-all | bytes 1572864 | tf_op jit(solution)/shard_map/all_to_all | solution.py:268
  104.2 0.0 copy-done.4
  104.2 0.0 all-gather.6.cloned.1.call-update
  104.3 0.1 pad_add_fusion.place_ref
  104.3 3.5 %all-gather.8.cloned.1.call-done = f32[32,32,256]{2,1,0:T(8,128)} async-done(((f32[2,32,256]{2,1,0:T(8,128)}), f32[32,32,256]{2,1,0:T(8,128)}) %all-gather.8.cloned.1.call-update) | async-done | bytes 1048592 | tf_op jit(solution)/shard_map/all_gather | solution.py:284
  107.9 18.5 %factor.1 = (f32[512,512]{1,0:T(8,128)S(1)}, f32[3,256,256]{2,1,0:T(8,128)S(1)}, f32[512,512]{1,0:T(8,128)S(1)}) custom-call(f32[8,3,32,256]{3,2,1,0:T(8,128)S(1)} %all_to_all.10.tiles_ref, f32[8,2,2,32,256]{4,3,2,1,0:T(8,128)} %bitcast.85), custom_call_target="tpu_custom_call" | custom-call | tf_op jit(solution)/shard_map/factor/pallas_call | solution.py:169
  126.4 0.0 copy-start.1
  126.4 1.0 copy-done.1
  127.4 0.0 copy-start.2
  127.4 1.0 copy-done.2
  128.4 0.0 copy-start.3
  128.4 0.9 copy-done.3
  129.2 15.5 %all-gather.6.cloned.1.call-done = f32[32,2,32,256]{3,2,1,0:T(8,128)} async-done(((f32[8,2,32,256]{3,2,1,0:T(8,128)}), f32[32,2,32,256]{3,2,1,0:T(8,128)}) %all-gather.6.cloned.1.call-update) | async-done | bytes 2097168 | tf_op jit(solution)/shard_map/all_gather | solution.py:312
  144.8 0.0 copy-done
  144.8 13.0 %update.1 = f32[2,256,4,256]{3,2,1,0:T(4,128)} custom-call(s32[2]{0:T(128)S(1)} %pad_add_fusion.place_ref, f32[2,256,4,256]{3,2,1,0:T(4,128)S(1)} %copy-done, f32[4,8,2,32,256]{4,3,2,1,0:T(8,128)} %bitcast.84, f32[3,256,256]{2,1,0:T(8,128)} %copy-done.3, f32[512,512]{1,0:T(8,128)} %copy-done.1, f32[512,512]{1,0:T(8,128)} %copy-done.2), custom_call_target="tpu_custom_call" | custom-call | tf_op jit(solution)/shard_map/update/pallas_call | solution.py:248
  (9 shorter events, 0.2 us)
Async XLA Ops:
  8.6 16.1 %collective-permute-start = (f32[2,32,256]{2,1,0:T(8,128)S(1)}, f32[2,32,256]{2,1,0:T(8,128)S(1)}, u32[]{:S(2)}, u32[]{:S(2)}) collective-permute-start(f32[2,32,256]{2,1,0:T(8,128)S(1)} %get-tuple-element.15), channel_id=1, source_target_pairs={{0,2},{1,3},{16,18},{17,19},{32,34},{33,35},{48,50},{49,51},{64,66... | collective-permute-start | bytes 196616 | tf_op jit(solution)/shard_map/ppermute | solution.py:283
  13.4 12.5 %collective-permute-start.4 = (f32[2,32,256]{2,1,0:T(8,128)S(1)}, f32[2,32,256]{2,1,0:T(8,128)S(1)}, u32[]{:S(2)}, u32[]{:S(2)}) collective-permute-start(f32[2,32,256]{2,1,0:T(8,128)S(1)} %get-tuple-element.16), channel_id=1, source_target_pairs={{0,10},{1,11},{16,26},{17,27},{32,42},{33,43},{48,58},{49,59},{64,... | collective-permute-start | bytes 196616 | tf_op jit(solution)/shard_map/ppermute | solution.py:283
  20.7 6.5 %collective-permute-start.3 = (f32[2,32,256]{2,1,0:T(8,128)S(1)}, f32[2,32,256]{2,1,0:T(8,128)S(1)}, u32[]{:S(2)}, u32[]{:S(2)}) collective-permute-start(f32[2,32,256]{2,1,0:T(8,128)S(1)} %get-tuple-element.17), channel_id=1, source_target_pairs={{0,8},{1,9},{16,24},{17,25},{32,40},{33,41},{48,56},{49,57},{64,72... | collective-permute-start | bytes 196616 | tf_op jit(solution)/shard_map/ppermute | solution.py:283
  22.0 5.3 %collective-permute-start.2 = (f32[2,32,256]{2,1,0:T(8,128)S(1)}, f32[2,32,256]{2,1,0:T(8,128)S(1)}, u32[]{:S(2)}, u32[]{:S(2)}) collective-permute-start(f32[2,32,256]{2,1,0:T(8,128)S(1)} %get-tuple-element.18), channel_id=1, source_target_pairs={{0,6},{1,7},{16,22},{17,23},{32,38},{33,39},{48,54},{49,55},{64,70... | collective-permute-start | bytes 196616 | tf_op jit(solution)/shard_map/ppermute | solution.py:283
  23.3 4.0 %collective-permute-start.1 = (f32[2,32,256]{2,1,0:T(8,128)S(1)}, f32[2,32,256]{2,1,0:T(8,128)S(1)}, u32[]{:S(2)}, u32[]{:S(2)}) collective-permute-start(f32[2,32,256]{2,1,0:T(8,128)S(1)} %get-tuple-element.19), channel_id=1, source_target_pairs={{0,4},{1,5},{16,20},{17,21},{32,36},{33,37},{48,52},{49,53},{64,68... | collective-permute-start | bytes 196616 | tf_op jit(solution)/shard_map/ppermute | solution.py:283
  24.6 2.7 %collective-permute-start.6 = (f32[2,32,256]{2,1,0:T(8,128)S(1)}, f32[2,32,256]{2,1,0:T(8,128)S(1)}, u32[]{:S(2)}, u32[]{:S(2)}) collective-permute-start(f32[2,32,256]{2,1,0:T(8,128)S(1)} %get-tuple-element.20), channel_id=1, source_target_pairs={{0,14},{1,15},{16,30},{17,31},{32,46},{33,47},{48,62},{49,63},{64,... | collective-permute-start | bytes 196616 | tf_op jit(solution)/shard_map/ppermute | solution.py:283
  26.0 3.0 %collective-permute-start.5 = (f32[2,32,256]{2,1,0:T(8,128)S(1)}, f32[2,32,256]{2,1,0:T(8,128)S(1)}, u32[]{:S(2)}, u32[]{:S(2)}) collective-permute-start(f32[2,32,256]{2,1,0:T(8,128)S(1)} %get-tuple-element.21), channel_id=1, source_target_pairs={{0,12},{1,13},{16,28},{17,29},{32,44},{33,45},{48,60},{49,61},{64,... | collective-permute-start | bytes 196616 | tf_op jit(solution)/shard_map/ppermute | solution.py:283
  29.0 27.0 %copy-start.5 = (f32[2,32,256]{2,1,0:T(8,128)}, f32[2,32,256]{2,1,0:T(8,128)S(1)}, u32[]{:S(2)}) copy-start(f32[2,32,256]{2,1,0:T(8,128)S(1)} %fusion.8) | copy-start | bytes 196612
  29.0 9.4 %collective-permute-start.7 = (f32[2,32,256]{2,1,0:T(8,128)S(1)}, f32[2,32,256]{2,1,0:T(8,128)S(1)}, u32[]{:S(2)}, u32[]{:S(2)}) collective-permute-start(f32[2,32,256]{2,1,0:T(8,128)S(1)} %fusion.8), channel_id=1, source_target_pairs={{0,0},{1,128},{2,16},{3,144},{4,32},{5,160},{6,48},{7,176},{8,64},... | collective-permute-start | bytes 196616 | tf_op jit(solution)/shard_map/ppermute | solution.py:292
  33.2 17.4 %collective-permute-start.9 = (f32[32,256]{1,0:T(8,128)S(1)}, f32[32,256]{1,0:T(8,128)S(1)}, u32[]{:S(2)}, u32[]{:S(2)}) collective-permute-start(f32[32,256]{1,0:T(8,128)S(1)} %slice_bitcast_fusion.11), channel_id=1, source_target_pairs={{0,256},{16,272},{17,273},{2,258},{18,274},{19,275},{4,260},{20,27... | collective-permute-start | bytes 98312 | tf_op jit(solution)/shard_map/ppermute | solution.py:298
  33.8 16.7 %collective-permute-start.8 = (f32[32,256]{1,0:T(8,128)S(1)}, f32[32,256]{1,0:T(8,128)S(1)}, u32[]{:S(2)}, u32[]{:S(2)}) collective-permute-start(f32[32,256]{1,0:T(8,128)S(1)} %slice_bitcast_fusion.11), channel_id=1, source_target_pairs={{0,128},{16,144},{17,145},{2,130},{18,146},{19,147},{4,132},{20,14... | collective-permute-start | bytes 98312 | tf_op jit(solution)/shard_map/ppermute | solution.py:298
  34.5 16.1 %collective-permute-start.10 = (f32[32,256]{1,0:T(8,128)S(1)}, f32[32,256]{1,0:T(8,128)S(1)}, u32[]{:S(2)}, u32[]{:S(2)}) collective-permute-start(f32[32,256]{1,0:T(8,128)S(1)} %slice_bitcast_fusion.11), channel_id=1, source_target_pairs={{0,384},{16,400},{17,401},{2,386},{18,402},{19,403},{4,388},{20,40... | collective-permute-start | bytes 98312 | tf_op jit(solution)/shard_map/ppermute | solution.py:298
  39.2 34.7 %all-to-all-start = ((f32[8,2,32,256]{3,2,1,0:T(8,128)}), f32[8,2,32,256]{3,2,1,0:T(8,128)S(1)}, u32[]{:S(2)}, u32[]{:S(2)}) async-start(f32[8,2,32,256]{3,2,1,0:T(8,128)} %broadcast_in_dim.23), calls=%async_computation | async-start | bytes 1048576 | tf_op jit(solution)/shard_map/all_to_all | solution.py:268
  50.5 57.3 %all-gather.8.cloned.1.call-start = ((), (), s32[]{:S(2)}) async-start(), calls=%async_computation.3 | async-start | bytes 1114112 | tf_op jit(solution)/shard_map/all_gather | solution.py:284
  50.6 3.4 %collective-permute-start.17 = (f32[32,256]{1,0:T(8,128)S(1)}, f32[32,256]{1,0:T(8,128)S(1)}, u32[]{:S(2)}, u32[]{:S(2)}) collective-permute-start(f32[32,256]{1,0:T(8,128)S(1)} %add_add_fusion), channel_id=1, source_target_pairs={{0,16},{16,32},{17,33},{2,18},{18,34},{19,35},{4,20},{20,36},{21,3... | collective-permute-start | bytes 98312 | tf_op jit(solution)/shard_map/ppermute | solution.py:305
  51.3 3.4 %collective-permute-start.16 = (f32[32,256]{1,0:T(8,128)S(1)}, f32[32,256]{1,0:T(8,128)S(1)}, u32[]{:S(2)}, u32[]{:S(2)}) collective-permute-start(f32[32,256]{1,0:T(8,128)S(1)} %add_add_fusion), channel_id=1, source_target_pairs={{0,32},{16,48},{17,49},{2,34},{18,50},{19,51},{4,36},{20,52},{21,5... | collective-permute-start | bytes 98312 | tf_op jit(solution)/shard_map/ppermute | solution.py:305
  52.0 4.1 %collective-permute-start.15 = (f32[32,256]{1,0:T(8,128)S(1)}, f32[32,256]{1,0:T(8,128)S(1)}, u32[]{:S(2)}, u32[]{:S(2)}) collective-permute-start(f32[32,256]{1,0:T(8,128)S(1)} %add_add_fusion), channel_id=1, source_target_pairs={{0,48},{16,64},{17,65},{2,50},{18,66},{19,67},{4,52},{20,68},{21,6... | collective-permute-start | bytes 98312 | tf_op jit(solution)/shard_map/ppermute | solution.py:305
  52.6 3.5 %collective-permute-start.14 = (f32[32,256]{1,0:T(8,128)S(1)}, f32[32,256]{1,0:T(8,128)S(1)}, u32[]{:S(2)}, u32[]{:S(2)}) collective-permute-start(f32[32,256]{1,0:T(8,128)S(1)} %add_add_fusion), channel_id=1, source_target_pairs={{0,64},{16,80},{17,81},{2,66},{18,82},{19,83},{4,68},{20,84},{21,8... | collective-permute-start | bytes 98312 | tf_op jit(solution)/shard_map/ppermute | solution.py:305
  53.3 2.8 %collective-permute-start.13 = (f32[32,256]{1,0:T(8,128)S(1)}, f32[32,256]{1,0:T(8,128)S(1)}, u32[]{:S(2)}, u32[]{:S(2)}) collective-permute-start(f32[32,256]{1,0:T(8,128)S(1)} %add_add_fusion), channel_id=1, source_target_pairs={{0,80},{16,96},{17,97},{2,82},{18,98},{19,99},{4,84},{20,100},{21,... | collective-permute-start | bytes 98312 | tf_op jit(solution)/shard_map/ppermute | solution.py:305
  54.0 2.1 %collective-permute-start.12 = (f32[32,256]{1,0:T(8,128)S(1)}, f32[32,256]{1,0:T(8,128)S(1)}, u32[]{:S(2)}, u32[]{:S(2)}) collective-permute-start(f32[32,256]{1,0:T(8,128)S(1)} %add_add_fusion), channel_id=1, source_target_pairs={{0,96},{16,112},{17,113},{2,98},{18,114},{19,115},{4,100},{20,116}... | collective-permute-start | bytes 98312 | tf_op jit(solution)/shard_map/ppermute | solution.py:305
  54.7 11.8 %collective-permute-start.11 = (f32[32,256]{1,0:T(8,128)S(1)}, f32[32,256]{1,0:T(8,128)S(1)}, u32[]{:S(2)}, u32[]{:S(2)}) collective-permute-start(f32[32,256]{1,0:T(8,128)S(1)} %add_add_fusion), channel_id=1, source_target_pairs={{0,112},{16,0},{17,1},{2,114},{18,2},{19,3},{4,116},{20,4},{21,5},... | collective-permute-start | bytes 98312 | tf_op jit(solution)/shard_map/ppermute | solution.py:305
  56.0 88.7 %all-gather.6.cloned.1.call-start = ((), (), s32[]{:S(2)}) async-start(), calls=%async_computation.2 | async-start | bytes 2621440 | tf_op jit(solution)/shard_map/all_gather | solution.py:312
  74.0 30.2 %copy-start.4 = (f32[8,2,32,256]{3,2,1,0:T(8,128)}, f32[8,2,32,256]{3,2,1,0:T(8,128)S(1)}, u32[]{:S(2)}) copy-start(f32[8,2,32,256]{3,2,1,0:T(8,128)S(1)} %all-to-all-done) | copy-start | bytes 1572868
  74.1 70.7 %copy-start = (f32[2,256,4,256]{3,2,1,0:T(4,128)S(1)}, f32[2,256,4,256]{3,2,1,0:T(4,128)}, u32[]{:S(2)}) copy-start(f32[2,256,4,256]{3,2,1,0:T(4,128)} %cov_ref.1) | copy-start | bytes 6291460
  126.4 1.0 copy-start.1
  127.4 1.0 copy-start.2
  128.4 0.9 copy-start.3
Sparse Core Ops, SparseCore 0:
  56.1 51.6 all-gather.7
  110.0 34.7 all-gather.5

commit v6 on v5

--- a/solution.py
+++ b/solution.py
@@ -270,7 +270,7 @@
 
 def on_device(cov):
     row, col = lax.axis_index("row"), lax.axis_index("col")
-    x, y, z = row // Y, row % Y, col // CORE
+    x, z = row // Y, col // CORE
     along_x = [[i * Y + j for i in range(X)] for j in range(Y)]
     along_y = [[i * Y + j for j in range(Y)] for i in range(X)]
     along_z = [[c * CORE + k for c in range(Z)] for k in range(CORE)]
@@ -290,26 +290,16 @@
         for k in range(CORE)
     ]
     moved = lax.ppermute(mine, BOTH, pairs)
-    got = shared(moved, "row", along_y)
 
     head = jnp.where(x == 0, mine[0], 0.0)
     for s in range(1, X):
         pairs = [(device(0, j, c, k), device(s, j, c, k)) for c in range(Z) for j, k in ROOTS]
         head = head + lax.ppermute(mine[0], BOTH, pairs)
-    first = jnp.where(y == 0, head, 0.0)
-    second = jnp.where(y == 1, head, 0.0)
-    for s in range(1, Y):
-        pairs = [
-            (device(i, j, c, k), device(i, (j + s) % Y, c, k)) for i in range(X) for c in range(Z) for j, k in ROOTS
-        ]
-        came = lax.ppermute(head, BOTH, pairs)
-        first = jnp.where(y == s, came, first)
-        second = jnp.where(y == (s + 1) % Y, came, second)
-
-    head = lax.all_gather(jnp.stack([first, second]), "col", axis_index_groups=chips)
+    got = shared(jnp.concatenate([moved, head[None]]), "row", along_y)
+    g = lax.all_gather(got[:, :2], "row", axis_index_groups=along_x)
+
+    head = lax.all_gather(got[:2, 2], "col", axis_index_groups=chips)
     tiles = shared(jnp.stack([head[0, 0], head[0, 1], head[1, 1]]), "col", along_z)
-    got, tiles = lax.optimization_barrier((got, tiles))
-    g = lax.all_gather(got, "row", axis_index_groups=along_x)
     lower, w, left = factor(tiles, r)
     return update(jnp.stack([row, col]).astype(jnp.int32), cov, g, w, lower, left)
 

time: 165 us -> 153 us (0.927)
  starting transfers between devices: 41.4 us -> 31 us
  waiting for transfers between devices: 34.3 us -> 31.5 us
  local copies, waits for them, and re-layouts: 5.81 us -> 7.54 us
    all_to_all x1, waiting for transfers between devices: 0.01 us -> 23.5 us  [shared(): return lax.all_to_all(many, axis, 0, 0, axis_index_groups=groups)]
    all_gather x1, waiting for transfers between devices: 15.5 us -> 0.01 us  [on_device(): g = lax.all_gather(got[:, :2], 'row', axis_index_groups=along_x)]
    ppermute x7 -> x0, waiting for transfers between devices: 10.3 us -> none  [on_device(): came = lax.ppermute(head, BOTH, pairs)]
    all_to_all x1, starting transfers between devices: 11.3 us -> 5.58 us  [shared(): return lax.all_to_all(many, axis, 0, 0, axis_index_groups=groups)]
    ppermute x7 -> x0, starting transfers between devices: 5.27 us -> none  [on_device(): came = lax.ppermute(head, BOTH, pairs)]
    all_gather x1, waiting for transfers between devices: 3.53 us -> 0.01 us  [on_device(): r = lax.all_gather(mine, 'col')]
    ppermute x1, waiting for transfers between devices: 3.19 us -> 6.3 us  [on_device(): moved = lax.ppermute(mine, BOTH, pairs)]
    all_gather x1, blocking collectives: 7.49 us -> 4.41 us  [on_device(): head = lax.all_gather(got[:2, 2], 'col', axis_index_groups=chips)]
  transfers between devices with their start and end apart: 21 -> 14, of which waited for: 5 -> 3; matrix products, arithmetic and copies ran while one was open for 1% -> 2% of each run, Pallas kernels for 11% -> 12%
where the time goes in v6:
time: 153 us
  blocking collectives  36 us (24%)
  waiting for transfers between devices  31.5 us (21%)
  Pallas kernels  31.5 us (21%)
  starting transfers between devices  31 us (20%)
  between operations  13.7 us (9%)
  local copies, waits for them, and re-layouts  7.54 us (5%)
  other arithmetic  1.53 us (1%)
    all_to_all x1, blocking collectives, shared(): return lax.all_to_all(many, axis, 0, 0, axis_index_groups=groups)  31.6 us
    all_to_all x1, waiting for transfers between devices, shared(): return lax.all_to_all(many, axis, 0, 0, axis_index_groups=groups)  23.5 us
    ppermute x7, starting transfers between devices, on_device(): mine = mine + lax.ppermute(panel[:, s], BOTH, pairs)  18.6 us
    pallas_call x1, Pallas kernels, factor(): pl.pallas_call(factor_kernel, out_shape=[jax.ShapeDtypeStruct(shape, jnp....  18.5 us
    pallas_call x1, Pallas kernels, update(): pl.pallas_call(update_kernel, out_shape=jax.ShapeDtypeStruct(cov.shape, j...  13 us
    ppermute x1, waiting for transfers between devices, on_device(): moved = lax.ppermute(mine, BOTH, pairs)  6.3 us
    all_to_all x1, starting transfers between devices, shared(): return lax.all_to_all(many, axis, 0, 0, axis_index_groups=groups)  5.58 us
    ppermute x1, starting transfers between devices, on_device(): moved = lax.ppermute(mine, BOTH, pairs)  4.76 us
  transfers between devices with their start and end apart: 14, of which 3 were waited for; matrix products, arithmetic and copies ran while one was open for 2% of the time, Pallas kernels for 12%

profile of v6, /device:TPU:1, one launch (start us, length us, event | category | flops | bytes accessed | tf_op | source)
XLA Modules:
  0.0 152.7 jit_solution(3381808335830702525)
XLA Ops:
  6.5 0.0 all-gather.8.cloned.1.call-start
  6.5 2.0 %slice.48 = f32[2,256,1,256]{3,2,1,0:T(1,128)S(1)} slice(f32[2,256,4,256]{3,2,1,0:T(4,128)} %cov_ref.1), slice={[0:2], [0:256], [0:1], [0:256]} | slice | bytes 1048576 | tf_op jit(solution)/shard_map/slice | solution.py:278
  8.6 4.8 %collective-permute-start = (f32[2,32,256]{2,1,0:T(8,128)S(1)}, f32[2,32,256]{2,1,0:T(8,128)S(1)}, u32[]{:S(2)}, u32[]{:S(2)}) collective-permute-start(f32[2,32,256]{2,1,0:T(8,128)S(1)} %get-tuple-element.11), channel_id=1, source_target_pairs={{0,2},{1,3},{16,18},{17,19},{32,34},{33,35},{48,50},{49,51},{64,66... | collective-permute-start | bytes 196616 | tf_op jit(solution)/shard_map/ppermute | solution.py:283
  13.4 7.3 %collective-permute-start.4 = (f32[2,32,256]{2,1,0:T(8,128)S(1)}, f32[2,32,256]{2,1,0:T(8,128)S(1)}, u32[]{:S(2)}, u32[]{:S(2)}) collective-permute-start(f32[2,32,256]{2,1,0:T(8,128)S(1)} %get-tuple-element.12), channel_id=1, source_target_pairs={{0,10},{1,11},{16,26},{17,27},{32,42},{33,43},{48,58},{49,59},{64,... | collective-permute-start | bytes 196616 | tf_op jit(solution)/shard_map/ppermute | solution.py:283
  20.7 1.3 collective-permute-start.3
  22.0 1.3 collective-permute-start.2
  23.3 1.3 collective-permute-start.1
  24.6 0.0 collective-permute-done
  24.6 1.3 collective-permute-start.6
  25.9 0.0 collective-permute-done.4
  26.0 1.3 collective-permute-start.5
  27.3 0.0 collective-permute-done.3
  27.3 0.0 collective-permute-done.2
  27.3 0.0 collective-permute-done.1
  27.3 0.0 collective-permute-done.6
  27.3 1.7 %collective-permute-done.5 = f32[2,32,256]{2,1,0:T(8,128)S(1)} collective-permute-done((f32[2,32,256]{2,1,0:T(8,128)S(1)}, f32[2,32,256]{2,1,0:T(8,128)S(1)}, u32[]{:S(2)}, u32[]{:S(2)}) %collective-permute-start.5) | collective-permute-done | bytes 65568 | tf_op jit(solution)/shard_map/ppermute | solution.py:283
  29.0 0.7 fusion.8
  29.6 0.0 all-gather.8.cloned.1.call-update
  29.6 0.0 all-gather.6.cloned.1.call-start
  29.7 0.8 slice_bitcast_fusion.11
  30.5 0.7 collective-permute-start.9
  31.1 0.7 collective-permute-start.8
  31.8 0.7 collective-permute-start.10
  32.5 4.8 %collective-permute-start.7 = (f32[2,32,256]{2,1,0:T(8,128)}, f32[2,32,256]{2,1,0:T(8,128)S(1)}, u32[]{:S(2)}, u32[]{:S(2)}) collective-permute-start(f32[2,32,256]{2,1,0:T(8,128)} %fusion.8), channel_id=1, source_target_pairs={{0,0},{1,128},{2,16},{3,144},{4,32},{5,160},{6,48},{7,176},{8,64},... | collective-permute-start | bytes 196616 | tf_op jit(solution)/shard_map/ppermute | solution.py:292
  37.2 0.0 collective-permute-done.9
  37.3 0.0 collective-permute-done.8
  37.3 0.0 collective-permute-done.10
  37.3 0.8 add_bitcast_fusion
  38.1 6.3 %collective-permute-done.7 = f32[2,32,256]{2,1,0:T(8,128)S(1)} collective-permute-done((f32[2,32,256]{2,1,0:T(8,128)}, f32[2,32,256]{2,1,0:T(8,128)S(1)}, u32[]{:S(2)}, u32[]{:S(2)}) %collective-permute-start.7) | collective-permute-done | bytes 65568 | tf_op jit(solution)/shard_map/ppermute | solution.py:292
  44.4 0.1 broadcast_in_dim.26
  44.5 31.6 %all_to_all.10 = f32[8,3,32,256]{3,2,1,0:T(8,128)S(1)} all-to-all(f32[8,3,32,256]{3,2,1,0:T(8,128)S(1)} %broadcast_in_dim.26), channel_id=1, replica_groups={{0,16,32,48,64,80,96,112},{128,144,160,176,192,208,224,240},{256,272,28..., dimensions={0} | all-to-all | bytes 1572864 | tf_op jit(solution)/shard_map/all_to_all | solution.py:268
  76.1 0.9 slice.72
  76.9 0.0 all-gather.6.cloned.1.call-update
  77.0 4.4 %all-gather.1 = f32[4,1,32,256]{3,2,1,0:T(8,128)S(1)} all-gather(f32[2,1,32,256]{3,2,1,0:T(8,128)S(1)} %slice.73), channel_id=3, replica_groups={{0,1},{2,3},{4,5},{6,7},{8,9},{10,11},{12,13},{14,15},{16,17},{18,19},{..., dimensions={0}, use_global_device_ids=true | all-gather | bytes 196608 | tf_op jit(solution)/shard_map/all_gather | solution.py:301
  81.4 0.0 copy-start
  81.4 1.0 broadcast_in_dim.27
  82.4 5.6 %all-to-all-start.1 = ((f32[8,3,32,256]{3,2,1,0:T(8,128)}), f32[8,3,32,256]{3,2,1,0:T(8,128)S(1)}, u32[]{:S(2)}, u32[]{:S(2)}) async-start(f32[8,3,32,256]{3,2,1,0:T(8,128)} %broadcast_in_dim.27), calls=%async_computation.1 | async-start | bytes 1572864 | tf_op jit(solution)/shard_map/all_to_all | solution.py:268
  88.0 0.1 pad_add_fusion.place_ref
  88.0 0.0 all-gather.8.cloned.1.call-done
  88.0 23.5 %all-to-all-done.1.tiles_ref = f32[8,3,32,256]{3,2,1,0:T(8,128)S(1)} async-done(((f32[8,3,32,256]{3,2,1,0:T(8,128)}), f32[8,3,32,256]{3,2,1,0:T(8,128)S(1)}, u32[]{:S(2)}, u32[]{:S(2)}) %all-to-all-start.1) | async-done | bytes 786464 | tf_op jit(solution)/shard_map/all_to_all | solution.py:268
  111.5 18.5 %factor.1 = (f32[512,512]{1,0:T(8,128)S(1)}, f32[3,256,256]{2,1,0:T(8,128)S(1)}, f32[512,512]{1,0:T(8,128)S(1)}) custom-call(f32[8,3,32,256]{3,2,1,0:T(8,128)S(1)} %all-to-all-done.1.tiles_ref, f32[8,2,2,32,256]{4,3,2,1,0:T(8,128)} %bitcast.83), custom_call_target="tpu_custom_call" | custom-call | tf_op jit(solution)/shard_map/factor/pallas_call | solution.py:169
  130.1 0.0 copy-start.1
  130.1 1.0 copy-done.1
  131.0 0.0 copy-start.2
  131.0 1.0 copy-done.2
  132.0 0.0 copy-start.3
  132.0 0.9 copy-done.3
  132.9 0.0 all-gather.6.cloned.1.call-done
  132.9 0.0 copy-done
  132.9 13.0 %update.1 = f32[2,256,4,256]{3,2,1,0:T(4,128)} custom-call(s32[2]{0:T(128)S(1)} %pad_add_fusion.place_ref, f32[2,256,4,256]{3,2,1,0:T(4,128)S(1)} %copy-done, f32[4,8,2,32,256]{4,3,2,1,0:T(8,128)} %bitcast.82, f32[3,256,256]{2,1,0:T(8,128)} %copy-done.3, f32[512,512]{1,0:T(8,128)} %copy-done.1, f32[512,512]{1,0:T(8,128)} %copy-done.2), custom_call_target="tpu_custom_call" | custom-call | tf_op jit(solution)/shard_map/update/pallas_call | solution.py:248
  (6 shorter events, 0.1 us)
Async XLA Ops:
  6.5 81.5 %all-gather.8.cloned.1.call-start = ((), (), s32[]{:S(2)}) async-start(), calls=%async_computation.3 | async-start | bytes 1114112 | tf_op jit(solution)/shard_map/all_gather | solution.py:284
  8.6 16.1 %collective-permute-start = (f32[2,32,256]{2,1,0:T(8,128)S(1)}, f32[2,32,256]{2,1,0:T(8,128)S(1)}, u32[]{:S(2)}, u32[]{:S(2)}) collective-permute-start(f32[2,32,256]{2,1,0:T(8,128)S(1)} %get-tuple-element.11), channel_id=1, source_target_pairs={{0,2},{1,3},{16,18},{17,19},{32,34},{33,35},{48,50},{49,51},{64,66... | collective-permute-start | bytes 196616 | tf_op jit(solution)/shard_map/ppermute | solution.py:283
  13.4 12.5 %collective-permute-start.4 = (f32[2,32,256]{2,1,0:T(8,128)S(1)}, f32[2,32,256]{2,1,0:T(8,128)S(1)}, u32[]{:S(2)}, u32[]{:S(2)}) collective-permute-start(f32[2,32,256]{2,1,0:T(8,128)S(1)} %get-tuple-element.12), channel_id=1, source_target_pairs={{0,10},{1,11},{16,26},{17,27},{32,42},{33,43},{48,58},{49,59},{64,... | collective-permute-start | bytes 196616 | tf_op jit(solution)/shard_map/ppermute | solution.py:283
  20.7 6.5 %collective-permute-start.3 = (f32[2,32,256]{2,1,0:T(8,128)S(1)}, f32[2,32,256]{2,1,0:T(8,128)S(1)}, u32[]{:S(2)}, u32[]{:S(2)}) collective-permute-start(f32[2,32,256]{2,1,0:T(8,128)S(1)} %get-tuple-element.13), channel_id=1, source_target_pairs={{0,8},{1,9},{16,24},{17,25},{32,40},{33,41},{48,56},{49,57},{64,72... | collective-permute-start | bytes 196616 | tf_op jit(solution)/shard_map/ppermute | solution.py:283
  22.0 5.3 %collective-permute-start.2 = (f32[2,32,256]{2,1,0:T(8,128)S(1)}, f32[2,32,256]{2,1,0:T(8,128)S(1)}, u32[]{:S(2)}, u32[]{:S(2)}) collective-permute-start(f32[2,32,256]{2,1,0:T(8,128)S(1)} %get-tuple-element.14), channel_id=1, source_target_pairs={{0,6},{1,7},{16,22},{17,23},{32,38},{33,39},{48,54},{49,55},{64,70... | collective-permute-start | bytes 196616 | tf_op jit(solution)/shard_map/ppermute | solution.py:283
  23.3 4.0 %collective-permute-start.1 = (f32[2,32,256]{2,1,0:T(8,128)S(1)}, f32[2,32,256]{2,1,0:T(8,128)S(1)}, u32[]{:S(2)}, u32[]{:S(2)}) collective-permute-start(f32[2,32,256]{2,1,0:T(8,128)S(1)} %get-tuple-element.15), channel_id=1, source_target_pairs={{0,4},{1,5},{16,20},{17,21},{32,36},{33,37},{48,52},{49,53},{64,68... | collective-permute-start | bytes 196616 | tf_op jit(solution)/shard_map/ppermute | solution.py:283
  24.6 2.7 %collective-permute-start.6 = (f32[2,32,256]{2,1,0:T(8,128)S(1)}, f32[2,32,256]{2,1,0:T(8,128)S(1)}, u32[]{:S(2)}, u32[]{:S(2)}) collective-permute-start(f32[2,32,256]{2,1,0:T(8,128)S(1)} %get-tuple-element.16), channel_id=1, source_target_pairs={{0,14},{1,15},{16,30},{17,31},{32,46},{33,47},{48,62},{49,63},{64,... | collective-permute-start | bytes 196616 | tf_op jit(solution)/shard_map/ppermute | solution.py:283
  26.0 3.0 %collective-permute-start.5 = (f32[2,32,256]{2,1,0:T(8,128)S(1)}, f32[2,32,256]{2,1,0:T(8,128)S(1)}, u32[]{:S(2)}, u32[]{:S(2)}) collective-permute-start(f32[2,32,256]{2,1,0:T(8,128)S(1)} %get-tuple-element.17), channel_id=1, source_target_pairs={{0,12},{1,13},{16,28},{17,29},{32,44},{33,45},{48,60},{49,61},{64,... | collective-permute-start | bytes 196616 | tf_op jit(solution)/shard_map/ppermute | solution.py:283
  29.6 103.2 %all-gather.6.cloned.1.call-start = ((), (), s32[]{:S(2)}) async-start(), calls=%async_computation.2 | async-start | bytes 2621440 | tf_op jit(solution)/shard_map/all_gather | solution.py:299
  30.5 6.8 %collective-permute-start.9 = (f32[32,256]{1,0:T(8,128)S(1)}, f32[32,256]{1,0:T(8,128)S(1)}, u32[]{:S(2)}, u32[]{:S(2)}) collective-permute-start(f32[32,256]{1,0:T(8,128)S(1)} %slice_bitcast_fusion.11), channel_id=1, source_target_pairs={{0,256},{16,272},{17,273},{2,258},{18,274},{19,275},{4,260},{20,27... | collective-permute-start | bytes 98312 | tf_op jit(solution)/shard_map/ppermute | solution.py:297
  31.1 6.1 %collective-permute-start.8 = (f32[32,256]{1,0:T(8,128)S(1)}, f32[32,256]{1,0:T(8,128)S(1)}, u32[]{:S(2)}, u32[]{:S(2)}) collective-permute-start(f32[32,256]{1,0:T(8,128)S(1)} %slice_bitcast_fusion.11), channel_id=1, source_target_pairs={{0,128},{16,144},{17,145},{2,130},{18,146},{19,147},{4,132},{20,14... | collective-permute-start | bytes 98312 | tf_op jit(solution)/shard_map/ppermute | solution.py:297
  31.8 5.5 %collective-permute-start.10 = (f32[32,256]{1,0:T(8,128)S(1)}, f32[32,256]{1,0:T(8,128)S(1)}, u32[]{:S(2)}, u32[]{:S(2)}) collective-permute-start(f32[32,256]{1,0:T(8,128)S(1)} %slice_bitcast_fusion.11), channel_id=1, source_target_pairs={{0,384},{16,400},{17,401},{2,386},{18,402},{19,403},{4,388},{20,40... | collective-permute-start | bytes 98312 | tf_op jit(solution)/shard_map/ppermute | solution.py:297
  32.5 11.9 %collective-permute-start.7 = (f32[2,32,256]{2,1,0:T(8,128)}, f32[2,32,256]{2,1,0:T(8,128)S(1)}, u32[]{:S(2)}, u32[]{:S(2)}) collective-permute-start(f32[2,32,256]{2,1,0:T(8,128)} %fusion.8), channel_id=1, source_target_pairs={{0,0},{1,128},{2,16},{3,144},{4,32},{5,160},{6,48},{7,176},{8,64},... | collective-permute-start | bytes 196616 | tf_op jit(solution)/shard_map/ppermute | solution.py:292
  81.4 51.5 %copy-start = (f32[2,256,4,256]{3,2,1,0:T(4,128)S(1)}, f32[2,256,4,256]{3,2,1,0:T(4,128)}, u32[]{:S(2)}) copy-start(f32[2,256,4,256]{3,2,1,0:T(4,128)} %cov_ref.1) | copy-start | bytes 6291460
  82.4 29.2 %all-to-all-start.1 = ((f32[8,3,32,256]{3,2,1,0:T(8,128)}), f32[8,3,32,256]{3,2,1,0:T(8,128)S(1)}, u32[]{:S(2)}, u32[]{:S(2)}) async-start(f32[8,3,32,256]{3,2,1,0:T(8,128)} %broadcast_in_dim.27), calls=%async_computation.1 | async-start | bytes 1572864 | tf_op jit(solution)/shard_map/all_to_all | solution.py:268
  130.1 1.0 copy-start.1
  131.0 1.0 copy-start.2
  132.0 0.9 copy-start.3
Sparse Core Ops, SparseCore 0:
  29.8 43.0 all-gather.7
  77.1 31.6 all-gather.5

commit v7 on v2

--- a/solution.py
+++ b/solution.py
@@ -42,7 +42,7 @@
     return terms[0]
 
 
-def factor_block(rows, s_ref):
+def factor_block(rows, s_ref, between):
     count = len(rows)
     rows = list(rows)
     sub = lax.broadcasted_iota(jnp.int32, (SUB, LANE), 0)
@@ -96,54 +96,8 @@
             y = jnp.where(sub == k, ys[k], y)
         rows[p] = jnp.where(lane >= sub + SUB * p, x, 0.0)
         aug[p] = y
+        between()
     return jnp.concatenate(rows, 0), jnp.concatenate(aug, 0)
-
-
-def factor_kernel(core_ref, mine_ref, other_ref, l_ref, w_ref, a_ref, s_ref):
-    n = a_ref.shape[0]
-    nb = n // LANE
-
-    for core, (first, second) in enumerate(((mine_ref, other_ref), (other_ref, mine_ref))):
-
-        @pl.when(core_ref[0] == core)
-        def _():
-            a_ref[:NB, :NB] = first[:, 0].reshape(NB, NB)
-            a_ref[NB:, :NB] = first[:, 1].reshape(NB, NB)
-            a_ref[NB:, NB:] = second[:, 1].reshape(NB, NB)
-
-    def blk(i):
-        return slice(i * LANE, (i + 1) * LANE)
-
-    inverses = []
-    for b in range(nb):
-        rows = [a_ref[b * LANE + SUB * g : b * LANE + SUB * (g + 1), blk(b)] for g in range(LANE // SUB)]
-        upper, inverse = factor_block(rows, s_ref)
-        inverses.append(inverse)
-        l_ref[blk(b), blk(b)] = upper
-        for i in range(b + 1, nb):
-            panel = dot_nt(a_ref[blk(i), blk(b)], inverse)
-            l_ref[blk(i), blk(b)] = panel
-            for j in range(b + 1, i + 1):
-                a_ref[blk(i), blk(j)] = a_ref[blk(i), blk(j)] - dot_nt(panel, l_ref[blk(j), blk(b)])
-        half, odd = divmod(b, 2)
-        w_ref[half, blk(odd), blk(odd)] = inverse
-        if odd:
-            w_ref[half, blk(0), blk(1)] = jnp.zeros((LANE, LANE), jnp.float32)
-            w_ref[half, blk(1), blk(0)] = -dot_nn(inverse, dot_nn(l_ref[blk(b), blk(b - 1)], inverses[b - 1]))
-
-
-def factor(core, mine, other):
-    n = 2 * NB
-    vmem = pl.BlockSpec(memory_space=pltpu.VMEM)
-    return pl.pallas_call(
-        factor_kernel,
-        out_shape=[jax.ShapeDtypeStruct((n, n), jnp.float32), jax.ShapeDtypeStruct((2, NB, NB), jnp.float32)],
-        in_specs=[pl.BlockSpec(memory_space=pltpu.SMEM), vmem, vmem],
-        out_specs=[vmem, vmem],
-        scratch_shapes=[pltpu.VMEM((n, n), jnp.float32), pltpu.VMEM((2 * SUB * (SUB + 2), LANE), jnp.float32)],
-        compiler_params=pltpu.CompilerParams(vmem_limit_bytes=16 * 2**20),
-        name="factor",
-    )(core, mine, other)
 
 
 def split(x):
@@ -162,40 +116,124 @@
     return out
 
 
-def update_kernel(place_ref, cov_hbm, r_ref, g_ref, w_ref, l_ref, out_ref, cov_ref, s_ref, sem):
+def head_and_update_kernel(
+    place_ref, cov_ref, mine_hbm, other_hbm, r_hbm, g_hbm, out_ref,
+    tiles_ref, r_ref, g_ref, a_ref, l_ref, w_ref, s0_ref, t_ref, s1_ref, spread_ref, sems,
+):
     trd, nb, tcd, _ = cov_ref.shape
-    copy = pltpu.make_async_copy(cov_hbm, cov_ref, sem)
-    copy.start()
-    w0, l10, w1 = split(w_ref[0]), split(l_ref[NB:, :NB]), split(w_ref[1])
-
-    def solve(p0, p1):
-        s0 = dot6(split(p0), w0)
-        a0 = split(s0)
-        s1 = dot6(split(p1 - dot6(a0, l10)), w1)
-        return s0, a0, s1, split(s1)
-
-    for b in range(0, tcd, 2):
-        p0, p1 = (
-            jnp.concatenate([g_ref[2 * h + k, :, b // 2].reshape(NB, NB) for h in range(2)], 0) for k in range(2)
-        )
-        _, a0, _, a1 = solve(p0, p1)
-        for j in range(3):
-            for h in range(2):
-                s_ref[j, b + h, :, :NB] = a0[j][h * NB : (h + 1) * NB]
-                s_ref[j, b + h, :, NB:] = a1[j][h * NB : (h + 1) * NB]
-    p0, p1 = (jnp.concatenate([r_ref[:, k, a].reshape(NB, NB) for a in range(trd)], 0) for k in range(2))
-    s0, a0, s1, a1 = solve(p0, p1)
-    left = [jnp.concatenate([u, v], 1) for u, v in zip(a0, a1)]
-    copy.wait()
-    for b in range(tcd):
-        u = dot6(left, [s_ref[j, b] for j in range(3)])
+    row, col = place_ref[0], place_ref[1]
+    fetches = [pltpu.make_async_copy(r_hbm, r_ref, sems.at[3])]
+    fetches += [pltpu.make_async_copy(g_hbm.at[:, :, a], g_ref.at[a], sems.at[4 + a]) for a in range(2)]
+    for core, sources in enumerate(((mine_hbm, mine_hbm, other_hbm), (other_hbm, other_hbm, mine_hbm))):
+
+        @pl.when(lax.rem(col, CORE) == core)
+        def _():
+            copies = [
+                pltpu.make_async_copy(source.at[:, min(i, 1)], tiles_ref.at[i], sems.at[i])
+                for i, source in enumerate(sources)
+            ]
+            for copy in copies:
+                copy.start()
+            for copy in copies:
+                copy.wait()
+
+    for fetch in fetches:
+        fetch.start()
+    for i, at in enumerate(((0, 0), (1, 0), (1, 1))):
+        a_ref[at[0] * NB : (at[0] + 1) * NB, at[1] * NB : (at[1] + 1) * NB] = tiles_ref[i].reshape(NB, NB)
+
+    def blk(i):
+        return slice(i * LANE, (i + 1) * LANE)
+
+    def panel(k, pair):
+        if pair == 0:
+            parts = [r_ref[:, k, a] for a in range(trd)]
+        else:
+            parts = [g_ref[pair - 1, 2 * h + k] for h in range(2)]
+        return jnp.concatenate([part.reshape(NB, NB) for part in parts], 0)
+
+    def rows_of(pair):
+        return slice(pair * 2 * NB, (pair + 1) * 2 * NB)
+
+    def keep(ref, rows, parts):
+        for j, part in enumerate(parts):
+            ref[j, rows] = part
+
+    def parts_of(ref, rows):
+        return [ref[j, rows] for j in range(3)]
+
+    def tile_of(b):
+        return slice((trd + b) * NB, (trd + b + 1) * NB)
+
+    pairs = 1 + tcd // 2
+    weights = {}
+
+    def first_solve(pair):
+        keep(s0_ref, rows_of(pair), split(dot6(split(panel(0, pair)), weights[0])))
+
+    def second_panel(pair):
+        keep(t_ref, rows_of(pair), split(panel(1, pair) - dot6(parts_of(s0_ref, rows_of(pair)), weights[1])))
+
+    def first_update(b):
+        u = dot6(parts_of(s0_ref, rows_of(0)), parts_of(s0_ref, tile_of(b)))
         for a in range(trd):
             out_ref[a, :, b, :] = cov_ref[a, :, b, :] - u[a * nb : (a + 1) * nb]
-    row, col = place_ref[0], place_ref[1]
-    for k, s in enumerate((s0, s1)):
+
+    work = []
+    for pair in range(pairs):
+        work.append((first_solve, pair))
+    for pair in range(pairs):
+        work.append((second_panel, pair))
+    for b in range(tcd):
+        work.append((first_update, b))
+    ticks = [0]
+
+    def nothing():
+        pass
+
+    def some_work():
+        ticks[0] += 1
+        if ticks[0] % 3 == 0 and work:
+            step, index = work.pop(0)
+            step(index)
+
+    count = a_ref.shape[0] // LANE
+    inverses = []
+    for b in range(count):
+        rows = [a_ref[b * LANE + SUB * g : b * LANE + SUB * (g + 1), blk(b)] for g in range(LANE // SUB)]
+        upper, inverse = factor_block(rows, spread_ref, some_work if b > 1 else nothing)
+        inverses.append(inverse)
+        l_ref[blk(b), blk(b)] = upper
+        for i in range(b + 1, count):
+            below = dot_nt(a_ref[blk(i), blk(b)], inverse)
+            l_ref[blk(i), blk(b)] = below
+            for j in range(b + 1, i + 1):
+                a_ref[blk(i), blk(j)] = a_ref[blk(i), blk(j)] - dot_nt(below, l_ref[blk(j), blk(b)])
+        half, odd = divmod(b, 2)
+        w_ref[half, blk(odd), blk(odd)] = inverse
+        if odd:
+            w_ref[half, blk(0), blk(1)] = jnp.zeros((LANE, LANE), jnp.float32)
+            w_ref[half, blk(1), blk(0)] = -dot_nn(inverse, dot_nn(l_ref[blk(b), blk(b - 1)], inverses[b - 1]))
+        if b == 1:
+            weights[0], weights[1] = split(w_ref[0]), split(l_ref[NB:, :NB])
+            for fetch in fetches:
+                fetch.wait()
+    while work:
+        step, index = work.pop(0)
+        step(index)
+    last = split(w_ref[1])
+    for pair in range(pairs):
+        keep(s1_ref, rows_of(pair), split(dot6(parts_of(t_ref, rows_of(pair)), last)))
+    for b in range(tcd):
+        u = dot6(parts_of(s1_ref, rows_of(0)), parts_of(s1_ref, tile_of(b)))
+        for a in range(trd):
+            out_ref[a, :, b, :] = out_ref[a, :, b, :] - u[a * nb : (a + 1) * nb]
+
+    for k, ref in enumerate((s0_ref, s1_ref)):
 
         @pl.when(col == k)
         def _():
+            s = sum(ref[j, rows_of(0)].astype(jnp.float32) for j in (2, 1, 0))
             for a in range(trd):
                 out_ref[a, :, 0, :] = s[a * nb : (a + 1) * nb]
 
@@ -212,30 +250,38 @@
                     for v in range(2):
                         if i == j and u < v:
                             continue
-                        block = l_ref[
-                            i * NB + u * LANE : i * NB + (u + 1) * LANE, j * NB + v * LANE : j * NB + (v + 1) * LANE
-                        ]
-                        out_ref[0, u * LANE : (u + 1) * LANE, 0, v * LANE : (v + 1) * LANE] = (
-                            block.T if i == j and u == v else block
-                        )
-
-
-def update(place, cov, r, g, w, lower):
+                        block = l_ref[blk(2 * i + u), blk(2 * j + v)]
+                        out_ref[0, blk(u), 0, blk(v)] = block.T if i == j and u == v else block
+
+
+def head_and_update(place, cov, mine, other, r, g):
     trd, nb, tcd, _ = cov.shape
-    vmem = pl.BlockSpec(memory_space=pltpu.VMEM)
+    n = 2 * NB
+    vmem, hbm = (pl.BlockSpec(memory_space=space) for space in (pltpu.VMEM, pltpu.HBM))
+    moved = [mine, other, r.reshape(Z, CORE, trd, PART, nb), g]
+    moved = [pltpu.with_memory_space_constraint(array, pltpu.HBM) for array in moved]
+    solved = pltpu.VMEM((3, (trd + tcd) * nb, nb), jnp.bfloat16)
     return pl.pallas_call(
-        update_kernel,
+        head_and_update_kernel,
         out_shape=jax.ShapeDtypeStruct(cov.shape, jnp.float32),
-        in_specs=[pl.BlockSpec(memory_space=pltpu.SMEM), pl.BlockSpec(memory_space=pl.ANY), vmem, vmem, vmem, vmem],
+        in_specs=[pl.BlockSpec(memory_space=pltpu.SMEM), vmem] + [hbm] * len(moved),
         out_specs=vmem,
         scratch_shapes=[
-            pltpu.VMEM(cov.shape, jnp.float32),
-            pltpu.VMEM((3, tcd, nb, 2 * nb), jnp.bfloat16),
-            pltpu.SemaphoreType.DMA,
+            pltpu.VMEM((3, Z, PART, nb), jnp.float32),
+            pltpu.VMEM((Z, CORE, trd, PART, nb), jnp.float32),
+            pltpu.VMEM((2, X, Y, PART, nb), jnp.float32),
+            pltpu.VMEM((n, n), jnp.float32),
+            pltpu.VMEM((n, n), jnp.float32),
+            pltpu.VMEM((2, nb, nb), jnp.float32),
+            solved,
+            solved,
+            solved,
+            pltpu.VMEM((2 * SUB * (SUB + 2), LANE), jnp.float32),
+            pltpu.SemaphoreType.DMA((6,)),
         ],
-        compiler_params=pltpu.CompilerParams(vmem_limit_bytes=28 * 2**20),
+        compiler_params=pltpu.CompilerParams(vmem_limit_bytes=32 * 2**20),
         name="update",
-    )(place, cov, r.reshape(Z, CORE, trd, PART, nb), g, w, lower)
+    )(place, cov, *moved)
 
 
 def shared(block, groups):
@@ -245,7 +291,7 @@
 
 def on_device(cov):
     row, col = lax.axis_index("row"), lax.axis_index("col")
-    x, z, core = row // Y, col // CORE, col % CORE
+    x, z = row // Y, col // CORE
     panel = cov[:, :, 0, :].reshape(2, Z, PART, NB)
 
     mine = jnp.where(z == 0, panel[:, 0], 0.0)
@@ -272,8 +318,7 @@
     many = jnp.broadcast_to(got[None, :2, 2], (Z, 2, PART, NB))
     tiles = lax.all_to_all(many, "col", 0, 0, axis_index_groups=[[c * CORE + k for c in range(Z)] for k in range(CORE)])
     other = lax.ppermute(tiles, "col", [(i, i ^ 1) for i in range(N_COL)])
-    lower, w = factor(core.astype(jnp.int32).reshape(1), tiles, other)
-    return update(jnp.stack([row, col]).astype(jnp.int32), cov, r, g, w, lower)
+    return head_and_update(jnp.stack([row, col]).astype(jnp.int32), cov, tiles, other, r, g)
 
 
 def solution(mesh):

time: 144 us -> 142 us (0.986)
  local copies, waits for them, and re-layouts: 10.6 us -> 3.76 us
  waiting for transfers between devices: 9.45 us -> 14.5 us
    unnamed x15 -> x7, local copies, waits for them, and re-layouts: 6.88 us -> 0.05 us
    all_gather x1, waiting for transfers between devices: 0.01 us -> 5.03 us  [on_device(): lax.all_gather(got[:, :2], 'row', axis_index_groups=[[i * Y + j for i in...]
    pallas_call x2 -> x1, Pallas kernels: 26.5 us -> 25.4 us  [head_and_update(): pl.pallas_call(head_and_update_kernel, out_shape=jax.ShapeDtypeStruct(cov...]
  transfers between devices with their start and end apart: 14 -> 14, of which waited for: 3 -> 4; matrix products, arithmetic and copies ran while one was open for 2% -> 2% of each run, Pallas kernels for 10% -> 0%
where the time goes in v7:
time: 142 us; the launch traced here: 141 us
  blocking collectives  49.4 us (35%)
  starting transfers between devices  32.8 us (23%)
  Pallas kernels  25.4 us (18%)
  waiting for transfers between devices  14.5 us (10%)
  between operations  13.7 us (10%)
  local copies, waits for them, and re-layouts  3.76 us (3%)
  other arithmetic  1.53 us (1%)
    all_to_all x1, blocking collectives, shared(): return lax.all_to_all(many, 'row', 0, 0, axis_index_groups=groups)  31.7 us
    pallas_call x1, Pallas kernels, head_and_update(): pl.pallas_call(head_and_update_kernel, out_shape=jax.ShapeDtypeStruct(cov...  25.4 us
    ppermute x7, starting transfers between devices, on_device(): mine = mine + lax.ppermute(panel[:, s], BOTH, pairs)  18.6 us
    all_to_all x1, blocking collectives, on_device(): lax.all_to_all(many, 'col', 0, 0, axis_index_groups=[[c * CORE + k for c...  17.7 us
    ppermute x1, starting transfers between devices, on_device(): other = lax.ppermute(tiles, 'col', [(i, i ^ 1) for i in range(N_COL)])  7.37 us
    ppermute x1, waiting for transfers between devices, on_device(): mine = lax.ppermute(mine, BOTH, pairs)  6.3 us
    all_gather x1, waiting for transfers between devices, on_device(): lax.all_gather(got[:, :2], 'row', axis_index_groups=[[i * Y + j for i in...  5.03 us
    ppermute x1, starting transfers between devices, on_device(): mine = lax.ppermute(mine, BOTH, pairs)  4.76 us
  transfers between devices with their start and end apart: 14, of which 4 were waited for; matrix products, arithmetic and copies ran while one was open for 2% of the time, Pallas kernels for 0%

profile of v7, /device:TPU:1, one launch (start us, length us, event | category | flops | bytes accessed | tf_op | source)
XLA Modules:
  0.0 141.0 jit_solution(7403325174244566451)
XLA Ops:
  6.5 0.0 all-gather.5.cloned.1.call-start
  6.5 2.0 %slice.39 = f32[2,256,1,256]{3,2,1,0:T(1,128)S(1)} slice(f32[2,256,4,256]{3,2,1,0:T(4,128)} %cov_ref.1), slice={[0:2], [0:256], [0:1], [0:256]} | slice | bytes 1048576 | tf_op jit(solution)/shard_map/slice | solution.py:295
  8.6 4.8 %collective-permute-start = (f32[2,32,256]{2,1,0:T(8,128)S(1)}, f32[2,32,256]{2,1,0:T(8,128)S(1)}, u32[]{:S(2)}, u32[]{:S(2)}) collective-permute-start(f32[2,32,256]{2,1,0:T(8,128)S(1)} %get-tuple-element.5), channel_id=1, source_target_pairs={{0,2},{1,3},{16,18},{17,19},{32,34},{33,35},{48,50},{49,51},{64,66... | collective-permute-start | bytes 196616 | tf_op jit(solution)/shard_map/ppermute | solution.py:300
  13.4 7.3 %collective-permute-start.4 = (f32[2,32,256]{2,1,0:T(8,128)S(1)}, f32[2,32,256]{2,1,0:T(8,128)S(1)}, u32[]{:S(2)}, u32[]{:S(2)}) collective-permute-start(f32[2,32,256]{2,1,0:T(8,128)S(1)} %get-tuple-element.6), channel_id=1, source_target_pairs={{0,10},{1,11},{16,26},{17,27},{32,42},{33,43},{48,58},{49,59},{64,... | collective-permute-start | bytes 196616 | tf_op jit(solution)/shard_map/ppermute | solution.py:300
  20.7 1.3 collective-permute-start.3
  22.0 1.3 collective-permute-start.2
  23.3 1.3 collective-permute-start.1
  24.6 0.0 collective-permute-done
  24.6 1.3 collective-permute-start.6
  25.9 0.0 collective-permute-done.4
  26.0 1.3 collective-permute-start.5
  27.3 0.0 collective-permute-done.3
  27.3 0.0 collective-permute-done.2
  27.3 0.0 collective-permute-done.1
  27.3 0.0 collective-permute-done.6
  27.3 1.7 %collective-permute-done.5 = f32[2,32,256]{2,1,0:T(8,128)S(1)} collective-permute-done((f32[2,32,256]{2,1,0:T(8,128)S(1)}, f32[2,32,256]{2,1,0:T(8,128)S(1)}, u32[]{:S(2)}, u32[]{:S(2)}) %collective-permute-start.5) | collective-permute-done | bytes 65568 | tf_op jit(solution)/shard_map/ppermute | solution.py:300
  29.0 0.7 fusion.8
  29.6 0.0 all-gather.5.cloned.1.call-update
  29.7 0.0 all-gather.7.cloned.1.call-start
  29.7 0.8 slice_bitcast_fusion.9
  30.5 0.7 collective-permute-start.9
  31.1 0.7 collective-permute-start.8
  31.8 0.7 collective-permute-start.10
  32.5 4.8 %collective-permute-start.7 = (f32[2,32,256]{2,1,0:T(8,128)}, f32[2,32,256]{2,1,0:T(8,128)S(1)}, u32[]{:S(2)}, u32[]{:S(2)}) collective-permute-start(f32[2,32,256]{2,1,0:T(8,128)} %fusion.8), channel_id=1, source_target_pairs={{0,0},{1,128},{2,16},{3,144},{4,32},{5,160},{6,48},{7,176},{8,64},... | collective-permute-start | bytes 196616 | tf_op jit(solution)/shard_map/ppermute | solution.py:314
  37.2 0.0 collective-permute-done.9
  37.3 0.0 collective-permute-done.8
  37.3 0.0 collective-permute-done.10
  37.3 0.8 add_bitcast_fusion
  38.1 6.3 %collective-permute-done.7 = f32[2,32,256]{2,1,0:T(8,128)S(1)} collective-permute-done((f32[2,32,256]{2,1,0:T(8,128)}, f32[2,32,256]{2,1,0:T(8,128)S(1)}, u32[]{:S(2)}, u32[]{:S(2)}) %collective-permute-start.7) | collective-permute-done | bytes 65568 | tf_op jit(solution)/shard_map/ppermute | solution.py:314
  44.4 0.1 broadcast_in_dim.27
  44.5 0.0 copy-start
  44.5 31.7 %all_to_all.10 = f32[8,3,32,256]{3,2,1,0:T(8,128)S(1)} all-to-all(f32[8,3,32,256]{3,2,1,0:T(8,128)S(1)} %broadcast_in_dim.27), channel_id=1, replica_groups={{0,16,32,48,64,80,96,112},{128,144,160,176,192,208,224,240},{256,272,28..., dimensions={0} | all-to-all | bytes 1572864 | tf_op jit(solution)/shard_map/all_to_all | solution.py:289
  76.2 0.8 slice.61
  77.1 0.0 all-gather.7.cloned.1.call-update
  77.2 17.7 %all_to_all.11.mine_hbm = f32[8,2,32,256]{3,2,1,0:T(8,128)S(1)} all-to-all(f32[8,2,32,256]{3,2,1,0:T(8,128)S(1)} %broadcast_in_dim.29), channel_id=1, replica_groups={{0,2,4,6,8,10,12,14},{1,3,5,7,9,11,13,15},{16,18,20,22,24,26,28,30},{17..., dimensions={0} | all-to-all | bytes 1048576 | tf_op jit(solution)/shard_map/all_to_all | solution.py:319
  94.8 0.0 copy-start.1
  94.8 7.4 %collective-permute-start.11 = (f32[8,2,32,256]{3,2,1,0:T(8,128)S(1)}, f32[8,2,32,256]{3,2,1,0:T(8,128)S(1)}, u32[]{:S(2)}, u32[]{:S(2)}) collective-permute-start(f32[8,2,32,256]{3,2,1,0:T(8,128)S(1)} %all_to_all.11.mine_hbm), channel_id=1, source_target_pairs={{0,1},{1,0},{2,3},{3,2},{4,5},{5,4},{6,7},{7,6},{8,9},{9,8},{10,11... | collective-permute-start | bytes 1572872 | tf_op jit(solution)/shard_map/ppermute | solution.py:320
  102.2 0.1 pad_add_fusion.place_ref
  102.3 0.0 all-gather.5.cloned.1.call-done
  102.3 1.4 %collective-permute-done.11.other_hbm = f32[8,2,32,256]{3,2,1,0:T(8,128)S(1)} collective-permute-done((f32[8,2,32,256]{3,2,1,0:T(8,128)S(1)}, f32[8,2,32,256]{3,2,1,0:T(8,128)S(1)}, u32[]{:S(2)}, u32[]{:S(2)}) %collective-permute-start.11) | collective-permute-done | bytes 524320 | tf_op jit(solution)/shard_map/ppermute | solution.py:320
  103.7 0.0 copy-start.2
  103.7 5.0 %all-gather.7.cloned.1.call-done = f32[32,2,32,256]{3,2,1,0:T(8,128)} async-done(((f32[8,2,32,256]{3,2,1,0:T(8,128)}), f32[32,2,32,256]{3,2,1,0:T(8,128)}) %all-gather.7.cloned.1.call-update) | async-done | bytes 2097168 | tf_op jit(solution)/shard_map/all_gather | solution.py:316
  108.8 0.0 copy-done.1
  108.8 0.0 copy-done.2
  108.8 0.0 copy-done
  108.8 25.4 %update.1 = f32[2,256,4,256]{3,2,1,0:T(4,128)} custom-call(s32[2]{0:T(128)S(1)} %pad_add_fusion.place_ref, f32[2,256,4,256]{3,2,1,0:T(4,128)S(1)} %copy-done, f32[8,2,32,256]{3,2,1,0:T(8,128)} %copy-done.1, f32[8,2,32,256]{3,2,1,0:T(8,128)} %copy-done.2, f32[8,2,2,32,256]{4,3,2,1,0:T(8,128)} %bitcast.78, f32[4,8,2,32,256]{4,3,2,1,0:T(8,128)} %bitcast.77), custom_call_target="tpu_custom_call" | custom-call | tf_op jit(solution)/shard_map/update/pallas_call | solution.py:264
  (5 shorter events, 0.1 us)
Async XLA Ops:
  6.5 95.8 %all-gather.5.cloned.1.call-start = ((), (), s32[]{:S(2)}) async-start(), calls=%async_computation.2 | async-start | bytes 1114112 | tf_op jit(solution)/shard_map/all_gather | solution.py:301
  8.6 16.1 %collective-permute-start = (f32[2,32,256]{2,1,0:T(8,128)S(1)}, f32[2,32,256]{2,1,0:T(8,128)S(1)}, u32[]{:S(2)}, u32[]{:S(2)}) collective-permute-start(f32[2,32,256]{2,1,0:T(8,128)S(1)} %get-tuple-element.5), channel_id=1, source_target_pairs={{0,2},{1,3},{16,18},{17,19},{32,34},{33,35},{48,50},{49,51},{64,66... | collective-permute-start | bytes 196616 | tf_op jit(solution)/shard_map/ppermute | solution.py:300
  13.4 12.5 %collective-permute-start.4 = (f32[2,32,256]{2,1,0:T(8,128)S(1)}, f32[2,32,256]{2,1,0:T(8,128)S(1)}, u32[]{:S(2)}, u32[]{:S(2)}) collective-permute-start(f32[2,32,256]{2,1,0:T(8,128)S(1)} %get-tuple-element.6), channel_id=1, source_target_pairs={{0,10},{1,11},{16,26},{17,27},{32,42},{33,43},{48,58},{49,59},{64,... | collective-permute-start | bytes 196616 | tf_op jit(solution)/shard_map/ppermute | solution.py:300
  20.7 6.5 %collective-permute-start.3 = (f32[2,32,256]{2,1,0:T(8,128)S(1)}, f32[2,32,256]{2,1,0:T(8,128)S(1)}, u32[]{:S(2)}, u32[]{:S(2)}) collective-permute-start(f32[2,32,256]{2,1,0:T(8,128)S(1)} %get-tuple-element.7), channel_id=1, source_target_pairs={{0,8},{1,9},{16,24},{17,25},{32,40},{33,41},{48,56},{49,57},{64,72... | collective-permute-start | bytes 196616 | tf_op jit(solution)/shard_map/ppermute | solution.py:300
  22.0 5.3 %collective-permute-start.2 = (f32[2,32,256]{2,1,0:T(8,128)S(1)}, f32[2,32,256]{2,1,0:T(8,128)S(1)}, u32[]{:S(2)}, u32[]{:S(2)}) collective-permute-start(f32[2,32,256]{2,1,0:T(8,128)S(1)} %get-tuple-element.8), channel_id=1, source_target_pairs={{0,6},{1,7},{16,22},{17,23},{32,38},{33,39},{48,54},{49,55},{64,70... | collective-permute-start | bytes 196616 | tf_op jit(solution)/shard_map/ppermute | solution.py:300
  23.3 4.0 %collective-permute-start.1 = (f32[2,32,256]{2,1,0:T(8,128)S(1)}, f32[2,32,256]{2,1,0:T(8,128)S(1)}, u32[]{:S(2)}, u32[]{:S(2)}) collective-permute-start(f32[2,32,256]{2,1,0:T(8,128)S(1)} %get-tuple-element.9), channel_id=1, source_target_pairs={{0,4},{1,5},{16,20},{17,21},{32,36},{33,37},{48,52},{49,53},{64,68... | collective-permute-start | bytes 196616 | tf_op jit(solution)/shard_map/ppermute | solution.py:300
  24.6 2.7 %collective-permute-start.6 = (f32[2,32,256]{2,1,0:T(8,128)S(1)}, f32[2,32,256]{2,1,0:T(8,128)S(1)}, u32[]{:S(2)}, u32[]{:S(2)}) collective-permute-start(f32[2,32,256]{2,1,0:T(8,128)S(1)} %get-tuple-element.10), channel_id=1, source_target_pairs={{0,14},{1,15},{16,30},{17,31},{32,46},{33,47},{48,62},{49,63},{64,... | collective-permute-start | bytes 196616 | tf_op jit(solution)/shard_map/ppermute | solution.py:300
  26.0 3.0 %collective-permute-start.5 = (f32[2,32,256]{2,1,0:T(8,128)S(1)}, f32[2,32,256]{2,1,0:T(8,128)S(1)}, u32[]{:S(2)}, u32[]{:S(2)}) collective-permute-start(f32[2,32,256]{2,1,0:T(8,128)S(1)} %get-tuple-element.11), channel_id=1, source_target_pairs={{0,12},{1,13},{16,28},{17,29},{32,44},{33,45},{48,60},{49,61},{64,... | collective-permute-start | bytes 196616 | tf_op jit(solution)/shard_map/ppermute | solution.py:300
  29.7 79.1 %all-gather.7.cloned.1.call-start = ((), (), s32[]{:S(2)}) async-start(), calls=%async_computation.3 | async-start | bytes 2621440 | tf_op jit(solution)/shard_map/all_gather | solution.py:316
  30.5 6.8 %collective-permute-start.9 = (f32[32,256]{1,0:T(8,128)S(1)}, f32[32,256]{1,0:T(8,128)S(1)}, u32[]{:S(2)}, u32[]{:S(2)}) collective-permute-start(f32[32,256]{1,0:T(8,128)S(1)} %slice_bitcast_fusion.9), channel_id=1, source_target_pairs={{0,256},{16,272},{17,273},{2,258},{18,274},{19,275},{4,260},{20,27... | collective-permute-start | bytes 98312 | tf_op jit(solution)/shard_map/ppermute | solution.py:306
  31.1 6.1 %collective-permute-start.8 = (f32[32,256]{1,0:T(8,128)S(1)}, f32[32,256]{1,0:T(8,128)S(1)}, u32[]{:S(2)}, u32[]{:S(2)}) collective-permute-start(f32[32,256]{1,0:T(8,128)S(1)} %slice_bitcast_fusion.9), channel_id=1, source_target_pairs={{0,128},{16,144},{17,145},{2,130},{18,146},{19,147},{4,132},{20,14... | collective-permute-start | bytes 98312 | tf_op jit(solution)/shard_map/ppermute | solution.py:306
  31.8 5.5 %collective-permute-start.10 = (f32[32,256]{1,0:T(8,128)S(1)}, f32[32,256]{1,0:T(8,128)S(1)}, u32[]{:S(2)}, u32[]{:S(2)}) collective-permute-start(f32[32,256]{1,0:T(8,128)S(1)} %slice_bitcast_fusion.9), channel_id=1, source_target_pairs={{0,384},{16,400},{17,401},{2,386},{18,402},{19,403},{4,388},{20,40... | collective-permute-start | bytes 98312 | tf_op jit(solution)/shard_map/ppermute | solution.py:306
  32.5 11.9 %collective-permute-start.7 = (f32[2,32,256]{2,1,0:T(8,128)}, f32[2,32,256]{2,1,0:T(8,128)S(1)}, u32[]{:S(2)}, u32[]{:S(2)}) collective-permute-start(f32[2,32,256]{2,1,0:T(8,128)} %fusion.8), channel_id=1, source_target_pairs={{0,0},{1,128},{2,16},{3,144},{4,32},{5,160},{6,48},{7,176},{8,64},... | collective-permute-start | bytes 196616 | tf_op jit(solution)/shard_map/ppermute | solution.py:314
  44.5 64.3 %copy-start = (f32[2,256,4,256]{3,2,1,0:T(4,128)S(1)}, f32[2,256,4,256]{3,2,1,0:T(4,128)}, u32[]{:S(2)}) copy-start(f32[2,256,4,256]{3,2,1,0:T(4,128)} %cov_ref.1) | copy-start | bytes 6291460
  94.8 13.9 %copy-start.1 = (f32[8,2,32,256]{3,2,1,0:T(8,128)}, f32[8,2,32,256]{3,2,1,0:T(8,128)S(1)}, u32[]{:S(2)}) copy-start(f32[8,2,32,256]{3,2,1,0:T(8,128)S(1)} %all_to_all.11.mine_hbm) | copy-start | bytes 1572868
  94.8 8.9 %collective-permute-start.11 = (f32[8,2,32,256]{3,2,1,0:T(8,128)S(1)}, f32[8,2,32,256]{3,2,1,0:T(8,128)S(1)}, u32[]{:S(2)}, u32[]{:S(2)}) collective-permute-start(f32[8,2,32,256]{3,2,1,0:T(8,128)S(1)} %all_to_all.11.mine_hbm), channel_id=1, source_target_pairs={{0,1},{1,0},{2,3},{3,2},{4,5},{5,4},{6,7},{7,6},{8,9},{9,8},{10,11... | collective-permute-start | bytes 1572872 | tf_op jit(solution)/shard_map/ppermute | solution.py:320
  103.7 5.0 %copy-start.2 = (f32[8,2,32,256]{3,2,1,0:T(8,128)}, f32[8,2,32,256]{3,2,1,0:T(8,128)S(1)}, u32[]{:S(2)}) copy-start(f32[8,2,32,256]{3,2,1,0:T(8,128)S(1)} %collective-permute-done.11.other_hbm) | copy-start | bytes 1572868
Sparse Core Ops, SparseCore 0:
  29.8 43.0 all-gather.4
  77.2 31.5 all-gather.6

commit v8 on v7

--- a/solution.py
+++ b/solution.py
@@ -12,7 +12,6 @@
 NB = 256
 PART = NB // Z
 BOTH = ("row", "col")
-ROOTS = ((0, 0), (1, 0), (1, 1))
 
 
 def device(x, y, z, core):
@@ -300,22 +299,21 @@
         mine = mine + lax.ppermute(panel[:, s], BOTH, pairs)
     r = lax.all_gather(mine, "col")
 
-    head = jnp.where(x == 0, mine[0], 0.0)
-    for s in range(1, X):
-        pairs = [(device(0, y, c, k), device(s, y, c, k)) for c in range(Z) for y, k in ROOTS]
-        head = head + lax.ppermute(mine[0], BOTH, pairs)
-
     pairs = [
         (p * N_COL + c * CORE + k, device(2 * (p // N_COL) + k, c, (p % N_COL) // CORE, p % CORE))
         for p in range(N_ROW)
         for c in range(Z)
         for k in range(CORE)
     ]
-    mine = lax.ppermute(mine, BOTH, pairs)
-    got = shared(jnp.concatenate([mine, head[None]]), [[i * Y + j for j in range(Y)] for i in range(X)])
+    moved = lax.ppermute(mine, BOTH, pairs)
+    got = shared(jnp.concatenate([moved, mine[:1]]), [[i * Y + j for j in range(Y)] for i in range(X)])
     g = lax.all_gather(got[:, :2], "row", axis_index_groups=[[i * Y + j for i in range(X)] for j in range(Y)])
 
-    many = jnp.broadcast_to(got[None, :2, 2], (Z, 2, PART, NB))
+    head = jnp.where(x == 0, got[:2, 2], 0.0)
+    for s in range(1, X):
+        pairs = [(device(0, y, c, k), device(s, y, c, k)) for y in range(Y) for c in range(Z) for k in range(CORE)]
+        head = head + lax.ppermute(got[:2, 2], BOTH, pairs)
+    many = jnp.broadcast_to(head[None], (Z, 2, PART, NB))
     tiles = lax.all_to_all(many, "col", 0, 0, axis_index_groups=[[c * CORE + k for c in range(Z)] for k in range(CORE)])
     other = lax.ppermute(tiles, "col", [(i, i ^ 1) for i in range(N_COL)])
     return head_and_update(jnp.stack([row, col]).astype(jnp.int32), cov, tiles, other, r, g)

time: 142 us -> 143 us (level)
  waiting for transfers between devices: 14.5 us -> 9.1 us
  blocking collectives: 49.4 us -> 53.4 us
  starting transfers between devices: 32.8 us -> 35.7 us
    all_to_all x1, blocking collectives: 17.7 us -> 22.8 us  [on_device(): lax.all_to_all(many, 'col', 0, 0, axis_index_groups=[[c * CORE + k for c...]
    all_gather x1, waiting for transfers between devices: 5.03 us -> 0.01 us  [on_device(): lax.all_gather(got[:, :2], 'row', axis_index_groups=[[i * Y + j for i in...]
    ppermute x4, starting transfers between devices: 6.74 us -> 11.6 us  [the longest x3 7.44 us: on_device(): head = head + lax.ppermute(got[:2, 2], BOTH, pairs)]
    ppermute x1, starting transfers between devices: 7.37 us -> 5.52 us  [on_device(): other = lax.ppermute(tiles, 'col', [(i, i ^ 1) for i in range(N_COL)])]
  transfers between devices with their start and end apart: 14 -> 14, of which waited for: 4 -> 4; matrix products, arithmetic and copies ran while one was open for 2% -> 1% of each run, Pallas kernels for 0% -> 0%
where the time goes in v8:
time: 143 us
  blocking collectives  53.4 us (37%)
  starting transfers between devices  35.7 us (25%)
  Pallas kernels  25.4 us (18%)
  between operations  13.7 us (10%)
  waiting for transfers between devices  9.1 us (6%)
  local copies, waits for them, and re-layouts  4.54 us (3%)
    all_to_all x1, blocking collectives, shared(): return lax.all_to_all(many, 'row', 0, 0, axis_index_groups=groups)  30.6 us
    pallas_call x1, Pallas kernels, head_and_update(): pl.pallas_call(head_and_update_kernel, out_shape=jax.ShapeDtypeStruct(cov...  25.4 us
    all_to_all x1, blocking collectives, on_device(): lax.all_to_all(many, 'col', 0, 0, axis_index_groups=[[c * CORE + k for c...  22.8 us
    ppermute x7, starting transfers between devices, on_device(): mine = mine + lax.ppermute(panel[:, s], BOTH, pairs)  18.6 us
    ppermute x3, starting transfers between devices, on_device(): head = head + lax.ppermute(got[:2, 2], BOTH, pairs)  7.44 us
    ppermute x1, starting transfers between devices, on_device(): other = lax.ppermute(tiles, 'col', [(i, i ^ 1) for i in range(N_COL)])  5.52 us
    ppermute x1, waiting for transfers between devices, on_device(): moved = lax.ppermute(mine, BOTH, pairs)  4.68 us
    ppermute x1, starting transfers between devices, on_device(): moved = lax.ppermute(mine, BOTH, pairs)  4.13 us
  transfers between devices with their start and end apart: 14, of which 4 were waited for; matrix products, arithmetic and copies ran while one was open for 1% of the time, Pallas kernels for 0%

profile of v8, /device:TPU:1, one launch (start us, length us, event | category | flops | bytes accessed | tf_op | source)
XLA Modules:
  0.0 142.6 jit_solution(5114306894271589439)
XLA Ops:
  6.5 0.0 all-gather.5.cloned.1.call-start
  6.5 2.0 %slice.39 = f32[2,256,1,256]{3,2,1,0:T(1,128)S(1)} slice(f32[2,256,4,256]{3,2,1,0:T(4,128)} %cov_ref.1), slice={[0:2], [0:256], [0:1], [0:256]} | slice | bytes 1048576 | tf_op jit(solution)/shard_map/slice | solution.py:294
  8.6 4.8 %collective-permute-start = (f32[2,32,256]{2,1,0:T(8,128)S(1)}, f32[2,32,256]{2,1,0:T(8,128)S(1)}, u32[]{:S(2)}, u32[]{:S(2)}) collective-permute-start(f32[2,32,256]{2,1,0:T(8,128)S(1)} %get-tuple-element.5), channel_id=1, source_target_pairs={{0,2},{1,3},{16,18},{17,19},{32,34},{33,35},{48,50},{49,51},{64,66... | collective-permute-start | bytes 196616 | tf_op jit(solution)/shard_map/ppermute | solution.py:299
  13.4 7.3 %collective-permute-start.4 = (f32[2,32,256]{2,1,0:T(8,128)S(1)}, f32[2,32,256]{2,1,0:T(8,128)S(1)}, u32[]{:S(2)}, u32[]{:S(2)}) collective-permute-start(f32[2,32,256]{2,1,0:T(8,128)S(1)} %get-tuple-element.6), channel_id=1, source_target_pairs={{0,10},{1,11},{16,26},{17,27},{32,42},{33,43},{48,58},{49,59},{64,... | collective-permute-start | bytes 196616 | tf_op jit(solution)/shard_map/ppermute | solution.py:299
  20.7 1.3 collective-permute-start.3
  22.0 1.3 collective-permute-start.2
  23.3 1.3 collective-permute-start.1
  24.6 0.0 collective-permute-done
  24.6 1.3 collective-permute-start.6
  25.9 0.0 collective-permute-done.4
  26.0 1.3 collective-permute-start.5
  27.3 0.0 collective-permute-done.3
  27.3 0.0 collective-permute-done.2
  27.3 0.0 collective-permute-done.1
  27.3 0.0 collective-permute-done.6
  27.3 1.7 %collective-permute-done.5 = f32[2,32,256]{2,1,0:T(8,128)S(1)} collective-permute-done((f32[2,32,256]{2,1,0:T(8,128)S(1)}, f32[2,32,256]{2,1,0:T(8,128)S(1)}, u32[]{:S(2)}, u32[]{:S(2)}) %collective-permute-start.5) | collective-permute-done | bytes 65568 | tf_op jit(solution)/shard_map/ppermute | solution.py:299
  29.0 0.7 fusion.8
  29.6 0.0 all-gather.5.cloned.1.call-update
  29.7 0.0 all-gather.7.cloned.1.call-start
  29.7 4.1 %collective-permute-start.7 = (f32[2,32,256]{2,1,0:T(8,128)}, f32[2,32,256]{2,1,0:T(8,128)S(1)}, u32[]{:S(2)}, u32[]{:S(2)}) collective-permute-start(f32[2,32,256]{2,1,0:T(8,128)} %fusion.8), channel_id=1, source_target_pairs={{0,0},{1,128},{2,16},{3,144},{4,32},{5,160},{6,48},{7,176},{8,64},... | collective-permute-start | bytes 196616 | tf_op jit(solution)/shard_map/ppermute | solution.py:308
  33.8 0.8 slice.59
  34.6 4.7 %collective-permute-done.7 = f32[2,32,256]{2,1,0:T(8,128)S(1)} collective-permute-done((f32[2,32,256]{2,1,0:T(8,128)}, f32[2,32,256]{2,1,0:T(8,128)S(1)}, u32[]{:S(2)}, u32[]{:S(2)}) %collective-permute-start.7) | collective-permute-done | bytes 65568 | tf_op jit(solution)/shard_map/ppermute | solution.py:308
  39.3 0.1 broadcast_in_dim.20
  39.4 30.6 %all_to_all.10 = f32[8,3,32,256]{3,2,1,0:T(8,128)S(1)} all-to-all(f32[8,3,32,256]{3,2,1,0:T(8,128)S(1)} %broadcast_in_dim.20), channel_id=1, replica_groups={{0,16,32,48,64,80,96,112},{128,144,160,176,192,208,224,240},{256,272,28..., dimensions={0} | all-to-all | bytes 1572864 | tf_op jit(solution)/shard_map/all_to_all | solution.py:288
  70.0 0.0 copy-start
  70.0 0.8 slice.61
  70.8 0.0 all-gather.7.cloned.1.call-update
  70.9 4.9 %collective-permute-start.9 = (f32[2,32,256]{2,1,0:T(8,128)S(1)}, f32[2,32,256]{2,1,0:T(8,128)S(1)}, u32[]{:S(2)}, u32[]{:S(2)}) collective-permute-start(f32[2,32,256]{2,1,0:T(8,128)S(1)} %slice_bitcast_fusion), channel_id=1, source_target_pairs={{0,256},{1,257},{2,258},{3,259},{4,260},{5,261},{6,262},{7,263},{8... | collective-permute-start | bytes 196616 | tf_op jit(solution)/shard_map/ppermute | solution.py:315
  75.7 1.3 collective-permute-start.8
  77.0 1.3 collective-permute-start.10
  78.3 0.0 collective-permute-done.9
  78.3 0.0 collective-permute-done.8
  78.4 1.3 collective-permute-done.10
  79.7 22.8 %all_to_all.11.mine_hbm = f32[8,2,32,256]{3,2,1,0:T(8,128)S(1)} all-to-all(f32[8,2,32,256]{3,2,1,0:T(8,128)S(1)} %broadcast_in_dim.22), channel_id=1, replica_groups={{0,2,4,6,8,10,12,14},{1,3,5,7,9,11,13,15},{16,18,20,22,24,26,28,30},{17..., dimensions={0} | all-to-all | bytes 1048576 | tf_op jit(solution)/shard_map/all_to_all | solution.py:317
  102.5 0.0 copy-start.1
  102.5 5.5 %collective-permute-start.11 = (f32[8,2,32,256]{3,2,1,0:T(8,128)S(1)}, f32[8,2,32,256]{3,2,1,0:T(8,128)S(1)}, u32[]{:S(2)}, u32[]{:S(2)}) collective-permute-start(f32[8,2,32,256]{3,2,1,0:T(8,128)S(1)} %all_to_all.11.mine_hbm), channel_id=1, source_target_pairs={{0,1},{1,0},{2,3},{3,2},{4,5},{5,4},{6,7},{7,6},{8,9},{9,8},{10,11... | collective-permute-start | bytes 1572872 | tf_op jit(solution)/shard_map/ppermute | solution.py:318
  108.0 0.1 pad_add_fusion.place_ref
  108.1 0.0 all-gather.5.cloned.1.call-done
  108.1 1.4 %collective-permute-done.11.other_hbm = f32[8,2,32,256]{3,2,1,0:T(8,128)S(1)} collective-permute-done((f32[8,2,32,256]{3,2,1,0:T(8,128)S(1)}, f32[8,2,32,256]{3,2,1,0:T(8,128)S(1)}, u32[]{:S(2)}, u32[]{:S(2)}) %collective-permute-start.11) | collective-permute-done | bytes 524320 | tf_op jit(solution)/shard_map/ppermute | solution.py:318
  109.6 0.0 copy-start.2
  109.6 0.0 all-gather.7.cloned.1.call-done
  109.6 0.0 copy-done.1
  109.6 0.8 copy-done.2
  110.3 0.0 copy-done
  110.3 25.4 %update.1 = f32[2,256,4,256]{3,2,1,0:T(4,128)} custom-call(s32[2]{0:T(128)S(1)} %pad_add_fusion.place_ref, f32[2,256,4,256]{3,2,1,0:T(4,128)S(1)} %copy-done, f32[8,2,32,256]{3,2,1,0:T(8,128)} %copy-done.1, f32[8,2,32,256]{3,2,1,0:T(8,128)} %copy-done.2, f32[8,2,2,32,256]{4,3,2,1,0:T(8,128)} %bitcast.74, f32[4,8,2,32,256]{4,3,2,1,0:T(8,128)} %bitcast.73), custom_call_target="tpu_custom_call" | custom-call | tf_op jit(solution)/shard_map/update/pallas_call | solution.py:263
  (6 shorter events, 0.1 us)
Async XLA Ops:
  6.5 101.6 %all-gather.5.cloned.1.call-start = ((), (), s32[]{:S(2)}) async-start(), calls=%async_computation.2 | async-start | bytes 1114112 | tf_op jit(solution)/shard_map/all_gather | solution.py:300
  8.6 16.1 %collective-permute-start = (f32[2,32,256]{2,1,0:T(8,128)S(1)}, f32[2,32,256]{2,1,0:T(8,128)S(1)}, u32[]{:S(2)}, u32[]{:S(2)}) collective-permute-start(f32[2,32,256]{2,1,0:T(8,128)S(1)} %get-tuple-element.5), channel_id=1, source_target_pairs={{0,2},{1,3},{16,18},{17,19},{32,34},{33,35},{48,50},{49,51},{64,66... | collective-permute-start | bytes 196616 | tf_op jit(solution)/shard_map/ppermute | solution.py:299
  13.4 12.5 %collective-permute-start.4 = (f32[2,32,256]{2,1,0:T(8,128)S(1)}, f32[2,32,256]{2,1,0:T(8,128)S(1)}, u32[]{:S(2)}, u32[]{:S(2)}) collective-permute-start(f32[2,32,256]{2,1,0:T(8,128)S(1)} %get-tuple-element.6), channel_id=1, source_target_pairs={{0,10},{1,11},{16,26},{17,27},{32,42},{33,43},{48,58},{49,59},{64,... | collective-permute-start | bytes 196616 | tf_op jit(solution)/shard_map/ppermute | solution.py:299
  20.7 6.5 %collective-permute-start.3 = (f32[2,32,256]{2,1,0:T(8,128)S(1)}, f32[2,32,256]{2,1,0:T(8,128)S(1)}, u32[]{:S(2)}, u32[]{:S(2)}) collective-permute-start(f32[2,32,256]{2,1,0:T(8,128)S(1)} %get-tuple-element.7), channel_id=1, source_target_pairs={{0,8},{1,9},{16,24},{17,25},{32,40},{33,41},{48,56},{49,57},{64,72... | collective-permute-start | bytes 196616 | tf_op jit(solution)/shard_map/ppermute | solution.py:299
  22.0 5.3 %collective-permute-start.2 = (f32[2,32,256]{2,1,0:T(8,128)S(1)}, f32[2,32,256]{2,1,0:T(8,128)S(1)}, u32[]{:S(2)}, u32[]{:S(2)}) collective-permute-start(f32[2,32,256]{2,1,0:T(8,128)S(1)} %get-tuple-element.8), channel_id=1, source_target_pairs={{0,6},{1,7},{16,22},{17,23},{32,38},{33,39},{48,54},{49,55},{64,70... | collective-permute-start | bytes 196616 | tf_op jit(solution)/shard_map/ppermute | solution.py:299
  23.3 4.0 %collective-permute-start.1 = (f32[2,32,256]{2,1,0:T(8,128)S(1)}, f32[2,32,256]{2,1,0:T(8,128)S(1)}, u32[]{:S(2)}, u32[]{:S(2)}) collective-permute-start(f32[2,32,256]{2,1,0:T(8,128)S(1)} %get-tuple-element.9), channel_id=1, source_target_pairs={{0,4},{1,5},{16,20},{17,21},{32,36},{33,37},{48,52},{49,53},{64,68... | collective-permute-start | bytes 196616 | tf_op jit(solution)/shard_map/ppermute | solution.py:299
  24.6 2.7 %collective-permute-start.6 = (f32[2,32,256]{2,1,0:T(8,128)S(1)}, f32[2,32,256]{2,1,0:T(8,128)S(1)}, u32[]{:S(2)}, u32[]{:S(2)}) collective-permute-start(f32[2,32,256]{2,1,0:T(8,128)S(1)} %get-tuple-element.10), channel_id=1, source_target_pairs={{0,14},{1,15},{16,30},{17,31},{32,46},{33,47},{48,62},{49,63},{64,... | collective-permute-start | bytes 196616 | tf_op jit(solution)/shard_map/ppermute | solution.py:299
  26.0 3.0 %collective-permute-start.5 = (f32[2,32,256]{2,1,0:T(8,128)S(1)}, f32[2,32,256]{2,1,0:T(8,128)S(1)}, u32[]{:S(2)}, u32[]{:S(2)}) collective-permute-start(f32[2,32,256]{2,1,0:T(8,128)S(1)} %get-tuple-element.11), channel_id=1, source_target_pairs={{0,12},{1,13},{16,28},{17,29},{32,44},{33,45},{48,60},{49,61},{64,... | collective-permute-start | bytes 196616 | tf_op jit(solution)/shard_map/ppermute | solution.py:299
  29.7 79.9 %all-gather.7.cloned.1.call-start = ((), (), s32[]{:S(2)}) async-start(), calls=%async_computation.3 | async-start | bytes 2621440 | tf_op jit(solution)/shard_map/all_gather | solution.py:310
  29.7 9.6 %collective-permute-start.7 = (f32[2,32,256]{2,1,0:T(8,128)}, f32[2,32,256]{2,1,0:T(8,128)S(1)}, u32[]{:S(2)}, u32[]{:S(2)}) collective-permute-start(f32[2,32,256]{2,1,0:T(8,128)} %fusion.8), channel_id=1, source_target_pairs={{0,0},{1,128},{2,16},{3,144},{4,32},{5,160},{6,48},{7,176},{8,64},... | collective-permute-start | bytes 196616 | tf_op jit(solution)/shard_map/ppermute | solution.py:308
  70.0 40.4 %copy-start = (f32[2,256,4,256]{3,2,1,0:T(4,128)S(1)}, f32[2,256,4,256]{3,2,1,0:T(4,128)}, u32[]{:S(2)}) copy-start(f32[2,256,4,256]{3,2,1,0:T(4,128)} %cov_ref.1) | copy-start | bytes 6291460
  70.9 7.5 %collective-permute-start.9 = (f32[2,32,256]{2,1,0:T(8,128)S(1)}, f32[2,32,256]{2,1,0:T(8,128)S(1)}, u32[]{:S(2)}, u32[]{:S(2)}) collective-permute-start(f32[2,32,256]{2,1,0:T(8,128)S(1)} %slice_bitcast_fusion), channel_id=1, source_target_pairs={{0,256},{1,257},{2,258},{3,259},{4,260},{5,261},{6,262},{7,263},{8... | collective-permute-start | bytes 196616 | tf_op jit(solution)/shard_map/ppermute | solution.py:315
  75.7 2.6 %collective-permute-start.8 = (f32[2,32,256]{2,1,0:T(8,128)S(1)}, f32[2,32,256]{2,1,0:T(8,128)S(1)}, u32[]{:S(2)}, u32[]{:S(2)}) collective-permute-start(f32[2,32,256]{2,1,0:T(8,128)S(1)} %slice_bitcast_fusion), channel_id=1, source_target_pairs={{0,128},{1,129},{2,130},{3,131},{4,132},{5,133},{6,134},{7,135},{8... | collective-permute-start | bytes 196616 | tf_op jit(solution)/shard_map/ppermute | solution.py:315
  77.0 2.6 %collective-permute-start.10 = (f32[2,32,256]{2,1,0:T(8,128)S(1)}, f32[2,32,256]{2,1,0:T(8,128)S(1)}, u32[]{:S(2)}, u32[]{:S(2)}) collective-permute-start(f32[2,32,256]{2,1,0:T(8,128)S(1)} %slice_bitcast_fusion), channel_id=1, source_target_pairs={{0,384},{1,385},{2,386},{3,387},{4,388},{5,389},{6,390},{7,391},{8... | collective-permute-start | bytes 196616 | tf_op jit(solution)/shard_map/ppermute | solution.py:315
  102.5 7.0 %copy-start.1 = (f32[8,2,32,256]{3,2,1,0:T(8,128)}, f32[8,2,32,256]{3,2,1,0:T(8,128)S(1)}, u32[]{:S(2)}) copy-start(f32[8,2,32,256]{3,2,1,0:T(8,128)S(1)} %all_to_all.11.mine_hbm) | copy-start | bytes 1572868
  102.5 7.0 %collective-permute-start.11 = (f32[8,2,32,256]{3,2,1,0:T(8,128)S(1)}, f32[8,2,32,256]{3,2,1,0:T(8,128)S(1)}, u32[]{:S(2)}, u32[]{:S(2)}) collective-permute-start(f32[8,2,32,256]{3,2,1,0:T(8,128)S(1)} %all_to_all.11.mine_hbm), channel_id=1, source_target_pairs={{0,1},{1,0},{2,3},{3,2},{4,5},{5,4},{6,7},{7,6},{8,9},{9,8},{10,11... | collective-permute-start | bytes 1572872 | tf_op jit(solution)/shard_map/ppermute | solution.py:318
  109.6 0.8 copy-start.2
Sparse Core Ops, SparseCore 0:
  29.8 42.9 all-gather.4
  74.9 33.8 all-gather.6

commit v9 on v7

--- a/solution.py
+++ b/solution.py
@@ -301,9 +301,10 @@
     r = lax.all_gather(mine, "col")
 
     head = jnp.where(x == 0, mine[0], 0.0)
-    for s in range(1, X):
-        pairs = [(device(0, y, c, k), device(s, y, c, k)) for c in range(Z) for y, k in ROOTS]
-        head = head + lax.ppermute(mine[0], BOTH, pairs)
+    for s in (X // 2, 1):
+        sources = range(0, X, 2 * s)
+        pairs = [(device(i, y, c, k), device(i + s, y, c, k)) for i in sources for c in range(Z) for y, k in ROOTS]
+        head = head + lax.ppermute(head, BOTH, pairs)
 
     pairs = [
         (p * N_COL + c * CORE + k, device(2 * (p // N_COL) + k, c, (p % N_COL) // CORE, p % CORE))

time: 142 us -> 143 us (level)
  waiting for transfers between devices: 14.5 us -> 18.9 us
    all_gather x1, waiting for transfers between devices: 5.03 us -> 7.83 us  [on_device(): lax.all_gather(got[:, :2], 'row', axis_index_groups=[[i * Y + j for i in...]
    ppermute x1, waiting for transfers between devices: 6.3 us -> 7.95 us  [on_device(): mine = lax.ppermute(mine, BOTH, pairs)]
  transfers between devices with their start and end apart: 14 -> 13, of which waited for: 4 -> 4; matrix products, arithmetic and copies ran while one was open for 2% -> 1% of each run, Pallas kernels for 0% -> 0%
where the time goes in v9:
time: 143 us
  blocking collectives  48.7 us (34%)
  starting transfers between devices  32 us (22%)
  Pallas kernels  25.4 us (18%)
  waiting for transfers between devices  18.9 us (13%)
  between operations  13.7 us (10%)
  local copies, waits for them, and re-layouts  3 us (2%)
    all_to_all x1, blocking collectives, shared(): return lax.all_to_all(many, 'row', 0, 0, axis_index_groups=groups)  30.9 us
    pallas_call x1, Pallas kernels, head_and_update(): pl.pallas_call(head_and_update_kernel, out_shape=jax.ShapeDtypeStruct(cov...  25.4 us
    ppermute x7, starting transfers between devices, on_device(): mine = mine + lax.ppermute(panel[:, s], BOTH, pairs)  18.6 us
    all_to_all x1, blocking collectives, on_device(): lax.all_to_all(many, 'col', 0, 0, axis_index_groups=[[c * CORE + k for c...  17.8 us
    ppermute x1, waiting for transfers between devices, on_device(): mine = lax.ppermute(mine, BOTH, pairs)  7.95 us
    all_gather x1, waiting for transfers between devices, on_device(): lax.all_gather(got[:, :2], 'row', axis_index_groups=[[i * Y + j for i in...  7.83 us
    ppermute x1, starting transfers between devices, on_device(): other = lax.ppermute(tiles, 'col', [(i, i ^ 1) for i in range(N_COL)])  7.32 us
    ppermute x1, starting transfers between devices, on_device(): mine = lax.ppermute(mine, BOTH, pairs)  4.76 us
  transfers between devices with their start and end apart: 13, of which 4 were waited for; matrix products, arithmetic and copies ran while one was open for 1% of the time, Pallas kernels for 0%

profile of v9, /device:TPU:1, one launch (start us, length us, event | category | flops | bytes accessed | tf_op | source)
XLA Modules:
  0.0 142.6 jit_solution(9564879093396161690)
XLA Ops:
  6.5 0.0 all-gather.5.cloned.1.call-start
  6.5 2.0 %slice.36 = f32[2,256,1,256]{3,2,1,0:T(1,128)S(1)} slice(f32[2,256,4,256]{3,2,1,0:T(4,128)} %cov_ref.1), slice={[0:2], [0:256], [0:1], [0:256]} | slice | bytes 1048576 | tf_op jit(solution)/shard_map/slice | solution.py:295
  8.6 4.8 %collective-permute-start = (f32[2,32,256]{2,1,0:T(8,128)S(1)}, f32[2,32,256]{2,1,0:T(8,128)S(1)}, u32[]{:S(2)}, u32[]{:S(2)}) collective-permute-start(f32[2,32,256]{2,1,0:T(8,128)S(1)} %get-tuple-element.5), channel_id=1, source_target_pairs={{0,2},{1,3},{16,18},{17,19},{32,34},{33,35},{48,50},{49,51},{64,66... | collective-permute-start | bytes 196616 | tf_op jit(solution)/shard_map/ppermute | solution.py:300
  13.4 7.3 %collective-permute-start.4 = (f32[2,32,256]{2,1,0:T(8,128)S(1)}, f32[2,32,256]{2,1,0:T(8,128)S(1)}, u32[]{:S(2)}, u32[]{:S(2)}) collective-permute-start(f32[2,32,256]{2,1,0:T(8,128)S(1)} %get-tuple-element.6), channel_id=1, source_target_pairs={{0,10},{1,11},{16,26},{17,27},{32,42},{33,43},{48,58},{49,59},{64,... | collective-permute-start | bytes 196616 | tf_op jit(solution)/shard_map/ppermute | solution.py:300
  20.7 1.3 collective-permute-start.3
  22.0 1.3 collective-permute-start.2
  23.3 1.3 collective-permute-start.1
  24.6 0.0 collective-permute-done
  24.6 1.3 collective-permute-start.6
  25.9 0.0 collective-permute-done.4
  26.0 1.3 collective-permute-start.5
  27.3 0.0 collective-permute-done.3
  27.3 0.0 collective-permute-done.2
  27.3 0.0 collective-permute-done.1
  27.3 0.0 collective-permute-done.6
  27.3 1.6 %collective-permute-done.5 = f32[2,32,256]{2,1,0:T(8,128)S(1)} collective-permute-done((f32[2,32,256]{2,1,0:T(8,128)S(1)}, f32[2,32,256]{2,1,0:T(8,128)S(1)}, u32[]{:S(2)}, u32[]{:S(2)}) %collective-permute-start.5) | collective-permute-done | bytes 65568 | tf_op jit(solution)/shard_map/ppermute | solution.py:300
  29.0 0.0 copy-start.2
  29.0 0.7 collective-permute-start.8
  29.7 0.0 copy-done.2
  29.7 0.0 all-gather.5.cloned.1.call-update
  29.7 0.0 all-gather.7.cloned.1.call-start
  29.8 0.0 collective-permute-done.8
  29.8 0.8 fusion.10
  30.6 0.7 collective-permute-start.9
  31.2 4.8 %collective-permute-start.7 = (f32[2,32,256]{2,1,0:T(8,128)}, f32[2,32,256]{2,1,0:T(8,128)S(1)}, u32[]{:S(2)}, u32[]{:S(2)}) collective-permute-start(f32[2,32,256]{2,1,0:T(8,128)} %copy-done.2), channel_id=1, source_target_pairs={{0,0},{1,128},{2,16},{3,144},{4,32},{5,160},{6,48},{7,176},{8,64},... | collective-permute-start | bytes 196616 | tf_op jit(solution)/shard_map/ppermute | solution.py:315
  36.0 0.0 collective-permute-done.9
  36.0 8.0 %collective-permute-done.7 = f32[2,32,256]{2,1,0:T(8,128)S(1)} collective-permute-done((f32[2,32,256]{2,1,0:T(8,128)}, f32[2,32,256]{2,1,0:T(8,128)S(1)}, u32[]{:S(2)}, u32[]{:S(2)}) %collective-permute-start.7) | collective-permute-done | bytes 65568 | tf_op jit(solution)/shard_map/ppermute | solution.py:315
  44.0 0.1 broadcast_in_dim.27
  44.1 0.0 copy-start
  44.1 30.9 %all_to_all.10 = f32[8,3,32,256]{3,2,1,0:T(8,128)S(1)} all-to-all(f32[8,3,32,256]{3,2,1,0:T(8,128)S(1)} %broadcast_in_dim.27), channel_id=1, replica_groups={{0,16,32,48,64,80,96,112},{128,144,160,176,192,208,224,240},{256,272,28..., dimensions={0} | all-to-all | bytes 1572864 | tf_op jit(solution)/shard_map/all_to_all | solution.py:289
  74.9 0.8 slice.58
  75.8 0.0 all-gather.7.cloned.1.call-update
  75.9 17.8 %all_to_all.11.mine_hbm = f32[8,2,32,256]{3,2,1,0:T(8,128)S(1)} all-to-all(f32[8,2,32,256]{3,2,1,0:T(8,128)S(1)} %broadcast_in_dim.29), channel_id=1, replica_groups={{0,2,4,6,8,10,12,14},{1,3,5,7,9,11,13,15},{16,18,20,22,24,26,28,30},{17..., dimensions={0} | all-to-all | bytes 1048576 | tf_op jit(solution)/shard_map/all_to_all | solution.py:320
  93.7 0.0 copy-start.1
  93.7 7.3 %collective-permute-start.10 = (f32[8,2,32,256]{3,2,1,0:T(8,128)S(1)}, f32[8,2,32,256]{3,2,1,0:T(8,128)S(1)}, u32[]{:S(2)}, u32[]{:S(2)}) collective-permute-start(f32[8,2,32,256]{3,2,1,0:T(8,128)S(1)} %all_to_all.11.mine_hbm), channel_id=1, source_target_pairs={{0,1},{1,0},{2,3},{3,2},{4,5},{5,4},{6,7},{7,6},{8,9},{9,8},{10,11... | collective-permute-start | bytes 1572872 | tf_op jit(solution)/shard_map/ppermute | solution.py:321
  101.0 0.1 pad_add_fusion.place_ref
  101.1 0.0 all-gather.5.cloned.1.call-done
  101.1 1.4 %collective-permute-done.10.other_hbm = f32[8,2,32,256]{3,2,1,0:T(8,128)S(1)} collective-permute-done((f32[8,2,32,256]{3,2,1,0:T(8,128)S(1)}, f32[8,2,32,256]{3,2,1,0:T(8,128)S(1)}, u32[]{:S(2)}, u32[]{:S(2)}) %collective-permute-start.10) | collective-permute-done | bytes 524320 | tf_op jit(solution)/shard_map/ppermute | solution.py:321
  102.6 0.0 copy-start.3
  102.6 7.8 %all-gather.7.cloned.1.call-done = f32[32,2,32,256]{3,2,1,0:T(8,128)} async-done(((f32[8,2,32,256]{3,2,1,0:T(8,128)}), f32[32,2,32,256]{3,2,1,0:T(8,128)}) %all-gather.7.cloned.1.call-update) | async-done | bytes 2097168 | tf_op jit(solution)/shard_map/all_gather | solution.py:317
  110.4 0.0 copy-done.1
  110.4 0.0 copy-done.3
  110.4 0.0 copy-done
  110.4 25.4 %update.1 = f32[2,256,4,256]{3,2,1,0:T(4,128)} custom-call(s32[2]{0:T(128)S(1)} %pad_add_fusion.place_ref, f32[2,256,4,256]{3,2,1,0:T(4,128)S(1)} %copy-done, f32[8,2,32,256]{3,2,1,0:T(8,128)} %copy-done.1, f32[8,2,32,256]{3,2,1,0:T(8,128)} %copy-done.3, f32[8,2,2,32,256]{4,3,2,1,0:T(8,128)} %bitcast.78, f32[4,8,2,32,256]{4,3,2,1,0:T(8,128)} %bitcast.77), custom_call_target="tpu_custom_call" | custom-call | tf_op jit(solution)/shard_map/update/pallas_call | solution.py:264
  (8 shorter events, 0.2 us)
Async XLA Ops:
  6.5 94.6 %all-gather.5.cloned.1.call-start = ((), (), s32[]{:S(2)}) async-start(), calls=%async_computation.2 | async-start | bytes 1114112 | tf_op jit(solution)/shard_map/all_gather | solution.py:301
  8.6 16.1 %collective-permute-start = (f32[2,32,256]{2,1,0:T(8,128)S(1)}, f32[2,32,256]{2,1,0:T(8,128)S(1)}, u32[]{:S(2)}, u32[]{:S(2)}) collective-permute-start(f32[2,32,256]{2,1,0:T(8,128)S(1)} %get-tuple-element.5), channel_id=1, source_target_pairs={{0,2},{1,3},{16,18},{17,19},{32,34},{33,35},{48,50},{49,51},{64,66... | collective-permute-start | bytes 196616 | tf_op jit(solution)/shard_map/ppermute | solution.py:300
  13.4 12.5 %collective-permute-start.4 = (f32[2,32,256]{2,1,0:T(8,128)S(1)}, f32[2,32,256]{2,1,0:T(8,128)S(1)}, u32[]{:S(2)}, u32[]{:S(2)}) collective-permute-start(f32[2,32,256]{2,1,0:T(8,128)S(1)} %get-tuple-element.6), channel_id=1, source_target_pairs={{0,10},{1,11},{16,26},{17,27},{32,42},{33,43},{48,58},{49,59},{64,... | collective-permute-start | bytes 196616 | tf_op jit(solution)/shard_map/ppermute | solution.py:300
  20.7 6.6 %collective-permute-start.3 = (f32[2,32,256]{2,1,0:T(8,128)S(1)}, f32[2,32,256]{2,1,0:T(8,128)S(1)}, u32[]{:S(2)}, u32[]{:S(2)}) collective-permute-start(f32[2,32,256]{2,1,0:T(8,128)S(1)} %get-tuple-element.7), channel_id=1, source_target_pairs={{0,8},{1,9},{16,24},{17,25},{32,40},{33,41},{48,56},{49,57},{64,72... | collective-permute-start | bytes 196616 | tf_op jit(solution)/shard_map/ppermute | solution.py:300
  22.0 5.3 %collective-permute-start.2 = (f32[2,32,256]{2,1,0:T(8,128)S(1)}, f32[2,32,256]{2,1,0:T(8,128)S(1)}, u32[]{:S(2)}, u32[]{:S(2)}) collective-permute-start(f32[2,32,256]{2,1,0:T(8,128)S(1)} %get-tuple-element.8), channel_id=1, source_target_pairs={{0,6},{1,7},{16,22},{17,23},{32,38},{33,39},{48,54},{49,55},{64,70... | collective-permute-start | bytes 196616 | tf_op jit(solution)/shard_map/ppermute | solution.py:300
  23.3 4.0 %collective-permute-start.1 = (f32[2,32,256]{2,1,0:T(8,128)S(1)}, f32[2,32,256]{2,1,0:T(8,128)S(1)}, u32[]{:S(2)}, u32[]{:S(2)}) collective-permute-start(f32[2,32,256]{2,1,0:T(8,128)S(1)} %get-tuple-element.9), channel_id=1, source_target_pairs={{0,4},{1,5},{16,20},{17,21},{32,36},{33,37},{48,52},{49,53},{64,68... | collective-permute-start | bytes 196616 | tf_op jit(solution)/shard_map/ppermute | solution.py:300
  24.6 2.7 %collective-permute-start.6 = (f32[2,32,256]{2,1,0:T(8,128)S(1)}, f32[2,32,256]{2,1,0:T(8,128)S(1)}, u32[]{:S(2)}, u32[]{:S(2)}) collective-permute-start(f32[2,32,256]{2,1,0:T(8,128)S(1)} %get-tuple-element.10), channel_id=1, source_target_pairs={{0,14},{1,15},{16,30},{17,31},{32,46},{33,47},{48,62},{49,63},{64,... | collective-permute-start | bytes 196616 | tf_op jit(solution)/shard_map/ppermute | solution.py:300
  26.0 3.0 %collective-permute-start.5 = (f32[2,32,256]{2,1,0:T(8,128)S(1)}, f32[2,32,256]{2,1,0:T(8,128)S(1)}, u32[]{:S(2)}, u32[]{:S(2)}) collective-permute-start(f32[2,32,256]{2,1,0:T(8,128)S(1)} %get-tuple-element.11), channel_id=1, source_target_pairs={{0,12},{1,13},{16,28},{17,29},{32,44},{33,45},{48,60},{49,61},{64,... | collective-permute-start | bytes 196616 | tf_op jit(solution)/shard_map/ppermute | solution.py:300
  29.0 0.7 copy-start.2
  29.0 0.8 collective-permute-start.8
  29.7 80.7 %all-gather.7.cloned.1.call-start = ((), (), s32[]{:S(2)}) async-start(), calls=%async_computation.3 | async-start | bytes 2621440 | tf_op jit(solution)/shard_map/all_gather | solution.py:317
  30.6 5.4 %collective-permute-start.9 = (f32[32,256]{1,0:T(8,128)S(1)}, f32[32,256]{1,0:T(8,128)S(1)}, u32[]{:S(2)}, u32[]{:S(2)}) collective-permute-start(f32[32,256]{1,0:T(8,128)S(1)} %fusion.10), channel_id=1, source_target_pairs={{0,128},{16,144},{17,145},{2,130},{18,146},{19,147},{4,132},{20,14... | collective-permute-start | bytes 98312 | tf_op jit(solution)/shard_map/ppermute | solution.py:307
  31.2 12.7 %collective-permute-start.7 = (f32[2,32,256]{2,1,0:T(8,128)}, f32[2,32,256]{2,1,0:T(8,128)S(1)}, u32[]{:S(2)}, u32[]{:S(2)}) collective-permute-start(f32[2,32,256]{2,1,0:T(8,128)} %copy-done.2), channel_id=1, source_target_pairs={{0,0},{1,128},{2,16},{3,144},{4,32},{5,160},{6,48},{7,176},{8,64},... | collective-permute-start | bytes 196616 | tf_op jit(solution)/shard_map/ppermute | solution.py:315
  44.1 66.3 %copy-start = (f32[2,256,4,256]{3,2,1,0:T(4,128)S(1)}, f32[2,256,4,256]{3,2,1,0:T(4,128)}, u32[]{:S(2)}) copy-start(f32[2,256,4,256]{3,2,1,0:T(4,128)} %cov_ref.1) | copy-start | bytes 6291460
  93.7 16.7 %copy-start.1 = (f32[8,2,32,256]{3,2,1,0:T(8,128)}, f32[8,2,32,256]{3,2,1,0:T(8,128)S(1)}, u32[]{:S(2)}) copy-start(f32[8,2,32,256]{3,2,1,0:T(8,128)S(1)} %all_to_all.11.mine_hbm) | copy-start | bytes 1572868
  93.7 8.8 %collective-permute-start.10 = (f32[8,2,32,256]{3,2,1,0:T(8,128)S(1)}, f32[8,2,32,256]{3,2,1,0:T(8,128)S(1)}, u32[]{:S(2)}, u32[]{:S(2)}) collective-permute-start(f32[8,2,32,256]{3,2,1,0:T(8,128)S(1)} %all_to_all.11.mine_hbm), channel_id=1, source_target_pairs={{0,1},{1,0},{2,3},{3,2},{4,5},{5,4},{6,7},{7,6},{8,9},{9,8},{10,11... | collective-permute-start | bytes 1572872 | tf_op jit(solution)/shard_map/ppermute | solution.py:321
  102.6 7.8 %copy-start.3 = (f32[8,2,32,256]{3,2,1,0:T(8,128)}, f32[8,2,32,256]{3,2,1,0:T(8,128)S(1)}, u32[]{:S(2)}) copy-start(f32[8,2,32,256]{3,2,1,0:T(8,128)S(1)} %collective-permute-done.10.other_hbm) | copy-start | bytes 1572868
Sparse Core Ops, SparseCore 0:
  29.9 43.0 all-gather.4
  75.9 34.4 all-gather.6
